TPU v7x, 32 devices: a whole 2x2x4 slice. The times are simulated.
32 devices in a mesh: fsdp: 16 (over z, x, core), seq: 2 (over y).
Axes of the slice: x: 2, y: 2, z: 4, core: 2. Of those that a mesh axis runs over, the one named last changes fastest.
Arguments:
- tokens: bfloat16 [8192, 1024], P(('fsdp', 'seq')), may hold values from -6 to 6
- cotangent: bfloat16 [8192, 1024], P(('fsdp', 'seq')), may hold values from -6 to 6
- doc_ids: int32 [8192], replicated, may hold values from 0 to 7, never falling along the last dimension, each value on 1 to 4096 neighbouring positions
- norm_gain: float32 [1024], replicated, may hold values from 0.7 to 6.5
- in_weight: float32 [1024, 4384], P(('fsdp', 'seq'))
- conv_params: float32 [5, 2304], replicated, may hold values from -0.5 to 0.5
- head_params: float32 [3, 32], replicated, may hold values from -6 to 2
- out_gain: float32 [2048], replicated, may hold values from 0.7 to 6.5
- out_weight: float32 [2048, 1024], P(('fsdp', 'seq'))
- norm_first: float32 [1024], replicated, may hold values from -20 to 20
- norm_second: float32 [1024], replicated, may hold values from 0.49152 to 8.192
- in_first: float32 [1024, 4384], P(('fsdp', 'seq')), may hold values from -32 to 32
- in_second: float32 [1024, 4384], P(('fsdp', 'seq')), may hold values from 1.024 to 16.384
- conv_first: float32 [5, 2304], replicated, may hold values from -24 to 24
- conv_second: float32 [5, 2304], replicated, may hold values from 0.65536 to 10.6496
- head_first: float32 [3, 32], replicated, may hold values from -64 to 64
- head_second: float32 [3, 32], replicated, may hold values from 4.096 to 65.536
- gain_first: float32 [2048], replicated, may hold values from -20 to 20
- gain_second: float32 [2048], replicated, may hold values from 0.49152 to 8.192
- out_first: float32 [2048, 1024], P(('fsdp', 'seq')), may hold values from -128 to 128
- out_second: float32 [2048, 1024], P(('fsdp', 'seq')), may hold values from 16.384 to 262.144
Outputs:
- mixed: bfloat16 [8192, 1024], P(('fsdp', 'seq'))
- grad_tokens: float32 [8192, 1024], P(('fsdp', 'seq'))
- new_norm_first: float32 [1024], replicated
- new_norm_second: float32 [1024], replicated
- new_norm_gain: float32 [1024], replicated
- new_in_first: float32 [1024, 4384], P(('fsdp', 'seq'))
- new_in_second: float32 [1024, 4384], P(('fsdp', 'seq'))
- new_in_weight: float32 [1024, 4384], P(('fsdp', 'seq'))
- new_conv_first: float32 [5, 2304], replicated
- new_conv_second: float32 [5, 2304], replicated
- new_conv_params: float32 [5, 2304], replicated
- new_head_first: float32 [3, 32], replicated
- new_head_second: float32 [3, 32], replicated
- new_head_params: float32 [3, 32], replicated
- new_gain_first: float32 [2048], replicated
- new_gain_second: float32 [2048], replicated
- new_out_gain: float32 [2048], replicated
- new_out_first: float32 [2048, 1024], P(('fsdp', 'seq'))
- new_out_second: float32 [2048, 1024], P(('fsdp', 'seq'))
- new_out_weight: float32 [2048, 1024], P(('fsdp', 'seq'))
Inputs may be any that keep to these rules, and one draw needn't show every extreme that they name: `doc_ids`: document numbers never fall along the stream; each document has 1 to 4096 tokens and one has exactly 4096.
All inputs are finite; a program needn't handle non-finite values.
Results may differ from a plain program's by a relative error of at most 0.0031.
The roundings to bfloat16 on the way count: a program that leaves them out, or rounds other values in their place, can miss the bound.
Values may be sent and summed in bfloat16 or wider, within the bound.
A program may use at most 128 MiB of HBM per device.

v0:
```python
import jax
import jax.numpy as jnp
from jax import lax
from jax.sharding import PartitionSpec as P

HEADS = 32
HEAD_DIM = 64
NSTATE = 128
CONV = 4
SPAN = 256
STEP = 10
INNER = 2048


EPS_NORM = 1e-05
BETA_ONE = 0.9
BETA_TWO = 0.999
ADAM_EPS = 1e-06
DECAY = 0.01
RATE = 0.5
PRECISE = lax.Precision.HIGHEST


def passed_along(shard, axis, by):
    peers = lax.axis_size(axis)
    pairs = [(i, i + by) for i in range(peers) if 0 <= i + by < peers]
    return lax.ppermute(shard, axis, pairs)


def prefix_2(part, axis, combine, identity, reverse):
    count = lax.axis_size(axis)
    place = lax.axis_index(axis)
    ahead = count - 1 - place if reverse else place
    gathered = jax.tree.map(lambda a: lax.all_gather(a, axis), part)
    state = jax.tree.map(lambda a, e: jnp.zeros_like(a) + jnp.asarray(e, a.dtype), part, identity)

    def one(hop, state):
        source = count - 1 - hop if reverse else hop
        return combine(
            state, jax.tree.map(lambda a: lax.dynamic_index_in_dim(a, source, 0, False), gathered)
        )

    return lax.fori_loop(0, ahead, one, state)


def convolve(extended, doc_window, kernel):
    rows_out = extended.shape[-2] - (CONV - 1)
    doc_now = doc_window[CONV - 1 :]
    result = kernel[CONV] + jnp.zeros(extended[..., CONV - 1 :, :].shape, jnp.float32)
    for offset in range(CONV):
        first_row = CONV - 1 - offset
        matched = (doc_window[first_row : first_row + rows_out] == doc_now)[:, None]
        result = result + jnp.where(
            matched, extended[..., first_row : first_row + rows_out, :] * kernel[offset], 0.0
        )
    return result


def convolve_back(extended, doc_window, kernel, grad_out):
    rows_out = grad_out.shape[0]
    doc_now = doc_window[CONV - 1 :]
    grad_ext = jnp.zeros(extended.shape, jnp.float32)
    kernel_rows = []
    for offset in range(CONV):
        first_row = CONV - 1 - offset
        matched = (doc_window[first_row : first_row + rows_out] == doc_now)[:, None]
        masked = jnp.where(matched, grad_out, 0.0)
        kernel_rows.append(jnp.sum(masked * extended[first_row : first_row + rows_out], axis=0))
        grad_ext = grad_ext.at[first_row : first_row + rows_out].add(masked * kernel[offset])
    kernel_rows.append(jnp.sum(grad_out, axis=0))
    return (grad_ext, jnp.stack(kernel_rows))


def span_masks(step_sizes, doc_span, doc_before, decay_rate):
    rows_in = doc_span.shape[0]
    cumulative = jnp.cumsum(step_sizes * decay_rate, axis=0)
    by_head = jnp.transpose(cumulative)
    below_diag = jnp.tril(jnp.ones((rows_in, rows_in), dtype=bool))
    matched = (doc_span[:, None] == doc_span[None, :]) & below_diag
    weights = jnp.where(
        matched[None], jnp.exp(jnp.minimum(by_head[:, :, None] - by_head[:, None, :], 0.0)), 0.0
    )
    rising = jnp.exp(cumulative) * (doc_span == doc_before).astype(jnp.float32)[:, None]
    ending = (
        jnp.exp(cumulative[-1][None, :] - cumulative)
        * (doc_span == doc_span[-1]).astype(jnp.float32)[:, None]
    )
    return (weights, rising, ending)


def chain_combine(earlier, later):
    return (earlier[0] * later[0], later[0][:, None, None] * earlier[1] + later[1])


def silu_slope(values_in):
    squashed = jax.nn.sigmoid(values_in)
    return squashed * (1.0 + values_in * (1.0 - squashed))


def adam_terms(weight, grad, first, second):
    first_new = BETA_ONE * first + (1.0 - BETA_ONE) * grad
    second_new = BETA_TWO * second + (1.0 - BETA_TWO) * grad * grad
    update = (
        first_new
        / (1.0 - BETA_ONE**STEP)
        / (jnp.sqrt(second_new / (1.0 - BETA_TWO**STEP)) + ADAM_EPS)
        + DECAY * weight
    )
    return (first_new, second_new, update)


def lamb_apply(weight, update, weight_sq, update_sq):
    return weight - RATE * (jnp.sqrt(weight_sq) / (jnp.sqrt(update_sq) + ADAM_EPS)) * update


def small_lamb(weight, grad, first, second):
    first_new, second_new, update = adam_terms(weight, grad, first, second)
    return (
        first_new,
        second_new,
        lamb_apply(weight, update, jnp.sum(weight * weight), jnp.sum(update * update)),
    )


def shards(
    tokens,
    cotangent,
    doc_ids,
    norm_gain,
    in_weight,
    conv_params,
    head_params,
    out_gain,
    out_weight,
    norm_first,
    norm_second,
    in_first,
    in_second,
    conv_first,
    conv_second,
    head_first,
    head_second,
    gain_first,
    gain_second,
    out_first,
    out_second,
):
    seq_count = lax.axis_size("seq")
    seq_index = lax.axis_index("seq")
    fsdp_index = lax.axis_index("fsdp")
    tok_rows = tokens.shape[0]
    group_rows = seq_count * tok_rows
    heads_here = HEADS // seq_count
    width_here = heads_here * HEAD_DIM
    span_count = group_rows // SPAN
    in_full, out_full = (
        lax.all_gather(in_weight.astype(jnp.bfloat16), ("fsdp", "seq"), axis=0, tiled=True),
        lax.all_gather(out_weight.astype(jnp.bfloat16), ("fsdp", "seq"), axis=0, tiled=True),
    )
    token_vals = tokens.astype(jnp.float32)
    inv_rms = lax.rsqrt(jnp.mean(token_vals * token_vals, axis=1, keepdims=True) + EPS_NORM)
    unit_tokens = token_vals * inv_rms
    normed = (unit_tokens * norm_gain).astype(jnp.bfloat16)
    projected = jnp.dot(normed, in_full, preferred_element_type=jnp.float32).astype(jnp.bfloat16)
    gate_vals = projected[:, :INNER].astype(jnp.float32)
    inner_raw = projected[:, INNER : 2 * INNER]
    state_proj = projected[:, 2 * INNER : 2 * INNER + 2 * NSTATE]
    step_raw = projected[:, 2 * INNER + 2 * NSTATE :]
    state_tiled = jnp.tile(state_proj, (1, seq_count))
    inner_heads, step_heads, state_heads = (
        lax.all_to_all(inner_raw, "seq", split_axis=1, concat_axis=0, tiled=True),
        lax.all_to_all(step_raw, "seq", split_axis=1, concat_axis=0, tiled=True),
        lax.all_to_all(state_tiled, "seq", split_axis=1, concat_axis=0, tiled=True),
    )
    doc_padded = jnp.concatenate([jnp.full((CONV - 1,), -1, dtype=jnp.int32), doc_ids])
    doc_window = lax.dynamic_slice(doc_padded, (fsdp_index * group_rows,), (group_rows + CONV - 1,))
    doc_now = doc_window[CONV - 1 :]
    doc_before = doc_window[CONV - 2 : CONV - 2 + group_rows : SPAN]
    doc_spans = doc_now.reshape(span_count, SPAN)
    channels = jnp.concatenate([inner_heads, state_heads], axis=1)
    edge_rows = passed_along(channels[group_rows - (CONV - 1) :], "fsdp", 1)
    extended = jnp.concatenate([edge_rows, channels], axis=0).astype(jnp.float32)
    kernel = jnp.concatenate(
        [
            lax.dynamic_slice(conv_params, (0, seq_index * width_here), (CONV + 1, width_here)),
            conv_params[:, INNER:],
        ],
        axis=1,
    )
    pre_act = convolve(extended, doc_window, kernel)
    activated_low = jax.nn.silu(pre_act).astype(jnp.bfloat16)
    activated = activated_low.astype(jnp.float32)
    inner_conv = activated[:, :width_here].reshape(span_count, SPAN, heads_here, HEAD_DIM)
    write_conv = activated[:, width_here : width_here + NSTATE].reshape(span_count, SPAN, NSTATE)
    read_conv = activated[:, width_here + NSTATE :].reshape(span_count, SPAN, NSTATE)
    write_low = activated_low[:, width_here : width_here + NSTATE].reshape(span_count, SPAN, NSTATE)
    read_low = activated_low[:, width_here + NSTATE :].reshape(span_count, SPAN, NSTATE)
    head_here = lax.dynamic_slice(head_params, (0, seq_index * heads_here), (3, heads_here))
    step_in = step_heads.astype(jnp.float32) + head_here[0]
    step_sizes = jax.nn.softplus(step_in).reshape(span_count, SPAN, heads_here)
    decay_rate = -jnp.exp(head_here[1])
    skip_gain = head_here[2]
    zero_state = jnp.zeros((heads_here, NSTATE, HEAD_DIM), jnp.float32)
    ones_head = jnp.ones((heads_here,), jnp.float32)

    def local_chain(carried, pieces):
        held_state, prefix = carried
        inner_c, write_c, steps_c, doc_c, before_c = pieces
        weights, rising, ending = span_masks(steps_c, doc_c, before_c, decay_rate)
        added_state = jnp.einsum(
            "jn,jhp->hnp",
            write_c,
            ending[:, :, None] * steps_c[:, :, None] * inner_c,
            precision=PRECISE,
        )
        decay_c = rising[-1]
        return (
            (decay_c[:, None, None] * held_state + added_state, prefix * decay_c),
            (held_state, prefix, decay_c),
        )

    (held_end, group_decay), (held_all, prefix_all, decay_all) = lax.scan(
        local_chain,
        (zero_state, ones_head),
        (inner_conv, write_conv, step_sizes, doc_spans, doc_before),
    )
    incoming = prefix_2(
        (group_decay, held_end), "fsdp", chain_combine, (ones_head, zero_state), False
    )
    entering = held_all + prefix_all[:, :, None, None] * incoming[1][None]

    def span_output(pieces):
        inner_c, write_c, read_c, write_b, read_b, steps_c, doc_c, before_c, state_c = pieces
        weights, rising, ending = span_masks(steps_c, doc_c, before_c, decay_rate)
        scores = jnp.dot(read_b, write_b.T, preferred_element_type=jnp.float32)
        scaled = steps_c[:, :, None] * inner_c
        within = jnp.einsum("hij,jhp->ihp", scores[None] * weights, scaled, precision=PRECISE)
        from_state = (
            jnp.einsum("in,hnp->ihp", read_c, state_c, precision=PRECISE) * rising[:, :, None]
        )
        return within + from_state + skip_gain[None, :, None] * inner_c

    ssd_out = lax.map(
        span_output,
        (
            inner_conv,
            write_conv,
            read_conv,
            write_low,
            read_low,
            step_sizes,
            doc_spans,
            doc_before,
            entering,
        ),
    )
    y_heads = ssd_out.reshape(group_rows, width_here).astype(jnp.bfloat16)
    y_tokens = lax.all_to_all(y_heads, "seq", split_axis=0, concat_axis=1, tiled=True).astype(
        jnp.float32
    )
    gate_act = jax.nn.silu(gate_vals)
    gated = y_tokens * gate_act
    inv_gated = lax.rsqrt(jnp.mean(gated * gated, axis=1, keepdims=True) + EPS_NORM)
    unit_gated = gated * inv_gated
    normed_out = (unit_gated * out_gain).astype(jnp.bfloat16)
    branch = jnp.dot(normed_out, out_full, preferred_element_type=jnp.float32)
    mixed = (token_vals + branch).astype(jnp.bfloat16)
    grad_out_full = jnp.dot(normed_out.T, cotangent, preferred_element_type=jnp.float32)
    grad_normed_out = jnp.dot(cotangent, out_full.T, preferred_element_type=jnp.float32)
    grad_out_gain = jnp.sum(grad_normed_out * unit_gated, axis=0)
    grad_unit = grad_normed_out * out_gain
    grad_gated = inv_gated * (
        grad_unit - unit_gated * jnp.mean(grad_unit * unit_gated, axis=1, keepdims=True)
    )
    grad_y = (grad_gated * gate_act).astype(jnp.bfloat16)
    grad_gate = grad_gated * y_tokens * silu_slope(gate_vals)
    grad_y_heads = (
        lax.all_to_all(grad_y, "seq", split_axis=1, concat_axis=0, tiled=True)
        .astype(jnp.float32)
        .reshape(span_count, SPAN, heads_here, HEAD_DIM)
    )

    def back_chain(carried, pieces):
        behind, suffix = carried
        read_c, steps_c, doc_c, before_c, grad_c = pieces
        weights, rising, ending = span_masks(steps_c, doc_c, before_c, decay_rate)
        pulled = jnp.einsum("in,ihp->hnp", read_c, rising[:, :, None] * grad_c, precision=PRECISE)
        decay_c = rising[-1]
        return ((pulled + decay_c[:, None, None] * behind, suffix * decay_c), (behind, suffix))

    (start_grad, unused_decay), (behind_all, suffix_all) = lax.scan(
        back_chain,
        (zero_state, ones_head),
        (read_conv, step_sizes, doc_spans, doc_before, grad_y_heads),
        reverse=True,
    )
    outgoing = prefix_2(
        (group_decay, start_grad), "fsdp", chain_combine, (ones_head, zero_state), True
    )
    leaving = behind_all + suffix_all[:, :, None, None] * outgoing[1][None]

    def span_grads(pieces):
        (
            inner_c,
            write_c,
            read_c,
            write_b,
            read_b,
            steps_c,
            doc_c,
            before_c,
            state_c,
            leave_c,
            grad_c,
        ) = pieces
        weights, rising, ending = span_masks(steps_c, doc_c, before_c, decay_rate)
        scores = jnp.dot(read_b, write_b.T, preferred_element_type=jnp.float32)
        mixing = scores[None] * weights
        scaled = steps_c[:, :, None] * inner_c
        from_state = jnp.einsum("jn,hnp->jhp", write_c, leave_c, precision=PRECISE)
        grad_scaled = (
            jnp.einsum("hij,ihp->jhp", mixing, grad_c, precision=PRECISE)
            + ending[:, :, None] * from_state
        )
        grad_mixing = jnp.einsum("ihp,jhp->hij", grad_c, scaled, precision=PRECISE)
        grad_scores = jnp.sum(grad_mixing * weights, axis=0)
        read_state = jnp.einsum("in,hnp->ihp", read_c, state_c, precision=PRECISE)
        grad_read = jnp.dot(grad_scores, write_c, precision=PRECISE) + jnp.einsum(
            "ihp,hnp->in", rising[:, :, None] * grad_c, state_c, precision=PRECISE
        )
        grad_write = jnp.dot(grad_scores.T, read_c, precision=PRECISE) + jnp.einsum(
            "jhp,hnp->jn", ending[:, :, None] * scaled, leave_c, precision=PRECISE
        )
        log_terms = grad_mixing * mixing
        grad_cum = jnp.transpose(jnp.sum(log_terms, axis=2) - jnp.sum(log_terms, axis=1))
        grad_rise = jnp.sum(grad_c * read_state, axis=2)
        grad_tail = jnp.sum(scaled * from_state, axis=2)
        grad_cum = grad_cum + grad_rise * rising - grad_tail * ending
        end_term = jnp.sum(grad_tail * ending, axis=0) + rising[-1] * jnp.sum(
            state_c * leave_c, axis=(1, 2)
        )
        grad_cum = grad_cum.at[-1].add(end_term)
        grad_log = jnp.flip(jnp.cumsum(jnp.flip(grad_cum, 0), axis=0), 0)
        grad_steps = grad_log * decay_rate + jnp.sum(inner_c * grad_scaled, axis=2)
        grad_inner = steps_c[:, :, None] * grad_scaled + skip_gain[None, :, None] * grad_c
        grad_rate = jnp.sum(grad_log * steps_c, axis=0)
        grad_skip = jnp.sum(inner_c * grad_c, axis=(0, 2))
        return (grad_inner, grad_write, grad_read, grad_steps, grad_rate, grad_skip)

    grad_inner, grad_write, grad_read, grad_steps, grad_rate, grad_skip = lax.map(
        span_grads,
        (
            inner_conv,
            write_conv,
            read_conv,
            write_low,
            read_low,
            step_sizes,
            doc_spans,
            doc_before,
            entering,
            leaving,
            grad_y_heads,
        ),
    )
    grad_act = jnp.concatenate(
        [
            grad_inner.reshape(group_rows, width_here),
            grad_write.reshape(group_rows, NSTATE),
            grad_read.reshape(group_rows, NSTATE),
        ],
        axis=1,
    )
    grad_pre = grad_act * silu_slope(pre_act)
    grad_ext, grad_kernel = convolve_back(extended, doc_window, kernel, grad_pre)
    edge_grad = passed_along(grad_ext[: CONV - 1], "fsdp", -1)
    grad_channels = grad_ext[CONV - 1 :].at[group_rows - (CONV - 1) :].add(edge_grad)
    grad_step_raw = grad_steps.reshape(group_rows, heads_here) * jax.nn.sigmoid(step_in)
    back_inner, back_step, back_state = (
        lax.all_to_all(
            grad_channels[:, :width_here].astype(jnp.bfloat16),
            "seq",
            split_axis=0,
            concat_axis=1,
            tiled=True,
        ),
        lax.all_to_all(
            grad_step_raw.astype(jnp.bfloat16), "seq", split_axis=0, concat_axis=1, tiled=True
        ),
        lax.all_to_all(
            grad_channels[:, width_here:].astype(jnp.bfloat16),
            "seq",
            split_axis=0,
            concat_axis=1,
            tiled=True,
        ),
    )
    state_total = jnp.sum(
        back_state.astype(jnp.float32).reshape(tok_rows, seq_count, 2 * NSTATE), axis=1
    )
    grad_proj = jnp.concatenate(
        [grad_gate, back_inner.astype(jnp.float32), state_total, back_step.astype(jnp.float32)],
        axis=1,
    ).astype(jnp.bfloat16)
    grad_in_full = jnp.dot(normed.T, grad_proj, preferred_element_type=jnp.float32)
    grad_normed = jnp.dot(grad_proj, in_full.T, preferred_element_type=jnp.float32)
    grad_norm_gain = jnp.sum(grad_normed * unit_tokens, axis=0)
    grad_unit_tok = grad_normed * norm_gain
    grad_tokens = cotangent.astype(jnp.float32) + inv_rms * (
        grad_unit_tok - unit_tokens * jnp.mean(grad_unit_tok * unit_tokens, axis=1, keepdims=True)
    )
    grad_conv = lax.dynamic_update_slice(
        jnp.zeros(conv_params.shape, jnp.float32),
        grad_kernel[:, :width_here],
        (0, seq_index * width_here),
    )
    grad_conv = grad_conv.at[:, INNER:].set(grad_kernel[:, width_here:])
    head_rows = jnp.stack(
        [
            jnp.sum(grad_step_raw, axis=0),
            jnp.sum(grad_rate, axis=0) * decay_rate,
            jnp.sum(grad_skip, axis=0),
        ]
    )
    grad_head = lax.dynamic_update_slice(
        jnp.zeros(head_params.shape, jnp.float32), head_rows, (0, seq_index * heads_here)
    )
    norm_total, gain_total, conv_total, head_total = lax.psum(
        (grad_norm_gain, grad_out_gain, grad_conv, grad_head), ("fsdp", "seq")
    )
    grad_in_w, grad_out_w = (
        lax.psum_scatter(grad_in_full, ("fsdp", "seq"), scatter_dimension=0, tiled=True),
        lax.psum_scatter(grad_out_full, ("fsdp", "seq"), scatter_dimension=0, tiled=True),
    )
    in_first_new, in_second_new, in_update = adam_terms(in_weight, grad_in_w, in_first, in_second)
    out_first_new, out_second_new, out_update = adam_terms(
        out_weight, grad_out_w, out_first, out_second
    )
    square_terms = jnp.stack(
        [
            jnp.sum(in_weight * in_weight),
            jnp.sum(in_update * in_update),
            jnp.sum(out_weight * out_weight),
            jnp.sum(out_update * out_update),
        ]
    )
    square_totals = lax.psum(square_terms, ("fsdp", "seq"))
    in_new = lamb_apply(in_weight, in_update, square_totals[0], square_totals[1])
    out_new = lamb_apply(out_weight, out_update, square_totals[2], square_totals[3])
    norm_f, norm_s, norm_w = small_lamb(norm_gain, norm_total, norm_first, norm_second)
    conv_f, conv_s, conv_w = small_lamb(conv_params, conv_total, conv_first, conv_second)
    head_f, head_s, head_w = small_lamb(head_params, head_total, head_first, head_second)
    gain_f, gain_s, gain_w = small_lamb(out_gain, gain_total, gain_first, gain_second)
    return (
        mixed,
        grad_tokens,
        norm_f,
        norm_s,
        norm_w,
        in_first_new,
        in_second_new,
        in_new,
        conv_f,
        conv_s,
        conv_w,
        head_f,
        head_s,
        head_w,
        gain_f,
        gain_s,
        gain_w,
        out_first_new,
        out_second_new,
        out_new,
    )


def solution(mesh):
    placed = (
        P(("fsdp", "seq"), None),
        P(("fsdp", "seq"), None),
        P(),
        P(),
        P(("fsdp", "seq"), None),
        P(),
        P(),
        P(),
        P(("fsdp", "seq"), None),
        P(),
        P(),
        P(("fsdp", "seq"), None),
        P(("fsdp", "seq"), None),
        P(),
        P(),
        P(),
        P(),
        P(),
        P(),
        P(("fsdp", "seq"), None),
        P(("fsdp", "seq"), None),
    )
    return jax.shard_map(
        shards,
        mesh=mesh,
        in_specs=placed,
        out_specs=(
            P(("fsdp", "seq"), None),
            P(("fsdp", "seq"), None),
            P(),
            P(),
            P(),
            P(("fsdp", "seq"), None),
            P(("fsdp", "seq"), None),
            P(("fsdp", "seq"), None),
            P(),
            P(),
            P(),
            P(),
            P(),
            P(),
            P(),
            P(),
            P(),
            P(("fsdp", "seq"), None),
            P(("fsdp", "seq"), None),
            P(("fsdp", "seq"), None),
        ),
        check_vma=False,
    )
```

profile of v0, /device:TPU:0, one launch (start us, length us, event | category | flops | bytes accessed | tf_op | source)
XLA Modules:
  0.0 1468.6 jit_solution(11913776922837712794)
XLA Ops:
  10.3 84.6 %all-gather.8.cloned.1.call-done = bf16[1024,4384]{1,0:T(8,128)(2,1)} async-done(((bf16[32,4384]{1,0:T(8,128)(2,1)}), bf16[1024,4384]{1,0:T(8,128)(2,1)}) %all-gather.8.cloned.1.call-update) | async-done | bytes 8978448 | tf_op jit(solution)/shard_map/all_gather | solution.py:157
  94.9 7.6 convolution_convert_fusion
  119.0 10.9 all-to-all-done.1
  155.5 17.8 %while.113 = (s32[]{:T(128)}, f32[16,128,64]{1,2,0:T(8,128)S(1)}, f32[16]{0:T(128)S(1)}, f32[2,16,128,64]{2,3,1,0:T(8,128)}, f32[2,16]{1,0:T(2,128)S(1)}, /*inde...) while((s32[]{:T(128)}, f32[16,128,64]{1,2,0:T(8,128)S(1)}, ...), condition=%wide.region_4.5_spmd.clone.clone, body=%wide.region_1.4_spmd.clone.sunk.clone | while | flops 403985504 | bytes 3448788 | solution.py:222
  176.7 31.8 %all-reduce.2 = f32[256]{0:T(256)S(1)} all-reduce(f32[256]{0:T(256)S(1)} %dynamic-update-slice.24), channel_id=2, replica_groups=mesh['fsdp'=16,'seq'=2] {'fsdp'}, use_global_device_ids=true, to_apply=%add.2 | all-reduce | flops 256 | bytes 2048
  210.4 40.3 %all-gather.12.cloned.1.call-done = f32[256,128,64]{1,2,0:T(8,128)} async-done(((f32[16,128,64]{1,2,0:T(8,128)}), f32[256,128,64]{1,2,0:T(8,128)}) %all-gather.12.cloned.1.call-update) | async-done | bytes 8388624 | tf_op jit(solution)/shard_map/all_gather | solution.py:34
  256.9 26.1 %while.110 = (s32[]{:T(128)}, bf16[2,256,16,64]{1,3,2,0:T(8,128)(2,1)}, f32[2,256,16]{1,2,0:T(8,128)S(1)}, f32[2,256,16,64]{1,3,2,0:T(8,128)}, bf16[2,256,128]{2...) while((s32[]{:T(128)}, ...), condition=%wide.region_10.11_spmd.clone, body=%wide.region_7.10_spmd.sunk.clone | while | flops 1230975488 | bytes 24765880 | solution.py:243
  263.2 5.7 fusion.305
  276.3 5.7 fusion.305
  283.0 14.1 all_to_all.107
  306.0 255.9 %reduce-scatter.5.cloned.1.call-done = f32[64,1024]{1,0:T(8,128)} async-done(((f32[2048,1024]{1,0:T(8,128)}), f32[64,1024]{1,0:T(8,128)}) %reduce-scatter.5.cloned.1.call-update) | async-done | bytes 262160 | tf_op jit(solution)/shard_map/reduce_scatter | solution.py:433
  564.9 62.9 %all-gather.10.cloned.1.call-done = bf16[2048,1024]{1,0:T(8,128)(2,1)} async-done(((bf16[64,1024]{1,0:T(8,128)(2,1)}), bf16[2048,1024]{1,0:T(8,128)(2,1)}) %all-gather.10.cloned.1.call-update) | async-done | bytes 4194320 | tf_op jit(solution)/shard_map/all_gather | solution.py:158
  627.8 5.2 multiply_reduce_fusion.9
  640.9 14.3 all-to-all-done.4
  659.1 12.7 while.114
  672.6 73.3 %all-gather.14.cloned.1.call-done = f32[256,128,64]{1,2,0:T(8,128)} async-done(((f32[16,128,64]{1,2,0:T(8,128)}), f32[256,128,64]{1,2,0:T(8,128)}) %all-gather.14.cloned.1.call-update) | async-done | bytes 8388624 | tf_op jit(solution)/shard_map/all_gather | solution.py:34
  747.1 76.4 %while.111 = (s32[]{:T(128)}, f32[16,128,64]{2,1,0:T(8,128)}, s32[]{:T(128)}, f32[16,16]{1,0:T(8,128)S(1)}, f32[16,16,128,64]{2,3,1,0:T(8,128)}) while((s32[]{:T(128)}, f32[16,128,64]{2,1,0:T(8,128)}, s32[]{:T(128)}, f32[16,16]{1,0:T(8,128)S(1)}, f32[16,16,128,64]{2,3,1,0:T(8,128)}) %tuple.357), condition=%wide.region_18.19_spmd.clone, body=%wide.region_17.18_spmd.sunk.clone | while | flops 262150 | bytes 3670331 | solution.py:43
  830.1 89.6 %while.112 = (s32[]{:T(128)}, f32[2,256,16,64]{1,3,2,0:T(8,128)}, f32[2,256,128]{2,1,0:T(8,128)}, f32[2,256,128]{2,1,0:T(8,128)}, f32[2,256,16]{1,2,0:T(8,128)},...) while((s32[]{:T(128)}, f32[2,256,16,64]{1,3,2,0:T(8,128)}, ...), condition=%wide.region_34.35_spmd.clone, body=%wide.region_19.34_spmd.sunk.clone | while | flops 3459240960 | bytes 51248944 | solution.py:350
  851.6 6.7 bitcast_dynamic-update-slice_fusion.12
  860.2 5.9 fusion.325
  891.3 6.7 bitcast_dynamic-update-slice_fusion.12
  899.9 5.9 fusion.325
  919.7 4.8 copy.142
  924.6 4.9 reshape.733
  939.6 7.5 scatter-add.22
  950.9 7.4 scatter-add.25
  971.6 5.3 all-to-all-done.6
  981.3 13.3 all-to-all-done.5
  1001.7 10.3 fusion.159
  1019.3 7.2 fusion.156
  1028.0 370.1 %reduce-scatter.3.cloned.1.call-done = f32[32,4384]{1,0:T(8,128)} async-done(((f32[1024,4384]{1,0:T(8,128)}), f32[32,4384]{1,0:T(8,128)}) %reduce-scatter.3.cloned.1.call-update) | async-done | bytes 561168 | tf_op jit(solution)/shard_map/reduce_scatter | solution.py:432
  1403.0 41.5 %all-reduce.3 = (f32[1024]{0:T(1024)S(1)}, f32[4]{0:T(128)S(1)}, f32[5,2304]{1,0:T(8,128)S(1)}, f32[3,32]{1,0:T(4,128)S(1)}, f32[2048]{0:T(1024)S(1)}) all-reduce(f32[1024]{0:T(1024)S(1)} %get-tuple-element.1108, f32[4]{0:T(128)S(1)} %pad_maximum_fusion.6, ...), channel_id=1, replica_groups=mesh['fsdp'=16,'seq'=2] {'fsdp','seq'}, use_global_device_ids=true, to_apply=%region_38.39 | all-reduce | flops 14692 | bytes 117536 | tf_op jit(solution)/shard_map/psum | solution.py:428
  (569 shorter events, 323.1 us)
Async XLA Ops:
  7.2 87.8 %all-gather.8.cloned.1.call-start = ((), (), s32[]{:S(2)}) async-start(), calls=%async_computation.10 | async-start | bytes 9461760 | tf_op jit(solution)/shard_map/all_gather | solution.py:157
  103.5 9.3 all-to-all-start.2
  112.8 17.1 %all-to-all-start.1 = ((bf16[256,2,1024]{2,0,1:T(8,128)(2,1)}), bf16[256,2,1024]{2,0,1:T(8,128)(2,1)S(1)}, u32[]{:S(2)}, u32[]{:S(2)}) async-start(bf16[256,2,1024]{2,0,1:T(8,128)(2,1)} %copy.125), calls=%async_computation.1 | async-start | bytes 2097152 | tf_op jit(solution)/shard_map/all_to_all | solution.py:171
  129.9 7.1 all-to-all-start
  133.1 117.5 %all-gather.12.cloned.1.call-start = ((), (), s32[]{:S(2)}) async-start(), calls=%async_computation.14 | async-start | bytes 8912896 | tf_op jit(solution)/shard_map/all_gather | solution.py:34
  133.2 3.9 collective-permute-start
  174.2 387.8 %reduce-scatter.5.cloned.1.call-start = ((), (), s32[]{:S(2)}) async-start(), calls=%async_computation.13 | async-start | bytes 8650752 | tf_op jit(solution)/shard_map/reduce_scatter | solution.py:433
  300.2 332.8 %copy-start.70 = (f32[256]{0:T(256)}, f32[256]{0:T(256)S(1)}, u32[]{:S(2)}) copy-start(f32[256]{0:T(256)S(1)} %add_rsqrt_fusion) | copy-start | bytes 3076
  306.0 321.8 %all-gather.10.cloned.1.call-start = ((), (), s32[]{:S(2)}) async-start(), calls=%async_computation.11 | async-start | bytes 4325376 | tf_op jit(solution)/shard_map/all_gather | solution.py:158
  636.4 18.8 %all-to-all-start.4 = ((bf16[256,2,1024]{0,2,1:T(8,128)(2,1)}), bf16[256,2,1024]{0,2,1:T(8,128)(2,1)}, u32[]{:S(2)}, u32[]{:S(2)}) async-start(bf16[256,2,1024]{0,2,1:T(8,128)(2,1)} %bitcast.738), calls=%async_computation.4 | async-start | bytes 2097152 | tf_op jit(solution)/shard_map/all_to_all | solution.py:278
  640.8 105.1 %all-gather.14.cloned.1.call-start = ((), (), s32[]{:S(2)}) async-start(), calls=%async_computation.15 | async-start | bytes 8912896 | tf_op jit(solution)/shard_map/all_gather | solution.py:34
  962.0 3.3 collective-permute-start.1
  967.0 9.9 all-to-all-start.6
  976.9 17.7 %all-to-all-start.5 = ((bf16[2,256,1024]{2,1,0:T(8,128)(2,1)}), bf16[2,256,1024]{2,1,0:T(8,128)(2,1)S(1)}, u32[]{:S(2)}, u32[]{:S(2)}) async-start(bf16[2,256,1024]{2,1,0:T(8,128)(2,1)} %bitcast.736), calls=%async_computation.5 | async-start | bytes 2097152 | tf_op jit(solution)/shard_map/all_to_all | solution.py:380
  994.6 7.1 all-to-all-start.7
  997.8 400.3 %reduce-scatter.3.cloned.1.call-start = ((), (), s32[]{:S(2)}) async-start(), calls=%async_computation.12 | async-start | bytes 18923520 | tf_op jit(solution)/shard_map/reduce_scatter | solution.py:432
  1026.5 371.6 %copy-start.17 = (f32[32,4384]{1,0:T(8,128)S(1)}, f32[32,4384]{1,0:T(8,128)}, u32[]{:S(2)}) copy-start(f32[32,4384]{1,0:T(8,128)} %param.51) | copy-start | bytes 1683460
  1026.5 371.6 %copy-start.31 = (f32[32,4384]{1,0:T(8,128)S(1)}, f32[32,4384]{1,0:T(8,128)}, u32[]{:S(2)}) copy-start(f32[32,4384]{1,0:T(8,128)} %param.58) | copy-start | bytes 1683460
  1026.5 376.5 %copy-start.78 = (f32[2048]{0:T(1024)S(1)}, f32[2048]{0:T(1024)}, u32[]{:S(2)}) copy-start(f32[2048]{0:T(1024)} %get-tuple-element.1105) | copy-start | bytes 24580
  1026.5 417.9 %copy-start.82 = (f32[1024]{0:T(1024)S(1)}, f32[1024]{0:T(1024)}, u32[]{:S(2)}) copy-start(f32[1024]{0:T(1024)} %param.57) | copy-start | bytes 12292
  1026.5 417.9 %copy-start.83 = (f32[1024]{0:T(1024)S(1)}, f32[1024]{0:T(1024)}, u32[]{:S(2)}) copy-start(f32[1024]{0:T(1024)} %param.56) | copy-start | bytes 12292
  1026.6 421.9 %copy-start.34 = (f32[5,2304]{1,0:T(8,128)S(1)}, f32[5,2304]{1,0:T(8,128)}, u32[]{:S(2)}) copy-start(f32[5,2304]{1,0:T(8,128)} %param.52) | copy-start | bytes 138244
  1026.6 421.9 %copy-start.58 = (f32[5,2304]{1,0:T(8,128)S(1)}, f32[5,2304]{1,0:T(8,128)}, u32[]{:S(2)}) copy-start(f32[5,2304]{1,0:T(8,128)} %param.61) | copy-start | bytes 138244
  1026.6 421.9 %copy-start.59 = (f32[5,2304]{1,0:T(8,128)S(1)}, f32[5,2304]{1,0:T(8,128)}, u32[]{:S(2)}) copy-start(f32[5,2304]{1,0:T(8,128)} %param.60) | copy-start | bytes 138244
  1027.9 422.8 %copy-start.67 = (f32[3,32]{1,0:T(4,128)S(1)}, f32[3,32]{1,0:T(4,128)}, u32[]{:S(2)}) copy-start(f32[3,32]{1,0:T(4,128)} %param.53) | copy-start | bytes 1156
  1027.9 422.8 %copy-start.84 = (f32[3,32]{1,0:T(4,128)S(1)}, f32[3,32]{1,0:T(4,128)}, u32[]{:S(2)}) copy-start(f32[3,32]{1,0:T(4,128)} %param.63) | copy-start | bytes 1156
  1027.9 422.8 %copy-start.85 = (f32[3,32]{1,0:T(4,128)S(1)}, f32[3,32]{1,0:T(4,128)}, u32[]{:S(2)}) copy-start(f32[3,32]{1,0:T(4,128)} %param.62) | copy-start | bytes 1156
  1027.9 425.4 %copy-start.76 = (f32[2048]{0:T(1024)S(1)}, f32[2048]{0:T(1024)}, u32[]{:S(2)}) copy-start(f32[2048]{0:T(1024)} %param.65) | copy-start | bytes 24580
  1027.9 425.4 %copy-start.77 = (f32[2048]{0:T(1024)S(1)}, f32[2048]{0:T(1024)}, u32[]{:S(2)}) copy-start(f32[2048]{0:T(1024)} %param.64) | copy-start | bytes 24580
  1027.9 432.6 %copy-start.28 = (f32[64,1024]{1,0:T(8,128)S(1)}, f32[64,1024]{1,0:T(8,128)}, u32[]{:S(2)}) copy-start(f32[64,1024]{1,0:T(8,128)} %param.55) | copy-start | bytes 786436
  1028.0 432.5 %copy-start.29 = (f32[64,1024]{1,0:T(8,128)S(1)}, f32[64,1024]{1,0:T(8,128)}, u32[]{:S(2)}) copy-start(f32[64,1024]{1,0:T(8,128)} %get-tuple-element.1282) | copy-start | bytes 786436
  1028.0 432.5 %copy-start.30 = (f32[64,1024]{1,0:T(8,128)S(1)}, f32[64,1024]{1,0:T(8,128)}, u32[]{:S(2)}) copy-start(f32[64,1024]{1,0:T(8,128)} %get-tuple-element.1283) | copy-start | bytes 786436
  (88 other events, 1197.5 us)
Sparse Core Ops, SparseCore 0:
  11.4 83.4 all-gather.7
  174.3 76.3 all-gather.11
  306.1 255.7 reduce-scatter.4
  565.3 62.4 all-gather.9
  672.7 73.2 all-gather.13
  1012.2 385.8 reduce-scatter.2
where the time goes:
time: 1480 us; the launch traced here: 1470 us
  waiting for transfers between devices  938 us (63%)
  local copies, waits for them, and re-layouts  138 us (9%)
  other arithmetic  130 us (9%)
  matrix products  111 us (8%)
  blocking collectives  87.3 us (6%)
  starting transfers between devices  28.4 us (2%)
  between operations  24.7 us (2%)
    reduce_scatter x1, waiting for transfers between devices, shards(): lax.psum_scatter(grad_in_full, ('fsdp', 'seq'), scatter_dimension=0, tile...  370 us
    reduce_scatter x1, waiting for transfers between devices, shards(): lax.psum_scatter(grad_out_full, ('fsdp', 'seq'), scatter_dimension=0, til...  256 us
    all_gather x2, waiting for transfers between devices, prefix_2(): gathered = jax.tree.map(lambda a: lax.all_gather(a, axis), part)  114 us
    all_gather x1, waiting for transfers between devices, shards(): lax.all_gather(in_weight.astype(jnp.bfloat16), ('fsdp', 'seq'), axis=0, t...  84.6 us
    all_gather x1, waiting for transfers between devices, shards(): lax.all_gather(out_weight.astype(jnp.bfloat16), ('fsdp', 'seq'), axis=0,...  62.9 us
    psum x1, blocking collectives, shards(): lax.psum((grad_norm_gain, grad_out_gain, grad_conv, grad_head), ('fsdp',...  41.5 us
    add x15, other arithmetic, chain_combine(): later[0][:, None, None] * earlier[1] + later[1]  40.3 us
    dynamic_slice x30, local copies, waits for them, and re-layouts, one(): lax.dynamic_index_in_dim(a, source, 0, False)  36 us
  transfers between devices with their start and end apart: 15, of which 13 were waited for; matrix products, arithmetic and copies ran while one was open for 2% of the time, Pallas kernels for 0%

commit v1 on v0

v1 whole, which is shorter than its diff:
```python
import functools

import jax
import jax.numpy as jnp
from jax import lax
from jax.experimental import pallas as pl
from jax.experimental.pallas import tpu as pltpu
from jax.sharding import Mesh, PartitionSpec as P

HEADS = 32
HEAD_DIM = 64
NSTATE = 128
CONV = 4
SPAN = 256
STEP = 10
INNER = 2048
D = 1024

EPS_NORM = 1e-05
BETA_ONE = 0.9
BETA_TWO = 0.999
ADAM_EPS = 1e-06
DECAY = 0.01
RATE = 0.5

PLANE = 8
HERE = HEADS // PLANE
WIDE = HERE * HEAD_DIM
STATES = 2 * NSTATE
LOCAL = WIDE + STATES
PACK = NSTATE + 8
MAIN = 2 * WIDE
SHARED = STATES + 128
SMALL = 24
TP = ("sub", "seq")
ALL = ("grp", "sub", "seq")

f32 = jnp.float32
bf16 = jnp.bfloat16


def dot(a, b, ca=1, cb=0):
    return lax.dot_general(a, b, (((ca,), (cb,)), ((), ())), preferred_element_type=f32)


def split2(x):
    high = x.astype(bf16)
    return high, (x - high.astype(f32)).astype(bf16)


def split3(x):
    high = x.astype(bf16)
    rest = x - high.astype(f32)
    mid = rest.astype(bf16)
    return high, mid, (rest - mid.astype(f32)).astype(bf16)


def exact_left(a, b, ca=1, cb=0):
    high, low = split2(b)
    return dot(a, high, ca, cb) + dot(a, low, ca, cb)


def exact_right(a, b, ca=1, cb=0):
    high, low = split2(a)
    return dot(high, b, ca, cb) + dot(low, b, ca, cb)


def both_split(a, b, ca=1, cb=0):
    ah, al = split2(a)
    bh, bl = split2(b)
    return dot(ah, bh, ca, cb) + dot(al, bh, ca, cb) + dot(ah, bl, ca, cb)


def running(mask, x):
    a, b, c = split3(x)
    return dot(mask, a) + dot(mask, b) + dot(mask, c)


def spread(cols):
    lane = lax.broadcasted_iota(jnp.int32, (cols.shape[0], 128), 1)
    halves = [
        jnp.where(lane < HEAD_DIM, cols[:, 2 * i : 2 * i + 1], cols[:, 2 * i + 1 : 2 * i + 2])
        for i in range(HERE // 2)
    ]
    return jnp.concatenate(halves, axis=1)


def head_sum(x):
    row = lax.broadcasted_iota(jnp.int32, (WIDE, 128), 0)
    lane = lax.broadcasted_iota(jnp.int32, (WIDE, 128), 1)
    pick = (row // HEAD_DIM == lane).astype(bf16)
    return exact_right(x, pick)


def sigmoid(x):
    return 1.0 / (1.0 + jnp.exp(-x))


def half_tanh(x):
    return 0.5 * jnp.tanh(0.5 * x) + 0.5


def silu(x):
    return x * half_tanh(x)


def silu_slope(x):
    s = half_tanh(x)
    return s * (1.0 + x * (1.0 - s))


def lower(rows):
    i = lax.broadcasted_iota(jnp.int32, (rows, rows), 0)
    j = lax.broadcasted_iota(jnp.int32, (rows, rows), 1)
    return j <= i


def head_mask(x, h):
    lane = lax.broadcasted_iota(jnp.int32, x.shape, 1)
    return jnp.where(lane // HEAD_DIM == h, x, jnp.zeros_like(x))


def pack_kernel(wi_ref, wo_ref, main_ref, shared_ref, out_ref):
    weight = wi_ref[...].astype(bf16)
    for base in (0, 1):
        for t in range(PLANE):
            lanes = slice(HEAD_DIM * (t % 2), HEAD_DIM * (t % 2 + 1))
            for half in range(HERE // 2):
                tiles = []
                for i in (2 * half, 2 * half + 1):
                    at = base * INNER + i * PLANE * HEAD_DIM + t // 2 * 128
                    tiles.append(weight[:, at : at + 128][:, lanes])
                at = base * WIDE + 128 * half
                main_ref[t, :, at : at + 128] = jnp.concatenate(tiles, axis=1)
    shared_ref[...] = jnp.zeros_like(shared_ref)
    shared_ref[:, : STATES + HEADS] = weight[:, 2 * INNER :]
    out_ref[...] = wo_ref[...].astype(bf16)


def prepare(
    group, place, conv_ref, head_ref, gain_ref,
    conv_out, bias_out, rate_out, skip_out, gain_out, pick_out, before_out, behind_out,
):
    pair = jnp.where(place >= 2, 1, 0) + jnp.where(place >= 4, 1, 0) + jnp.where(place >= 6, 1, 0)
    odd = place - 2 * pair == 1

    def half(x):
        return jnp.where(odd, x[:, HEAD_DIM:], x[:, :HEAD_DIM])

    def four(get):
        halves = [half(get(i)) for i in range(HERE)]
        return [jnp.concatenate(halves[2 * i : 2 * i + 2], axis=1) for i in range(HERE // 2)]

    conv_out[...] = jnp.zeros_like(conv_out)
    columns = lambda i: conv_ref[:, pl.ds(pl.multiple_of(i * PLANE * HEAD_DIM + pair * 128, 128), 128)]
    for i, tile in enumerate(four(columns)):
        conv_out[0 : CONV + 1, 128 * i : 128 * (i + 1)] = tile
    conv_out[0 : CONV + 1, WIDE:] = conv_ref[:, INNER:]
    for i, tile in enumerate(four(lambda i: gain_ref[pl.ds(i * PLANE // 2 + pair, 1), :])):
        gain_out[:, 128 * i : 128 * (i + 1)] = tile
    head = lax.broadcasted_iota(jnp.int32, (3, HEADS), 1)
    lane = lax.broadcasted_iota(jnp.int32, (3, 128), 1)
    mine = jnp.zeros((3, 128), f32)
    for i in range(HERE):
        one = jnp.sum(jnp.where(head == PLANE * i + place, head_ref[...], 0.0), axis=1, keepdims=True)
        mine = mine + jnp.where(lane == i, one, 0.0)
    bias_out[...] = mine[0:1]
    rate_out[...] = jnp.where(lane[0:1] < HERE, -jnp.exp(mine[1:2]), 0.0)
    skip_out[...] = spread(jnp.broadcast_to(mine[2:3], (8, 128)))[0:1]
    row = lax.broadcasted_iota(jnp.int32, (128, 128), 0)
    column = lax.broadcasted_iota(jnp.int32, (128, 128), 1)
    pick_out[...] = jnp.where((row == PLANE * column + place) & (row < HEADS), 1.0, 0.0).astype(bf16)
    rank = lax.broadcasted_iota(jnp.int32, before_out.shape, 0)
    before_out[...] = (rank < group).astype(f32)
    behind_out[...] = (rank > group).astype(f32)


def flags_of(z, docs, flags, doc_rows):
    lines = PLANE * SPAN // 128
    lane = lax.broadcasted_iota(jnp.int32, (1, 128), 1)
    total = docs.shape[0]
    first = z * lines

    def line(i):
        at = first + i
        inside = jnp.clip(at, 0, total - 1)
        got = docs[pl.ds(inside, 1), :].astype(f32)
        return jnp.where(at < 0, -1.0, jnp.where(at >= total, -2.0, got))

    rows = [line(i) for i in range(-1, lines + 1)]
    for i in range(lines + 1):
        now, last = rows[i + 1], rows[i]
        same = []
        for k in range(1, CONV):
            moved = jnp.where(lane < k, pltpu.roll(last, k, 1), pltpu.roll(now, k, 1))
            same.append((moved == now).astype(f32))
        span = min(i, lines - 1) // 2
        rise = (now == rows[2 * span][:, 127:128]).astype(f32)
        tail = (now == rows[2 * span + 2][:, 127:128]).astype(f32)
        both = jnp.concatenate([*same, rise, tail, now, now * 0.0, now * 0.0], axis=0).T
        if i < lines:
            flags[128 * i : 128 * (i + 1), :] = both
            doc_rows[i // 2, :, 128 * (i % 2) : 128 * (i % 2 + 1)] = now
        else:
            flags[128 * i : 128 * i + 8, :] = both[0:8, :]


def prep_kernel(at_ref, *refs):
    prepare(at_ref[0], at_ref[1], *refs)


def normalize(rows, gain):
    vals = rows.astype(f32)
    inv = lax.rsqrt(jnp.mean(vals * vals, axis=1, keepdims=True) + EPS_NORM)
    return (vals * inv * gain).astype(bf16)


def first_begin(halo_ref, ng_ref, wm_ref, ws_ref, edge_ref, ext, state, decay):
    before = normalize(halo_ref[...], ng_ref[...])
    inner = dot(before, wm_ref[:, WIDE : 2 * WIDE]).astype(bf16).astype(f32)
    shared = dot(before, ws_ref[:, :STATES]).astype(bf16).astype(f32)
    rows = jnp.concatenate([inner, shared], axis=1)[8:16]
    ext[SPAN : SPAN + 8, :] = rows
    edge_ref[...] = rows
    state[...] = jnp.zeros_like(state)
    decay[...] = jnp.ones_like(decay)


def first_phase(
    span, x_ref, halo_ref, ng_ref, wm_ref, ws_ref, pick_ref, conv_ref, bias_ref, rate_ref, fl_ref,
    normed_ref, gate_ref, chan_ref, pre_ref, act_ref, dt_ref, cum_ref, held_ref, pref_ref, edge_ref,
    ext, state, decay, end_ref, act_all, dt_all, cum_all,
):
    ext[0:8, :] = ext[SPAN : SPAN + 8, :]
    normed = normalize(x_ref[...], ng_ref[...])
    normed_ref[...] = normed
    main = dot(normed, wm_ref[...]).astype(bf16)
    shared = dot(normed, ws_ref[...]).astype(bf16)
    gate_ref[...] = main[:, :WIDE]
    chan = jnp.concatenate([main[:, WIDE:], shared[:, :STATES]], axis=1)
    chan_ref[...] = chan
    ext[8 : SPAN + 8, :] = chan.astype(f32)
    flags = fl_ref[...]
    pre = conv_ref[4:5, :] + ext[8 : SPAN + 8, :] * conv_ref[0:1, :]
    for k in range(1, CONV):
        moved = ext[8 - k : SPAN + 8 - k, :] * conv_ref[k : k + 1, :]
        pre = pre + jnp.where(flags[:, k - 1 : k] > 0.5, moved, 0.0)
    pre_ref[...] = pre
    act = silu(pre).astype(bf16)
    act_ref[...] = act
    act_all[span] = act
    step = dot(shared[:, STATES:], pick_ref[...]) + bias_ref[...]
    dt = jnp.maximum(step, 0.0) + jnp.log1p(jnp.exp(-jnp.abs(step)))
    lane = lax.broadcasted_iota(jnp.int32, dt.shape, 1)
    both = jnp.where(lane < HEAD_DIM, dt, pltpu.roll(sigmoid(step), HEAD_DIM, 1))
    dt_ref[...] = both
    dt_all[span] = both
    cum = running(lower(SPAN).astype(bf16), dt * rate_ref[...])
    cum_ref[...] = cum
    cum_all[span] = cum
    last = cum[SPAN - 1 : SPAN, :]
    ending = jnp.where(flags[:, 4:5] > 0.5, jnp.exp(last - cum), 0.0)
    inner = act[:, :WIDE]
    write = act[:, WIDE : WIDE + NSTATE]
    added = exact_left(write, spread(ending * dt) * inner.astype(f32), 0, 0)
    held = state[...]
    held_ref[0] = held
    pref_ref[0] = decay[...]
    closing = jnp.where(flags[SPAN - 1 : SPAN, 3:4] > 0.5, jnp.exp(last), 0.0)
    fade = spread(jnp.broadcast_to(closing, (8, 128)))
    held = fade[0:1, :] * held + added
    state[...] = held
    decay[...] = decay[...] * fade
    end_ref[0:NSTATE, :] = held
    end_ref[NSTATE:, :] = decay[...]


def carry_chain(ends_ref, ahead_ref, out_ref, reverse):
    out_ref[...] = jnp.zeros_like(out_ref)
    groups = ends_ref.shape[0]

    @pl.loop(0, groups)
    def _(step):
        g = groups - 1 - step if reverse else step
        one = ends_ref[g]
        on = ahead_ref[g] > 0.5
        held = out_ref[...]
        out_ref[...] = jnp.where(on, one[NSTATE : NSTATE + 1, :] * held + one[0:NSTATE, :], held)


def within_phase(span, fl_ref, row_ref, skip_ref, y_ref, act_all, dt_all, cum_all):
    act = act_all[span]
    inner = act[:, :WIDE]
    cum = cum_all[span]
    cum_t = cum.T
    dt_t = dt_all[span].T
    scores = dot(act[:, WIDE + NSTATE :], act[:, WIDE : WIDE + NSTATE], 1, 1)
    matched = (fl_ref[:, 5:6] == row_ref[0]) & lower(SPAN)
    y = skip_ref[...] * inner.astype(f32)
    for h in range(HERE):
        fade = jnp.exp(jnp.minimum(cum[:, h : h + 1] - cum_t[h : h + 1, :], 0.0))
        mixing = jnp.where(matched, fade, 0.0) * scores * dt_t[h : h + 1, :]
        y = y + exact_right(mixing, head_mask(inner, h))
    y_ref[...] = y


def second_kernel(
    read_ref, cum_ref, fl_ref, held_ref, pref_ref, inc_ref, part_ref, gate_ref, cot_ref, wo_ref, og_ref,
    y_ref, gno_ref, sums_ref,
):
    entering = held_ref[0] + pref_ref[0][0:1, :] * inc_ref[...]
    rising = jnp.where(fl_ref[:, 3:4] > 0.5, jnp.exp(cum_ref[...]), 0.0)
    y_low = (part_ref[...] + spread(rising) * exact_left(read_ref[...], entering)).astype(bf16)
    y_ref[...] = y_low
    gated = y_low.astype(f32) * silu(gate_ref[...].astype(f32))
    gno = dot(cot_ref[...], wo_ref[...], 1, 1)
    gno_ref[...] = gno
    squares = jnp.sum(gated * gated, axis=1, keepdims=True)
    along = jnp.sum(gno * og_ref[...] * gated, axis=1, keepdims=True)
    lane = lax.broadcasted_iota(jnp.int32, (SPAN, 128), 1)
    both = jnp.where(lane == 0, squares, jnp.where(lane == 1, along, 0.0))
    sums_ref[0] = both.T[0:2, :]


def third_begin(gog_ref, gskip_ref, gout_ref, ggw_ref, state, decay):
    for ref in (gog_ref, gskip_ref, gout_ref, ggw_ref, state):
        ref[...] = jnp.zeros_like(ref)
    decay[...] = jnp.ones_like(decay)


def third_first(
    at, y_ref, gate_ref, gno_ref, sums_ref, act_ref, cum_ref, fl_ref, og_ref,
    gy_ref, gg_ref, behind_ref, suff_ref, start_ref, gog_ref, gskip_ref,
    state, decay, no_all, gg_all,
):
    span = no_all.shape[0] - 1 - at
    act = act_ref[...]
    inner = act[:, :WIDE].astype(f32)
    read = act[:, WIDE + NSTATE :]
    flags = fl_ref[...]
    totals = jnp.sum(sums_ref[...], axis=0)
    inv_row = lax.rsqrt(totals[0:1, :] / INNER + EPS_NORM)
    mean_row = inv_row * totals[1:2, :] / INNER
    cols = jnp.concatenate([inv_row, mean_row, jnp.zeros((6, SPAN), f32)], axis=0).T
    inv = cols[:, 0:1]
    mean = cols[:, 1:2]
    y = y_ref[...].astype(f32)
    gate = gate_ref[...].astype(f32)
    gate_act = silu(gate)
    unit = y * gate_act * inv
    gno = gno_ref[...]
    no_all[span] = (unit * og_ref[...]).astype(bf16)
    grad_gated = inv * (gno * og_ref[...] - unit * mean)
    gy = (grad_gated * gate_act).astype(bf16)
    gy_ref[...] = gy
    ggate = (grad_gated * y * silu_slope(gate)).astype(bf16)
    gg_ref[...] = ggate
    gg_all[span] = ggate
    gyf = gy.astype(f32)
    gog_ref[...] += jnp.sum(gno * unit, axis=0, keepdims=True)
    gskip_ref[...] += jnp.sum(inner * gyf, axis=0, keepdims=True)
    rising = jnp.where(flags[:, 3:4] > 0.5, jnp.exp(cum_ref[...]), 0.0)
    wide = spread(rising)
    pulled = exact_left(read, wide * gyf, 0, 0)
    held = state[...]
    behind_ref[0] = held
    suff_ref[0] = decay[...]
    fade = wide[SPAN - 1 : SPAN, :]
    held = fade * held + pulled
    state[...] = held
    decay[...] = decay[...] * fade
    start_ref[0:NSTATE, :] = held
    start_ref[NSTATE:, :] = decay[...]


def third_second(span, place, cot_ref, wo_ref, normed_ref, mix_ref, gout_ref, ggw_ref, no_all, gg_all):
    mix_ref[...] = dot(no_all[place], wo_ref[...])
    gout_ref[...] += dot(no_all[span], cot_ref[...], 0, 0)
    ggw_ref[...] += dot(gg_all[span], normed_ref[...], 0, 0)


def fourth_kernel(
    at, act_ref, dt_ref, cum_ref, fl_ref, row_ref, held_ref, pref_ref, inc_ref, behind_ref, suff_ref,
    ends_ref, ahead_ref, gy_ref, pre_ref, skip_ref, rate_ref,
    gpre_ref, gst_ref, gstep_ref, hsum_ref,
    out_ref,
):
    @pl.when(at == 0)
    def _():
        hsum_ref[...] = jnp.zeros_like(hsum_ref)
        carry_chain(ends_ref, ahead_ref, out_ref, True)

    act = act_ref[...]
    inner = act[:, :WIDE]
    innerf = inner.astype(f32)
    write = act[:, WIDE : WIDE + NSTATE]
    read = act[:, WIDE + NSTATE :]
    flags = fl_ref[...]
    cum = cum_ref[...]
    dt = dt_ref[...]
    gy = gy_ref[...]
    gyf = gy.astype(f32)
    cum_t = cum.T
    entering = held_ref[0] + pref_ref[0][0:1, :] * inc_ref[...]
    leaving = behind_ref[0] + suff_ref[0][0:1, :] * out_ref[...]
    last = cum[SPAN - 1 : SPAN, :]
    rising = jnp.where(flags[:, 3:4] > 0.5, jnp.exp(cum), 0.0)
    ending = jnp.where(flags[:, 4:5] > 0.5, jnp.exp(last - cum), 0.0)
    scores = dot(write, read, 1, 1)
    i = lax.broadcasted_iota(jnp.int32, (SPAN, SPAN), 0)
    j = lax.broadcasted_iota(jnp.int32, (SPAN, SPAN), 1)
    matched = (flags[:, 5:6] == row_ref[0]) & (i <= j)
    lane = lax.broadcasted_iota(jnp.int32, (SPAN, 128), 1)
    from_state = exact_left(write, leaving)
    grad_scaled = spread(ending) * from_state
    grad_scores = jnp.zeros((SPAN, SPAN), f32)
    rows_of = []
    cols_of = jnp.zeros((SPAN, 128), f32)
    for h in range(HERE):
        fade = jnp.exp(jnp.minimum(cum_t[h : h + 1, :] - cum[:, h : h + 1], 0.0))
        weights = jnp.where(matched, fade, 0.0)
        grad_scaled = grad_scaled + exact_right(weights * scores, head_mask(gy, h))
        part = dot(head_mask(inner, h), gy, 1, 1) * weights * dt[:, h : h + 1]
        grad_scores = grad_scores + part
        logs = part * scores
        rows_of.append(jnp.sum(logs, axis=0, keepdims=True))
        cols_of = cols_of + jnp.where(lane == h, jnp.sum(logs, axis=1, keepdims=True), 0.0)
    rows_of.append(jnp.zeros((128 - HERE, SPAN), f32))
    grad_cum = jnp.concatenate(rows_of, axis=0).T - cols_of
    high, low = split2(grad_scores)
    grad_write = dot(high, read) + dot(low, read)
    grad_read = dot(high, write, 0, 0) + dot(low, write, 0, 0)
    read_state = exact_left(read, entering)
    grad_read = grad_read + both_split(spread(rising) * gyf, entering, 1, 1)
    grad_write = grad_write + both_split(spread(ending * dt) * innerf, leaving, 1, 1)
    tail = head_sum(innerf * from_state) * dt * ending
    grad_cum = grad_cum + head_sum(gyf * read_state) * rising - tail
    crossing = jnp.sum(entering * leaving, axis=0, keepdims=True)
    crossing = head_sum(jnp.broadcast_to(crossing, (8, WIDE)))[0:1, :] * rising[SPAN - 1 : SPAN, :]
    end_term = jnp.sum(tail, axis=0, keepdims=True) + crossing
    row = lax.broadcasted_iota(jnp.int32, (SPAN, 128), 0)
    grad_cum = grad_cum + jnp.where(row == SPAN - 1, end_term, 0.0)
    grad_log = running((i <= j).astype(bf16), grad_cum)
    grad_steps = grad_log * rate_ref[...] + head_sum(innerf * grad_scaled)
    grad_step_raw = jnp.where(lane < HERE, grad_steps * pltpu.roll(dt, HEAD_DIM, 1), 0.0)
    gstep_ref[...] = grad_step_raw.T[0:8, :]
    grad_rate = jnp.where(lane < HERE, grad_log * dt, 0.0)
    hsum_ref[0:1, :] += jnp.sum(grad_step_raw, axis=0, keepdims=True)
    hsum_ref[1:2, :] += jnp.sum(grad_rate, axis=0, keepdims=True)
    grad_inner = spread(dt) * grad_scaled + skip_ref[...] * gyf
    slope = silu_slope(pre_ref[...])
    gpre_ref[...] = grad_inner * slope[:, :WIDE]
    gst_ref[...] = jnp.concatenate([grad_write, grad_read], axis=1) * slope[:, WIDE:]


def conv_back(gpre, flags, chan_ext, conv_ref, masked):
    rows = gpre.shape[0] - 8
    total = gpre[0:rows, :] * conv_ref[0:1, :]
    sums = [jnp.sum(gpre[0:rows, :] * chan_ext[8 : rows + 8, :], axis=0, keepdims=True)]
    for k in range(1, CONV):
        masked[...] = jnp.where(flags[:, k - 1 : k] > 0.5, gpre, 0.0)
        total = total + masked[k : rows + k, :] * conv_ref[k : k + 1, :]
        sums.append(jnp.sum(masked[0:rows, :] * chan_ext[8 - k : rows + 8 - k, :], axis=0, keepdims=True))
    sums.append(jnp.sum(gpre[0:rows, :], axis=0, keepdims=True))
    sums.append(jnp.zeros((3, gpre.shape[1]), f32))
    return total, jnp.concatenate(sums, axis=0)


def fifth_begin(gstate_ref, gog_ref, gskip_ref, hsum_ref, giw_ref, small_ref):
    giw_ref[...] = jnp.zeros_like(giw_ref)
    small_ref[...] = jnp.zeros_like(small_ref)
    small_ref[8:16, :] = gstate_ref[...]
    small_ref[16:17, :] = gog_ref[...]
    small_ref[17:18, :] = gskip_ref[...]
    small_ref[18:19, 0:128] = hsum_ref[0:1, :]
    small_ref[18:19, 128:256] = hsum_ref[1:2, :]


def fifth_product(gg_ref, ginner, wm_ref):
    return dot(gg_ref[...], wm_ref[:, :WIDE], 1, 1) + dot(ginner, wm_ref[:, WIDE:], 1, 1)


def fifth_kernel(
    span, spans, gpre_ref, after_ref, fl_ref, chan_ref, edge_ref, conv_ref, normed_ref,
    ginner_ref, giw_ref, small_ref,
    chan_ext, gext, masked,
):
    start = pl.multiple_of(span * SPAN, SPAN)

    @pl.when(span == 0)
    def _():
        chan_ext[0:8, :] = edge_ref[:, :WIDE]

    @pl.when(span > 0)
    def _():
        chan_ext[0:8, :] = chan_ref[pl.ds(pl.multiple_of(start - 16, 16), 16), :WIDE].astype(f32)[8:16, :]

    chan_ext[8 : SPAN + 8, :] = chan_ref[pl.ds(start, SPAN), :WIDE].astype(f32)
    gext[0:SPAN, :] = gpre_ref[pl.ds(start, SPAN), :]

    @pl.when(span < spans - 1)
    def _():
        gext[SPAN : SPAN + 8, :] = gpre_ref[pl.ds(pl.multiple_of(start + SPAN, SPAN), 8), :]

    @pl.when(span == spans - 1)
    def _():
        gext[SPAN : SPAN + 8, :] = after_ref[...]

    total, sums = conv_back(gext[...], fl_ref[pl.ds(start, SPAN + 8), :], chan_ext, conv_ref, masked)
    ginner = total.astype(bf16)
    small_ref[0:8, :] += sums
    ginner_ref[...] = ginner
    giw_ref[...] += dot(ginner, normed_ref[...], 0, 0)


def sixth_kernel(count, *refs):
    sixth_body(refs[:count], *refs[count:])


def sixth_body(
    parts, tails_ref, steps_ref, fl_ref, chan_ref, edge_ref, conv_ref, x_ref, ng_ref,
    gs_ref, gconv_ref, gw_ref,
    gext, chan_ext, masked,
):
    place = lax.axis_index("sub") * lax.axis_size("seq") + lax.axis_index("seq")
    start = pl.multiple_of(place * SPAN, SPAN)
    total = jnp.sum(parts[0][...].astype(f32), axis=0)
    for part in parts[1:]:
        total = total + part[...]
    gext[0:SPAN, :] = total
    gext[SPAN : SPAN + 8, :] = jnp.sum(tails_ref[...], axis=0)
    chan_ext[8 : SPAN + 8, :] = chan_ref[pl.ds(start, SPAN), WIDE:].astype(f32)

    @pl.when(place == 0)
    def _():
        chan_ext[0:8, :] = edge_ref[:, WIDE:]

    @pl.when(place > 0)
    def _():
        chan_ext[0:8, :] = chan_ref[pl.ds(pl.multiple_of(start - 16, 16), 16), WIDE:].astype(f32)[8:16, :]

    conv = conv_ref.at[:, WIDE:]
    total, sums = conv_back(gext[...], fl_ref[pl.ds(start, SPAN + 8), :], chan_ext, conv, masked)
    gconv_ref[...] = sums
    steps = jnp.concatenate([steps_ref[:, i, :] for i in range(HERE)] + [jnp.zeros((128 - HEADS, SPAN), f32)], axis=0)
    grads = jnp.concatenate([total, steps.T], axis=1).astype(bf16)
    gs_ref[...] = grads
    vals = x_ref[...].astype(f32)
    inv = lax.rsqrt(jnp.mean(vals * vals, axis=1, keepdims=True) + EPS_NORM)
    gw_ref[...] = dot((vals * inv * ng_ref[...]).astype(bf16), grads, 0, 0)


def seventh_kernel(skip, count, many, *refs):
    refs = refs[skip:]
    parts, mixes, rest = refs[:count], refs[count : count + many], refs[count + many :]
    gs_ref, ws_ref, x_ref, cot_ref, ng_ref, mixed_ref, gt_ref, gain_ref = rest

    def add_all(total, refs):
        halves = [ref[...] for ref in refs if ref.shape[0] == SPAN // 2]
        if halves:
            total = total + jnp.concatenate(halves, axis=0).astype(f32)
        for ref in refs:
            if ref.shape[0] == SPAN // 2:
                continue
            if len(ref.shape) == 2:
                total = total + ref[...].astype(f32)
            else:
                for i in range(ref.shape[0]):
                    total = total + ref[i].astype(f32)
        return total

    vals = x_ref[...].astype(f32)
    mixed_ref[...] = add_all(vals, mixes).astype(bf16)
    grad = add_all(dot(gs_ref[...], ws_ref[...], 1, 1), parts)
    inv = lax.rsqrt(jnp.mean(vals * vals, axis=1, keepdims=True) + EPS_NORM)
    unit = vals * inv
    s = grad * ng_ref[...]
    gt_ref[...] = cot_ref[...].astype(f32) + inv * (s - unit * jnp.mean(s * unit, axis=1, keepdims=True))
    row = jnp.sum(grad * unit, axis=0, keepdims=True)
    for i in range(D // 128):
        gain_ref[i : i + 1, :] = row[:, 128 * i : 128 * (i + 1)]


def adam_terms(weight, grad, first, second):
    first_new = BETA_ONE * first + (1.0 - BETA_ONE) * grad
    second_new = BETA_TWO * second + (1.0 - BETA_TWO) * grad * grad
    update = (
        first_new / (1.0 - BETA_ONE**STEP) / (jnp.sqrt(second_new / (1.0 - BETA_TWO**STEP)) + ADAM_EPS)
        + DECAY * weight
    )
    return (first_new, second_new, update)


def square_sum(x):
    return jnp.sum(jnp.sum(x * x, axis=1, keepdims=True), axis=0, keepdims=True)


def lamb_apply(weight, update, weight_sq, update_sq):
    return weight - RATE * (jnp.sqrt(weight_sq) / (jnp.sqrt(update_sq) + ADAM_EPS)) * update


def two_heads(ref, rows, i, pair):
    cols = slice(HEAD_DIM * i, HEAD_DIM * (i + 1))
    return jnp.concatenate([ref[2 * pair, rows, cols], ref[2 * pair + 1, rows, cols]], axis=1)


def from_planes(z, own, near, far):
    first = jnp.where(z > 0, near[0], far[0].astype(f32))
    third = jnp.where(z < 3, near[1], far[2].astype(f32))
    return own + first + far[1].astype(f32) + third


def adam_kernel(count, gate_ref, inner_ref, shared_ref, gain_ref, wi_ref, mi_ref, vi_ref, wo_ref, mo_ref, vo_ref, *refs):
    outs, (mi_out, vi_out, ui_out, mo_out, vo_out, uo_out, sums_ref, grad) = refs[:count], refs[count:]
    for base, ref in ((0, gate_ref), (INNER, inner_ref)):
        for i in range(HERE):
            for pair in range(PLANE // 2):
                at = base + i * PLANE * HEAD_DIM + pair * 128
                grad[:, at : at + 128] = two_heads(ref, slice(None), i, pair)
    grad[:, 2 * INNER :] = jnp.sum(shared_ref[...], axis=0)[:, : STATES + HEADS]
    weight = wi_ref[...]
    mi_out[...], vi_out[...], update = adam_terms(weight, grad[...], mi_ref[...], vi_ref[...])
    ui_out[...] = update
    sums_ref[0:8, :] = gain_ref[...]
    sums_ref[8:16, :] = jnp.zeros((8, 128), f32)
    sums_ref[8:9, :] = jnp.broadcast_to(square_sum(weight), (1, 128))
    sums_ref[9:10, :] = jnp.broadcast_to(square_sum(update), (1, 128))
    if count > 1:
        z = lax.axis_index("grp")
        total = from_planes(z, outs[0][pl.ds(pl.multiple_of(z * HEAD_DIM, HEAD_DIM), HEAD_DIM), :], *outs[1:])
    else:
        total = outs[0][...]
    weight = wo_ref[...]
    mo_out[...], vo_out[...], update = adam_terms(weight, total, mo_ref[...], vo_ref[...])
    uo_out[...] = update
    sums_ref[10:11, :] = jnp.broadcast_to(square_sum(weight), (1, 128))
    sums_ref[11:12, :] = jnp.broadcast_to(square_sum(update), (1, 128))


def last_kernel(
    every_ref, small_ref, wi_ref, ui_ref, wo_ref, uo_ref,
    nw_ref, nm_ref, nv_ref, cw_ref, cm_ref, cv_ref, hw_ref, hm_ref, hv_ref, gw_ref, gm_ref, gv_ref,
    wi_out, wo_out, nm_out, nv_out, nw_out, cm_out, cv_out, cw_out, hm_out, hv_out, hw_out, gm_out, gv_out, gw_out,
    conv, gain,
):
    total = jnp.sum(every_ref[...], axis=0)
    wi_out[...] = lamb_apply(wi_ref[...], ui_ref[...], total[8:9, 0:1], total[9:10, 0:1])
    wo_out[...] = lamb_apply(wo_ref[...], uo_ref[...], total[10:11, 0:1], total[11:12, 0:1])

    def update(grad, weight_ref, first_ref, second_ref, first_out, second_out, weight_out):
        weight = weight_ref[...]
        first, second, step = adam_terms(weight, grad, first_ref[...], second_ref[...])
        first_out[...] = first
        second_out[...] = second
        weight_out[...] = lamb_apply(weight, step, square_sum(weight), square_sum(step))

    update(total[0:8], nw_ref, nm_ref, nv_ref, nm_out, nv_out, nw_out)
    for i in range(HERE):
        for pair in range(PLANE // 2):
            at = i * PLANE * HEAD_DIM + pair * 128
            conv[:, at : at + 128] = two_heads(small_ref, slice(0, 8), i, pair)
            gain[at // 128 : at // 128 + 1, :] = two_heads(small_ref, slice(16, 17), i, pair)
    conv[:, INNER:] = jnp.sum(small_ref[:, 8:16, :], axis=0)
    update(conv[0:5, :], cw_ref, cm_ref, cv_ref, cm_out, cv_out, cw_out)
    update(gain[...], gw_ref, gm_ref, gv_ref, gm_out, gv_out, gw_out)

    t = lax.broadcasted_iota(jnp.int32, (PLANE, 128), 0)
    lane = lax.broadcasted_iota(jnp.int32, (PLANE, 128), 1)

    def by_head(cols):
        row = jnp.zeros((PLANE, 128), f32)
        for i in range(HERE):
            row = row + jnp.where(lane == PLANE * i + t, cols[:, i : i + 1], 0.0)
        return jnp.sum(row, axis=0, keepdims=True)[:, :HEADS]

    steps = by_head(small_ref[:, 18, 0:128])
    rates = by_head(small_ref[:, 18, 128:256]) * -jnp.exp(hw_ref[1:2, :])
    skips = by_head(head_sum(small_ref[:, 17, :]))
    update(jnp.concatenate([steps, rates, skips], axis=0), hw_ref, hm_ref, hv_ref, hm_out, hv_out, hw_out)


def spec(block, index):
    return pl.BlockSpec(block, index)


def whole(*dims):
    return pl.BlockSpec(dims, lambda *_: (0,) * len(dims))


def shape(*dims, dtype=f32):
    return jax.ShapeDtypeStruct(dims, dtype)


ANY = pl.BlockSpec(memory_space=pl.ANY)
IN_VMEM = pl.BlockSpec(memory_space=pltpu.VMEM)
IN_HBM = pl.BlockSpec(memory_space=pltpu.HBM)
MIB = 1024 * 1024
VMEM_LIMIT = 60 * MIB
SMALL_LIMIT = 13 * MIB


def launch(kernel, name, steps, in_specs, ins, out_specs, outs, scratch=()):
    grid = {"grid": (steps,), "in_specs": list(in_specs), "out_specs": list(out_specs)} if steps else {}
    return pl.pallas_call(
        kernel,
        out_shape=list(outs),
        scratch_shapes=list(scratch),
        compiler_params=pltpu.CompilerParams(vmem_limit_bytes=VMEM_LIMIT),
        name=name,
        **grid,
    )(*ins)


class First:
    def __init__(self, spans, x, halo, gain, wm, ws, pick, conv, bias, rate, flags, doc_rows, skip, ahead):
        rows = spans * SPAN
        early = lambda s: jnp.minimum(s, spans - 1)
        late = lambda s: jnp.maximum(s - spans, 0)
        both = lambda s: jnp.where(s >= spans, s - spans, s)
        block = lambda cols, at=early: spec((SPAN, cols), lambda s: (at(s), 0))
        span3 = lambda a, b, at=early: spec((1, a, b), lambda s: (at(s), 0, 0))
        self.ins = [x, halo, gain, wm, ws, pick, conv, bias, rate, flags, doc_rows, skip, ahead]
        self.in_specs = [
            block(D), whole(16, D), whole(1, D), whole(D, MAIN), whole(D, SHARED), whole(128, 128), whole(8, LOCAL),
            whole(1, 128), whole(1, 128), block(8, both), span3(1, SPAN, late), whole(1, WIDE), whole(*ahead.shape),
        ]
        self.out_specs = [
            block(D), block(WIDE), block(LOCAL), block(LOCAL), block(LOCAL), block(128), block(128),
            span3(NSTATE, WIDE), span3(8, WIDE), whole(8, LOCAL), block(WIDE, late),
        ]
        self.outs = [
            shape(rows, D, dtype=bf16), shape(rows, WIDE, dtype=bf16), shape(rows, LOCAL, dtype=bf16), shape(rows, LOCAL),
            shape(rows, LOCAL, dtype=bf16), shape(rows, 128), shape(rows, 128),
            shape(spans, NSTATE, WIDE), shape(spans, 8, WIDE), shape(8, LOCAL), shape(rows, WIDE),
        ]
        self.scratch = [
            pltpu.VMEM((SPAN + 8, LOCAL), f32), pltpu.VMEM((NSTATE, WIDE), f32), pltpu.VMEM((8, WIDE), f32),
            pltpu.VMEM((PACK, WIDE), f32), pltpu.VMEM((spans, SPAN, LOCAL), bf16), pltpu.VMEM((spans, SPAN, 128), f32),
            pltpu.VMEM((spans, SPAN, 128), f32),
        ]


def first_steps(step, spans, ins, outs, scratch):
    @pl.when(step == 0)
    def _():
        first_begin(*ins[1:5], outs[9], *scratch[:3])

    @pl.when(step < spans)
    def _():
        first_phase(step, *ins[:10], *outs[:10], *scratch)

    @pl.when(step >= spans)
    def _():
        within_phase(step - spans, *ins[9:12], outs[10], *scratch[4:])


def first_plain(spans, *refs):
    ins, outs, end, scratch = refs[:13], refs[13:24], refs[24], refs[25:]
    step = pl.program_id(0)
    first_steps(step, spans, ins, outs, scratch)

    @pl.when(step == spans - 1)
    def _():
        end[...] = scratch[3][...]


class Second:
    def __init__(self, spans, act, cum, flags, held, pref, incoming, part, gate, cot, wo, gain):
        rows = spans * SPAN
        block = lambda cols: spec((SPAN, cols), lambda s: (s, 0))
        span3 = lambda a, b: spec((1, a, b), lambda s: (s, 0, 0))
        self.ins = [act, cum, flags, held, pref, incoming, part, gate, cot, wo, gain]
        self.in_specs = [
            spec((SPAN, NSTATE), lambda s: (s, (WIDE + NSTATE) // NSTATE)), block(128), block(8), span3(NSTATE, WIDE),
            span3(8, WIDE), whole(NSTATE, WIDE), block(WIDE), block(WIDE), block(D), whole(WIDE, D), whole(1, WIDE),
        ]
        self.out_specs = [block(WIDE), block(WIDE)]
        self.outs = [shape(rows, WIDE, dtype=bf16), shape(rows, WIDE)]
        self.scratch = []


class Third:
    def __init__(self, spans, y, gate, gno, sums, act, cum, flags, gain, cot, wo, normed):
        rows = spans * SPAN
        back = lambda s: jnp.maximum(spans - 1 - s, 0)
        after = lambda s: jnp.maximum(s - spans, 0)
        block = lambda cols: spec((SPAN, cols), lambda s: (back(s), 0))
        later = lambda cols: spec((SPAN, cols), lambda s: (after(s), 0))
        span3 = lambda a, b: spec((1, a, b), lambda s: (back(s), 0, 0))
        self.later = later
        self.ins = [y, gate, gno, sums, act, cum, flags, gain, cot, wo, normed]
        self.in_specs = [
            block(WIDE), block(WIDE), block(WIDE), spec((PLANE, pl.squeezed, 2, SPAN), lambda s: (0, back(s), 0, 0)),
            block(LOCAL), block(128), block(8), whole(1, WIDE), later(D), whole(WIDE, D), later(D),
        ]
        self.out_specs = [block(WIDE), block(WIDE), span3(NSTATE, WIDE), span3(8, WIDE), whole(1, WIDE), whole(1, WIDE),
                          whole(WIDE, D), whole(WIDE, D)]
        self.outs = [
            shape(rows, WIDE, dtype=bf16), shape(rows, WIDE, dtype=bf16), shape(spans, NSTATE, WIDE),
            shape(spans, 8, WIDE), shape(1, WIDE), shape(1, WIDE), shape(WIDE, D), shape(WIDE, D),
        ]
        keep = pltpu.VMEM((spans, SPAN, WIDE), bf16)
        self.scratch = [pltpu.VMEM((NSTATE, WIDE), f32), pltpu.VMEM((8, WIDE), f32), keep, keep]


def third_plain(spans, *refs):
    ins, (gy, gg, behind, suff, gog, gskip, gout, ggw, start, mix), scratch = refs[:11], refs[11:21], refs[21:]
    step = pl.program_id(0)

    @pl.when(step == 0)
    def _():
        third_begin(gog, gskip, gout, ggw, *scratch[:2])

    @pl.when(step < spans)
    def _():
        third_first(step, *ins[:8], gy, gg, behind, suff, start, gog, gskip, *scratch)

    @pl.when(step >= spans)
    def _():
        third_second(step - spans, step - spans, *ins[8:], mix, gout, ggw, *scratch[2:])


class Fourth:
    def __init__(
        self, spans, act, dt, cum, flags, doc_rows, held, pref, incoming, behind, suff, ends, after_us, gy, pre,
        skip, rate,
    ):
        rows = spans * SPAN
        groups = ends.shape[0]
        block = lambda cols: spec((SPAN, cols), lambda s: (s, 0))
        span3 = lambda a, b: spec((1, a, b), lambda s: (s, 0, 0))
        self.ins = [act, dt, cum, flags, doc_rows, held, pref, incoming, behind, suff, ends, after_us, gy, pre, skip, rate]
        self.in_specs = [
            block(LOCAL), block(128), block(128), block(8), span3(1, SPAN), span3(NSTATE, WIDE),
            span3(8, WIDE), whole(NSTATE, WIDE), span3(NSTATE, WIDE), span3(8, WIDE), whole(groups, PACK, WIDE),
            whole(groups, 1, WIDE), block(WIDE), block(LOCAL), whole(1, WIDE), whole(1, 128),
        ]
        self.out_specs = [block(WIDE), whole(8, 128)]
        self.outs = [shape(rows, WIDE), shape(8, 128)]
        self.scratch = [pltpu.VMEM((NSTATE, WIDE), f32)]


def fourth_plain(*refs):
    ins, (gpre, hsum, gst, gstep), scratch = refs[:16], refs[16:20], refs[20:]
    fourth_kernel(pl.program_id(0), *ins, gpre, gst, gstep, hsum, *scratch)


class Fifth:
    def __init__(self, spans, gpre, after, flags, chan, edge, conv, normed, gstate, gog, gskip, hsum, ggate, wm):
        rows = spans * SPAN
        block = lambda cols: spec((SPAN, cols), lambda s: (s, 0))
        self.ins = [gpre, after, flags, chan, edge, conv, normed, gstate, gog, gskip, hsum, ggate, wm]
        self.in_specs = [
            whole(rows, WIDE), whole(8, WIDE), whole(rows + 8, 8), whole(rows, LOCAL), whole(8, LOCAL), whole(8, WIDE),
            block(D), whole(8, STATES), whole(1, WIDE), whole(1, WIDE), whole(8, 128), block(WIDE), whole(D, MAIN),
        ]
        self.outs = []
        self.scratch = [pltpu.VMEM((SPAN + 8, WIDE), f32)] * 3


def fifth_plain(spans, *refs):
    step = pl.program_id(0)
    ins, (gp, giw, small), (*scratch, ginner) = refs[:13], refs[13:16], refs[16:]

    @pl.when(step == 0)
    def _():
        fifth_begin(*ins[7:11], giw, small)

    fifth_kernel(step, spans, *ins[:7], ginner, giw, small, *scratch)
    gp[...] = fifth_product(ins[11], ginner[...], ins[12])


def run_sixth(parts, tails, steps, flags, chan, edge, conv, x, gain):
    ins = [*parts, tails, steps, flags, chan, edge, conv, x, gain]
    return pl.pallas_call(
        functools.partial(sixth_kernel, len(parts)),
        in_specs=[IN_VMEM] * len(ins),
        out_shape=[shape(SPAN, SHARED, dtype=bf16), shape(8, STATES), shape(D, SHARED)],
        scratch_shapes=[pltpu.VMEM((SPAN + 8, STATES), f32)] * 3,
        compiler_params=pltpu.CompilerParams(vmem_limit_bytes=SMALL_LIMIT),
        name="conv_back_state",
    )(*ins)


def run_seventh(parts, mixes, gs, ws, x, cot, gain, spare):
    ins = [*spare, *parts, *mixes, gs, ws, x, cot, gain]
    return pl.pallas_call(
        functools.partial(seventh_kernel, len(spare), len(parts), len(mixes)),
        in_specs=[IN_VMEM] * len(ins),
        out_shape=[shape(SPAN, D, dtype=bf16), shape(SPAN, D), shape(D // 128, 128)],
        compiler_params=pltpu.CompilerParams(vmem_limit_bytes=SMALL_LIMIT),
        name="token_gradient",
    )(*ins)


def run_adam(gate, inner, shared, gain, wi, mi, vi, wo, mo, vo, grads_out):
    like = lambda a: shape(*a.shape)
    ins = [gate, inner, shared, gain, wi, mi, vi, wo, mo, vo, *grads_out]
    return pl.pallas_call(
        functools.partial(adam_kernel, len(grads_out)),
        in_specs=[IN_VMEM] * len(ins),
        out_shape=[like(wi), like(wi), like(wi), like(wo), like(wo), like(wo), shape(16, 128)],
        scratch_shapes=[pltpu.VMEM(wi.shape, f32)],
        compiler_params=pltpu.CompilerParams(vmem_limit_bytes=SMALL_LIMIT),
        name="adam_terms",
    )(*ins)


def run_prep(groups, at, conv, head, gain):
    return pl.pallas_call(
        prep_kernel,
        in_specs=[pl.BlockSpec(memory_space=pltpu.SMEM)] + [pl.BlockSpec(memory_space=pltpu.VMEM)] * 3,
        out_shape=[shape(8, LOCAL), shape(1, 128), shape(1, 128), shape(1, WIDE), shape(1, WIDE),
                   shape(128, 128, dtype=bf16), shape(groups, 1, WIDE), shape(groups, 1, WIDE)],
        compiler_params=pltpu.CompilerParams(vmem_limit_bytes=VMEM_LIMIT),
        name="prepare",
    )(at, conv, head, gain)


def run_last(every, small, big, params):
    like = lambda a: shape(*a.shape)
    outs = [like(big[0]), like(big[2])]
    for weight in params[::3]:
        outs += [like(weight)] * 3
    return pl.pallas_call(
        last_kernel,
        out_shape=outs,
        scratch_shapes=[pltpu.VMEM((8, INNER + STATES), f32), pltpu.VMEM((INNER // 128, 128), f32)],
        compiler_params=pltpu.CompilerParams(vmem_limit_bytes=SMALL_LIMIT),
        name="lamb_apply",
    )(every, small, *big, *params)


MESH = pl.DeviceIdType.MESH


def bits(place):
    x = jnp.where(place >= 4, 1, 0)
    rest = place - 4 * x
    c = jnp.where(rest >= 2, 1, 0)
    return x, c, rest - 2 * c


class Here:
    def __init__(self):
        self.z = lax.axis_index("grp")
        self.sub = lax.axis_index("sub")
        self.y = lax.axis_index("seq")
        self.x = jnp.where(self.sub >= 2, 1, 0)
        self.c = self.sub - 2 * self.x
        self.t = self.sub * 2 + self.y

    def mate(self, o, up=0):
        x = 1 - self.x if o & 4 else self.x
        c = 1 - self.c if o & 2 else self.c
        y = 1 - self.y if o & 1 else self.y
        sub = x * 2 + c
        return (self.onward(up), sub, y), sub * 2 + y

    def onward(self, up):
        z = self.z + up
        return jnp.where(z >= 4, z - 4, z) if up else self.z

    def plane(self, up):
        return (self.onward(up), self.sub, self.y), self.onward(up)


CHIPS = (5, 4, 1)
CORE = 2


def near(h):
    return [h.mate(o)[0] for o in range(1, 8)]


def same_core(h):
    return [h.mate(o)[0] for o in CHIPS]


def line(h):
    return [h.plane(up)[0] for up in range(1, 4)]


def call(devices):
    barrier = pltpu.get_barrier_semaphore()
    for device in devices:
        pl.semaphore_signal(barrier, inc=1, device_id=device, device_id_type=MESH)
    return barrier


def greet(devices):
    pl.semaphore_wait(call(devices), len(devices))


def rows_at(ref, at, size):
    return ref.at[pl.ds(pl.multiple_of(at * size, size), size)]


class Wires:
    def __init__(self, send, recv, local, started=False):
        self.send_sem, self.recv_sem, self.local_sem = send, recv, local
        self.sent, self.kept, self.started = [], [], started

    def make(self, src, dst, i, device, j=None):
        return pltpu.make_async_remote_copy(
            src_ref=src, dst_ref=dst, send_sem=self.send_sem.at[i], recv_sem=self.recv_sem.at[i if j is None else j],
            device_id=device, device_id_type=MESH,
        )

    def send(self, src, dst, i, device):
        copy = self.make(src, dst, i, device)
        if not self.started:
            copy.start()
        self.sent.append(copy)

    def arrived(self, dst, i, device):
        self.make(dst, dst, i, device).wait_recv()

    def keep(self, src, dst):
        copy = pltpu.make_async_copy(src, dst, self.local_sem.at[len(self.kept)])
        if not self.started:
            copy.start()
        self.kept.append(copy)
        return copy

    def finish(self):
        for copy in self.sent:
            copy.wait_send()


def wires(copies, kept):
    return [pltpu.SemaphoreType.DMA((copies,)), pltpu.SemaphoreType.DMA((copies,)), pltpu.SemaphoreType.DMA((kept,))]


def talk(kernel, number, name, outs, ins, scratch):
    return pl.pallas_call(
        kernel,
        in_specs=[IN_VMEM] * len(ins),
        out_specs=[IN_VMEM] * len(outs),
        out_shape=outs,
        scratch_shapes=scratch,
        compiler_params=pltpu.CompilerParams(collective_id=number, has_side_effects=True, vmem_limit_bytes=SMALL_LIMIT),
        name=name,
    )(*ins)


class Relay:
    def __init__(self, h, w, base, block):
        self.h, self.w, self.base, self.block = h, w, base, block

    def copies(self, hop):
        h = self.h
        above, below = h.plane(1)[0], h.plane(3)[0]
        up = self.w.make, jnp.maximum(h.z - hop + 1, 0), self.base + hop, above
        down = self.w.make, jnp.minimum(h.z + hop - 1, 3), self.base + 4 + hop, below
        yield (h.z < 3) & (h.z >= hop - 1), up, h.z >= hop, jnp.maximum(h.z - hop, 0), below
        yield (h.z > 0) & (h.z <= 4 - hop), down, h.z <= 3 - hop, jnp.minimum(h.z + hop, 3), above

    def first(self):
        for sends, (make, z, i, device), *_ in self.copies(1):

            @pl.when(sends)
            def _():
                make(self.block(z), self.block(z), i, device).start()

    def onward(self, hop):
        for _, (_, _, i, _), comes, z, device in self.copies(hop):

            @pl.when(comes)
            def _():
                self.w.arrived(self.block(z), i, device)

        if hop < 3:
            for sends, (make, z, i, device), *_ in self.copies(hop + 1):

                @pl.when(sends)
                def _():
                    make(self.block(z), self.block(z), i, device).start()

    def finish(self):
        for hop in range(1, 4):
            for sends, (make, z, i, device), *_ in self.copies(hop):

                @pl.when(sends)
                def _():
                    make(self.block(z), self.block(z), i, device).wait_send()


def start_kernel(wi_in, wo_in, tok, docs_in, conv_in, head_in, gain_in, norm_in, *refs):
    (wm, ws, x, halo), outputs, (flags, doc_rows, out_low, norm), refs = refs[:4], refs[4:12], refs[12:16], refs[16:]
    (wi, wo, docs, conv, head, gain, main, shared), sems = refs[:8], refs[8:]
    h = Here()
    w = Wires(*sems)
    near_x, near_y, mate = [h.mate(o)[0] for o in (4, 1, CORE)]
    friends = near(h) + line(h)
    barrier = call(friends)
    loads = [w.keep(wi_in, wi), w.keep(wo_in, wo)]
    loads += [w.keep(*pair) for pair in ((docs_in, docs), (conv_in, conv), (head_in, head), (gain_in, gain), (norm_in, norm))]
    own = w.keep(tok, rows_at(x, h.t, SPAN))
    loads[0].wait()
    loads[1].wait()
    pack_kernel(wi, wo, main, shared, out_low)
    pl.semaphore_wait(barrier, len(friends))

    in_rows = lambda place: wm.at[pl.ds(pl.multiple_of(h.z * SPAN + place * 32, 32), 32)]
    keep = [w.keep(main.at[h.t], in_rows(h.t)), w.keep(shared, ws.at[h.z, h.t])]
    for o in range(1, 8):
        device, place = h.mate(o)
        w.send(main.at[place], in_rows(h.t), o, device)
    for up in range(1, 4):
        w.send(shared, ws.at[h.z, h.t], 10 + up, h.plane(up)[0])
    block = lambda o: rows_at(x, h.mate(o)[1], SPAN)
    w.send(tok, block(0), 21, near_x)
    w.send(tok, block(0), 22, near_y)
    w.send(tok, block(0), 23, mate)
    for copy in loads[2:]:
        copy.wait()
    prepare(h.z, h.t, conv, head, gain, *outputs)
    flags_of(h.z, docs, flags, doc_rows)
    keep[0].wait()
    for o in range(1, 8):
        device, place = h.mate(o)
        w.arrived(in_rows(place), o, device)
    relay = Relay(h, w, 30, lambda z: rows_at(wm, z, SPAN))
    relay.first()
    keep[1].wait()
    for up in range(1, 4):
        device, z = h.plane(4 - up)
        w.arrived(ws.at[z, h.t], 10 + up, device)
    for i, o in enumerate(CHIPS):
        w.send(ws.at[:, h.t], ws.at[:, h.t], 40 + i, h.mate(o)[0])
    w.send(ws.at[:, h.t], ws.at[:, h.t], 43, mate)
    half = SPAN // 2
    upper, lower = pl.ds(0, half), pl.ds(half, half)
    relay.onward(1)
    w.arrived(block(4), 21, near_x)
    w.send(block(4).at[upper], block(4).at[upper], 20, near_y)
    w.send(block(4), block(4), 25, mate)
    w.arrived(block(1), 22, near_y)
    w.send(block(1).at[lower], block(1).at[lower], 27, near_x)
    w.send(block(1), block(1), 26, mate)
    for i, o in enumerate(CHIPS):
        device, place = h.mate(o)
        w.arrived(ws.at[:, place], 40 + i, device)
        w.send(ws.at[:, place], ws.at[:, place], 44 + i, mate)
    relay.onward(2)
    w.arrived(block(5).at[upper], 20, near_y)
    w.arrived(block(5).at[lower], 27, near_x)
    w.send(block(5), block(5), 24, mate)
    own.wait()
    w.arrived(block(CORE), 23, mate)
    w.arrived(ws.at[:, h.mate(CORE)[1]], 43, mate)
    for i, o in enumerate(CHIPS):
        w.arrived(block(o ^ CORE), 24 + i, mate)
    w.send(x.at[pl.ds(PLANE * SPAN - 16, 16)], halo, 50, h.plane(1)[0])
    for i, o in enumerate(CHIPS):
        w.arrived(ws.at[:, h.mate(o ^ CORE)[1]], 44 + i, mate)
    relay.onward(3)
    relay.finish()
    w.arrived(halo, 50, h.plane(3)[0])
    w.finish()


class Chain:
    def __init__(self, h, w, ends, low, lows, reverse):
        self.h, self.w, self.ends, self.low, self.lows = h, w, ends, low, lows
        self.hops = []
        for up in range(1, 4):
            ahead = 4 - up if reverse else up
            goes = h.z >= up if reverse else h.z < 4 - up
            comes = h.z < 4 - up if reverse else h.z >= up
            self.hops.append((up, goes, h.plane(ahead)[0], comes, *h.plane(4 - ahead)))

    def copy(self, up, device):
        z = self.h.z
        if up == 1:
            return self.w.make(self.ends.at[z], self.ends.at[z], up, device)
        return self.w.make(self.low, self.lows.at[z], up, device)

    def start(self):
        self.low[...] = self.ends[self.h.z].astype(bf16)
        for up, goes, device, *_ in self.hops:

            @pl.when(goes)
            def _():
                self.copy(up, device).start()

    def wait(self):
        for up, goes, device, comes, back, z in self.hops:

            @pl.when(comes)
            def _():
                self.w.arrived((self.lows if up > 1 else self.ends).at[z], up, back)
                if up > 1:
                    self.ends[z] = self.lows[z].astype(f32)

            @pl.when(goes)
            def _():
                self.copy(up, device).wait_send()


def first_direct(work, *refs):
    ins, (out, cot), refs = refs[:13], refs[13:15], refs[15:]
    outs, (inc, g, wo), refs = refs[:11], refs[11:14], refs[14:]
    (ext, state, decay, ends, low, lows), sems = refs[:6], refs[6:]
    h = Here()
    w = Wires(*sems)
    local = sems[2]
    mate, _ = h.mate(CORE)
    end = ends.at[h.z]
    spans = PLANE
    rows_of = [Rows(outs[i]) for i in (4, 5, 6)]

    greet(line(h) + same_core(h) + [mate])
    rows = [w.make(out, rows_at(wo, h.z, HEAD_DIM), 8 + up, h.plane(up)[0]) for up in range(1, 4)]
    block = lambda o: rows_at(g, h.mate(o)[1], SPAN)
    across = [w.make(cot, block(0), 4 + i, h.mate(o)[0]) for i, o in enumerate(CHIPS)]
    for copy in (*rows, *across):
        copy.start()
    loads = [pltpu.make_async_copy(cot, block(0), local.at[0]),
             pltpu.make_async_copy(out, rows_at(wo, h.z, HEAD_DIM), local.at[1])]
    for copy in loads:
        copy.start()
    first_begin(*ins[1:5], outs[9], ext, state, decay)

    @pl.loop(0, spans, unroll=2)
    def _(step):
        taken = views(work.in_specs[:10], ins, step)
        given = views(work.out_specs[:10], outs, step)
        first_phase(step, *taken, *given, ext, state, decay, end, *rows_of)

    chain = Chain(h, w, ends, low, lows, False)
    chain.start()
    over = [w.make(block(o), block(o), 12 + i, mate) for i, o in enumerate((*CHIPS, 0))]

    def within(span):
        taken = views(work.in_specs[9:12], ins[9:12], span + spans)
        within_phase(span, *taken, view(work.out_specs[10], outs[10], span + spans), *rows_of)

    pl.loop(0, spans // 2, unroll=2)(within)
    loads[0].wait()
    over[3].start()
    for i, o in enumerate(CHIPS):
        across[i].wait_send()
        w.arrived(block(o), 4 + i, h.mate(o)[0])
        over[i].start()
    pl.loop(spans // 2, spans, unroll=2)(within)
    for i, o in enumerate((*CHIPS, 0)):
        over[i].wait_send()
        w.arrived(block(o ^ CORE), 12 + i, mate)
    for up in range(1, 4):
        rows[up - 1].wait_send()
        w.arrived(rows_at(wo, h.onward(4 - up), HEAD_DIM), 8 + up, h.plane(4 - up)[0])
    loads[1].wait()
    chain.wait()
    carry_chain(ends, ins[12], inc, False)


def turn(step):
    h = Here()
    a, b, e = bits(7 - step)
    x, c, y = h.x + a - 2 * h.x * a, h.c + e - 2 * h.c * e, h.y + b - 2 * h.y * b
    return x * 4 + c * 2 + y


class Fold:
    def __init__(self, h, w, base, blocks, inbox, outbox, total, deliver):
        self.h, self.w, self.base, self.deliver = h, w, base, deliver
        self.blocks, self.inbox, self.outbox, self.total = blocks, inbox, outbox, total
        self.mate, _ = h.mate(CORE)
        self.slots = blocks.shape[0]

    def sent(self, i):
        self.w.make(self.inbox.at[i], self.inbox.at[i], self.base + i, self.mate).wait_send()

    def slot(self, step):
        for i in (2, 3):

            @pl.when(step == 2 * i)
            def _():
                self.sent(i - 2)

        return jnp.where(step >= 4, step - 4, step) if self.slots == 4 else step

    def add(self, pair, put):
        @pl.loop(0, SPAN, step=32)
        def _(row):
            rows = pl.ds(pl.multiple_of(row, 32), 32)
            put(rows, self.blocks[(2 * pair + 1) % self.slots, rows, :] + self.inbox[pair, rows, :])

    def settle(self, i):
        self.w.arrived(self.inbox.at[i], self.base + i, self.mate)
        self.add(i, put_in(self.outbox, i))
        self.deliver(i)

    def step(self, step, early=0):
        for i in range(4):

            @pl.when(step == 2 * i)
            def _():
                self.w.make(self.blocks.at[2 * i % self.slots], self.inbox.at[i], self.base + i, self.mate).start()
                if i > early:
                    self.settle(i - 1)

    def last(self):
        self.w.arrived(self.inbox.at[3], self.base + 3, self.mate)
        self.add(3, put_in(self.total))
        self.sent(2)
        self.sent(3)


class ToChips:
    def __init__(self, h, w, base, outbox, results):
        self.copies = [w.make(outbox.at[i], results.at[i], base + i, h.mate(o)[0]) for i, o in enumerate(CHIPS)]

    def __call__(self, i):
        self.copies[i].start()

    def last(self):
        for copy in self.copies:
            copy.wait()


def head_rows(ref, z):
    return rows_at(ref, z, HEAD_DIM)


def lanes_at(ref, z):
    return ref.at[:, pl.ds(pl.multiple_of(z * SPAN, SPAN), SPAN)]


class Planes:
    def __init__(self, h, w, base, full, low, piece, near, far):
        self.copies = []
        for up in range(1, 4):
            device, z = h.plane(up)
            wide = functools.partial(w.make, piece(full, z), near.at[up // 2], base + up, device)
            slim = functools.partial(w.make, piece(low, z), far.at[up - 1], base + up, device)
            to_near = {1: h.z < 3, 2: None, 3: h.z > 0}[up]
            from_near = {1: h.z > 0, 2: None, 3: h.z < 3}[up]
            self.copies.append((wide, slim, to_near, from_near))

    def each(self, near, act_wide, act_slim):
        if near is None:
            act_slim()
            return

        @pl.when(near)
        def _():
            act_wide()

        @pl.when(jnp.logical_not(near))
        def _():
            act_slim()

    def start(self):
        for wide, slim, to_near, _ in self.copies:
            self.each(to_near, lambda: wide().start(), lambda: slim().start())

    def wait(self):
        for wide, slim, to_near, from_near in self.copies:
            self.each(to_near, lambda: wide().wait_send(), lambda: slim().wait_send())
            self.each(from_near, lambda: wide().wait_recv(), lambda: slim().wait_recv())


def put_in(ref, *at):
    def put(rows, value):
        ref[(*at, rows, slice(None))] = value.astype(ref.dtype)

    return put


def third_direct(work, *refs):
    second, third = work.second, work
    ins, normed, refs = refs[:11], refs[11], refs[12:]
    (gy, gg, behind, suff, gog, gskip, gout, ggw), (gout_low, ggw_low, ends, chip, held, far) = refs[:8], refs[8:14]
    (blocks, inbox, state, decay, no_all, every, low, lows), sems = refs[14:22], refs[22:]
    act, cum, flags, _, _, _, _, gate, cot, wo, gain = ins
    h = Here()
    w = Wires(*sems)
    spans = PLANE
    across, _ = h.mate(CHIPS[0])
    start = ends.at[h.z]
    gates = Rows(gg)

    def gno(span):
        late = jnp.where(span >= 4, 1, 0)
        return blocks.at[span - 4 * late, :, pl.ds(pl.multiple_of(late * WIDE, WIDE), WIDE)]

    greet(near(h) + line(h))
    mine = every.at[h.t]
    third_begin(gog, gskip, gout, ggw, state, decay)

    @pl.loop(0, spans, unroll=2)
    def _(step):
        taken = views(second.in_specs, ins, step)
        second_kernel(*taken, view(second.out_specs[0], gy, step), gno(step), mine.at[pl.ds(step, 1)])

    for o in range(1, 8):
        w.send(mine, every.at[h.t], 10 + o, h.mate(o)[0])
    for o in range(1, 8):
        device, place = h.mate(o)
        w.arrived(every.at[place], 10 + o, device)

    taking = (gy, gate, None, every, act, cum, flags, gain, cot, wo, normed)

    @pl.loop(0, spans, unroll=2)
    def _(step):
        taken = [gno(spans - 1 - step) if i == 2 else view(third.in_specs[i], taking[i], step) for i in range(8)]
        one, two, three, four = views(third.out_specs[:4], (gy, gg, behind, suff), step)
        third_first(step, *taken, one, two, three, four, start, gog, gskip, state, decay, no_all, gates)

    chain = Chain(h, w, ends, low, lows, True)
    chain.start()
    cross = w.make(held.at[0, 0 : SPAN // 2], far, 8, across)
    fold = Fold(h, w, 4, blocks, inbox, held, chip, lambda i: None if i else cross.start())

    @pl.loop(0, spans)
    def _(span):
        taken = views(third.in_specs[8:], taking[8:], span + spans)
        third_second(span, turn(span), *taken, blocks.at[fold.slot(span)], gout, ggw, no_all, gates)
        fold.step(span)

    gout_low[...] = gout[...].astype(bf16)
    ggw_low[...] = ggw[...].astype(bf16)
    fold.last()
    cross.wait()
    chain.wait()
    w.finish()


def fourth_direct(work, *refs):
    ins, (held, ggw, ggw_low), refs = refs[:16], refs[16:19], refs[19:]
    (gpre, hsum), (rmix, far, near_gate, far_gate) = refs[:2], refs[2:6]
    (parts, total, tails, steps, after), refs = refs[6:11], refs[11:]
    (out, blocks, inbox, outbox, gstep, edge, first), sems = refs[:7], refs[7:]
    h = Here()
    w = Wires(*sems)
    local = sems[2]
    spans = PLANE
    below, above = h.plane(3)[0], h.plane(1)[0]
    gate_planes = Planes(h, w, 32, ggw, ggw_low, lanes_at, near_gate, far_gate)

    def to_place(src, dst, base, keep, place):
        @pl.when(place != h.t)
        def _():
            x, c, y = bits(place)
            device = (h.z, 2 * x + c, y)
            w.make(src, dst, base + place, device, base + h.t).start()

        @pl.when(place == h.t)
        def _():
            pltpu.make_async_copy(src, dst, local.at[keep]).start()

    greet(near(h) + line(h))
    gate_planes.start()
    branch = [w.make(held.at[1 + i], rmix.at[i], 12 + i, h.mate(o)[0]) for i, o in enumerate(CHIPS[1:])]
    branch.append(w.make(held.at[0, SPAN // 2 : SPAN], far, 11, h.mate(CHIPS[0])[0]))
    for copy in branch:
        copy.start()
    chips = ToChips(h, w, 8, outbox, parts)
    fold = Fold(h, w, 4, blocks, inbox, outbox, total, chips)

    @pl.loop(0, spans)
    def _(step):
        place = turn(step)
        taken = views(work.in_specs, ins, place)
        mine = view(work.out_specs[0], gpre, place)
        fourth_kernel(step, *taken, mine, blocks.at[fold.slot(step)], gstep.at[step], hsum, out)
        fold.step(step)
        to_place(gstep.at[step], steps.at[h.t], 16, 1, place)

        @pl.when(place == 0)
        def _():
            edge[...] = mine[0:8, :]
            w.make(edge, after, 14, below).start()
            w.make(blocks.at[step, 0:8], first, 15, below).start()

        @pl.when(place > 0)
        def _():
            to_place(blocks.at[step, 0:8], tails.at[h.t], 24, 2, place - 1)

    w.arrived(first, 15, above)
    to_place(first, tails.at[h.t], 24, 2, 7)
    fold.last()
    gate_planes.wait()
    for copy in branch:
        copy.wait()
    w.make(edge, after, 14, below).wait()
    w.make(blocks.at[0, 0:8], first, 15, below).wait_send()
    for place in range(PLANE):

        @pl.when(place != h.t)
        def _():
            device = (h.z, place // 2, place % 2)
            w.make(gstep.at[0], steps.at[place], 16 + place, device).wait()
            w.make(first, tails.at[place], 24 + place, device).wait()

    pltpu.make_async_copy(gstep.at[0], steps.at[h.t], local.at[1]).wait()
    pltpu.make_async_copy(first, tails.at[h.t], local.at[2]).wait()
    chips.last()


def fifth_direct(work, *refs):
    ins, (ggw, near_gate, far_gate, gstate, gout, gout_low), refs = refs[:13], refs[13:19], refs[19:]
    (rgp, chip, pgate, pinner, ps, psmall, near_out, far_out), refs = refs[:8], refs[8:]
    (blocks, inbox, outbox), scratch, (ginner, giw, giw_low, small) = refs[:3], refs[3:6], refs[6:10]
    (near_inner, far_inner, zsum, gatesum, state_in, state_low, state_got), refs = refs[10:17], refs[17:]
    (ssum, rsmall, smallsum), sems = refs[:3], refs[3:]
    h = Here()
    w = Wires(*sems)
    local = sems[2]
    spans = PLANE
    mate, _ = h.mate(CORE)

    friends = near(h) + line(h)
    barrier = call(friends)
    lanes = pl.ds(pl.multiple_of(h.z * SPAN, SPAN), SPAN)
    gatesum[...] = from_planes(h.z, ggw[:, lanes], near_gate, far_gate).T
    pl.semaphore_wait(barrier, len(friends))
    out_planes = Planes(h, w, 0, gout, gout_low, head_rows, near_out, far_out)
    out_planes.start()
    state = []
    for i, o in enumerate((*CHIPS, 0)):
        near_core = w.make(gstate.at[:, h.mate(o ^ CORE)[1]], state_in.at[i], 24 + i, mate)
        on = w.make(state_low.at[i], state_got.at[i], 28 + i, h.mate(o)[0]) if o else None
        state.append((near_core, on))
        near_core.start()
    for o in range(1, 8):
        device, place = h.mate(o)
        w.send(rows_at(gatesum, place, 32), pgate.at[h.t], 44 + o, device)
    keep = [w.keep(rows_at(gatesum, h.t, 32), pgate.at[h.t])]
    for i, (o, (near_core, on)) in enumerate(zip((*CHIPS, 0), state)):
        near_core.wait()
        both = gstate[:, h.mate(o)[1]] + state_in[i]
        if on is None:
            ssum[...] = both
        else:
            state_low[i] = both.astype(bf16)
            on.start()

    chips = ToChips(h, w, 8, outbox, rgp)
    fold = Fold(h, w, 4, blocks, inbox, outbox, chip, chips)

    def conv_step(step):
        place = turn(step)
        taken = views(work.in_specs[:7], ins, place)
        fifth_kernel(place, spans, *taken, ginner.at[step], giw, small, *scratch)

    def block_step(step):
        taken = views(work.in_specs[11:], ins[11:], turn(step))
        blocks[fold.slot(step)] = fifth_product(taken[0], ginner[step], taken[1])
        fold.step(step, early=1)

    fifth_begin(*ins[7:11], giw, small)

    @pl.loop(0, 2)
    def _(step):
        conv_step(step)
        block_step(step)

    @pl.loop(2, spans)
    def _(step):
        conv_step(step)

        @pl.when(step == 3)
        def _():
            fold.settle(0)

    giw_low[...] = giw[...].astype(bf16)
    inner_planes = Planes(h, w, 16, giw, giw_low, lanes_at, near_inner, far_inner)
    inner_planes.start()
    for up in range(1, 4):
        w.send(small, rsmall.at[h.z], 20 + up, h.plane(up)[0])
    keep_small = w.keep(small, rsmall.at[h.z])
    pl.loop(2, spans)(block_step)
    fold.last()

    for _, on in state[:3]:
        on.wait()
    ssum[...] = ssum[...] + jnp.sum(state_got[...].astype(f32), axis=0)
    for up in range(1, 4):
        device, z = h.plane(up)
        w.send(ssum.at[z], ps.at[h.z], 32 + up, device)
    keep.append(w.keep(ssum.at[h.z], ps.at[h.z]))

    keep_small.wait()
    for up in range(1, 4):
        device, z = h.plane(4 - up)
        w.arrived(rsmall.at[z], 20 + up, device)
    smallsum[...] = jnp.sum(rsmall[...], axis=0)
    for i, o in enumerate((*CHIPS, CORE)):
        w.send(smallsum, psmall.at[h.t], 36 + i, h.mate(o)[0])
    keep.append(w.keep(smallsum, psmall.at[h.t]))

    inner_planes.wait()
    zsum[...] = from_planes(h.z, giw[:, lanes], near_inner, far_inner).T
    for o in range(1, 8):
        device, place = h.mate(o)
        w.send(rows_at(zsum, place, 32), pinner.at[h.t], 52 + o, device)
    keep.append(w.keep(rows_at(zsum, h.t, 32), pinner.at[h.t]))

    for i, o in enumerate(CHIPS):
        device, place = h.mate(o)
        w.arrived(psmall.at[place], 36 + i, device)
        w.send(psmall.at[place], psmall.at[place], 40 + i, mate)
    w.arrived(psmall.at[h.mate(CORE)[1]], 39, mate)
    for i, o in enumerate(CHIPS):
        w.arrived(psmall.at[h.mate(o ^ CORE)[1]], 40 + i, mate)
    for o in range(1, 8):
        device, place = h.mate(o)
        w.arrived(pgate.at[place], 44 + o, device)
        w.arrived(pinner.at[place], 52 + o, device)
    for up in range(1, 4):
        device, z = h.plane(4 - up)
        w.arrived(ps.at[z], 32 + up, device)
    chips.last()
    out_planes.wait()
    for copy in keep:
        copy.wait()
    w.finish()


def view(block, ref, step):
    if block.block_shape is None:
        return ref
    cuts, full = [], True
    for at, size, total in zip(block.index_map(step), block.block_shape, ref.shape):
        if size is pl.squeezed:
            cuts.append(at)
        elif size == total:
            cuts.append(slice(None))
            continue
        else:
            cuts.append(pl.ds(at * size if isinstance(at, int) else pl.multiple_of(at * size, size), size))
        full = False
    return ref if full else ref.at[tuple(cuts)]


def views(blocks, refs, step):
    return [view(block, ref, step) for block, ref in zip(blocks, refs)]


class Rows:
    def __init__(self, ref):
        self.ref = ref

    def __getitem__(self, span):
        return self.ref[pl.ds(pl.multiple_of(span * SPAN, SPAN), SPAN), :]

    def __setitem__(self, span, value):
        pass


def kept(dims, dtype=f32):
    return pltpu.VMEM(dims, dtype)


def flat(kernel, number, name, work, ins, outs, scratch, far=()):
    shapes = [*[kept(a.shape, a.dtype) for a in work.outs], *outs]
    return pl.pallas_call(
        functools.partial(kernel, work),
        in_specs=[IN_VMEM] * (len(work.ins) + len(ins)) + [IN_HBM] * len(far),
        out_specs=[IN_VMEM] * len(shapes),
        out_shape=shapes,
        scratch_shapes=scratch,
        compiler_params=pltpu.CompilerParams(
            collective_id=number, has_side_effects=True, vmem_limit_bytes=SMALL_LIMIT
        ),
        name=name,
    )(*work.ins, *ins, *[pltpu.with_memory_space_constraint(a, pltpu.HBM) for a in far])


def total_kernel(mine, every, planes, lines, send, recv, local):
    h = Here()
    w = Wires(send, recv, local)
    greet(near(h) + line(h))
    keep = w.keep(mine, planes.at[h.z])
    for up in range(1, 4):
        w.send(mine, planes.at[h.z], up, h.plane(up)[0])
    keep.wait()
    for up in range(1, 4):
        device, z = h.plane(4 - up)
        w.arrived(planes.at[z], up, device)
    lines[...] = jnp.sum(planes[...], axis=0)
    for o in range(1, 8):
        w.send(lines, every.at[h.t], 3 + o, h.mate(o)[0])
    keep = w.keep(lines, every.at[h.t])
    for o in range(1, 8):
        device, place = h.mate(o)
        w.arrived(every.at[place], 3 + o, device)
    keep.wait()
    w.finish()


def vmem(*dims, dtype=f32):
    return pltpu.VMEM(dims, dtype)


class Direct:
    @staticmethod
    def start(in_weight, out_weight, tokens, docs, conv, head, gain, norm):
        rows = PLANE * SPAN
        outs = [kept((D, MAIN), bf16), kept((4, PLANE, 32, SHARED), bf16), kept((rows, D), bf16), kept((16, D), bf16),
                kept((8, LOCAL)), kept((1, 128)), kept((1, 128)), kept((1, WIDE)), kept((1, WIDE)),
                kept((128, 128), bf16), kept((4, 1, WIDE)), kept((4, 1, WIDE)), kept((rows + 8, 8)),
                kept((PLANE, 1, SPAN)), kept(out_weight.shape, bf16), kept((1, D))]
        ins = [in_weight, out_weight, tokens, docs.reshape(-1, 128), conv, head, gain, norm]
        ins = [pltpu.with_memory_space_constraint(a, pltpu.HBM) for a in ins]
        loaded = [ins[i] for i in (0, 1, 3, 4, 5, 6)]
        wm, ws, x, halo, *prepared, flags, doc_rows, out_low, norm = pl.pallas_call(
            start_kernel,
            in_specs=[IN_HBM] * len(ins),
            out_specs=[IN_VMEM] * len(outs),
            out_shape=outs,
            scratch_shapes=[*[pltpu.VMEM(a.shape, a.dtype) for a in loaded], vmem(PLANE, 32, MAIN, dtype=bf16),
                            vmem(32, SHARED, dtype=bf16)] + wires(51, 10),
            compiler_params=pltpu.CompilerParams(collective_id=0, has_side_effects=True, vmem_limit_bytes=SMALL_LIMIT),
            name="gather_start",
        )(*ins)
        return wm, ws.reshape(D, SHARED), x, halo, prepared, flags, doc_rows, out_low, norm

    @staticmethod
    def first(spans, work, cotangent, out):
        rows = spans * SPAN
        return flat(
            first_direct, 1, "project_scan", work, [out],
            [kept((NSTATE, WIDE)), kept((rows, D), bf16), kept((WIDE, D), bf16)],
            [*work.scratch[:3], vmem(4, PACK, WIDE), vmem(PACK, WIDE, dtype=bf16), vmem(4, PACK, WIDE, dtype=bf16)]
            + wires(16, 2), [cotangent],
        )

    @staticmethod
    def second(spans, work):
        return work, None, None

    @staticmethod
    def third(spans, work):
        work.second, normed = work.ins[0], work.ins[10]
        work.ins = [*work.second.ins, normed]
        *outs, gout, ggw, gout_low, ggw_low, ends, chip, held, far = flat(
            third_direct, 4, "carry_gate_back", work, [],
            [kept((WIDE, D), bf16), kept((WIDE, D), bf16), kept((4, PACK, WIDE)), kept((SPAN, D)),
             kept((3, SPAN, D), bf16), kept((SPAN // 2, D), bf16)],
            [vmem(4, SPAN, D), vmem(4, SPAN, D), *work.scratch[:3], vmem(PLANE, spans, 2, SPAN),
             vmem(PACK, WIDE, dtype=bf16), vmem(4, PACK, WIDE, dtype=bf16)] + wires(18, 1),
        )
        return *outs, (gout, gout_low), (ggw, ggw_low), ends, (chip, held, far)

    @staticmethod
    def fourth(spans, work, gout, ggw, mix):
        chip, held, far = mix
        gpre, hsum, rmix, far2, near_gate, far_gate, parts, own, tails, steps, after = flat(
            fourth_direct, 5, "scan_back", work, [held, *ggw],
            [kept((2, SPAN, D), bf16), kept((SPAN // 2, D), bf16), kept((2, WIDE, SPAN)),
             kept((3, WIDE, SPAN), bf16), kept((3, SPAN, STATES), bf16), kept((SPAN, STATES)), kept((PLANE, 8, STATES)),
             kept((PLANE, 8, SPAN)), kept((8, WIDE))],
            [*work.scratch, vmem(PLANE, SPAN, STATES), vmem(4, SPAN, STATES), vmem(3, SPAN, STATES, dtype=bf16), vmem(spans, 8, SPAN),
             vmem(8, WIDE), vmem(8, STATES)] + wires(36, 3),
        )
        ggw = [ggw[0], near_gate, far_gate]
        return gpre, hsum, [parts, own], tails, steps, after, gout, [chip, far, far2, rmix], ggw

    @staticmethod
    def fifth(spans, work, ggw, grad_state, gout):
        piece = vmem(4, 4, 32, SHARED)
        rgp, chip, pgate, pinner, ps, psmall, near_out, far_out, *spare = flat(
            fifth_direct, 6, "conv_back_reduce", work, [*ggw, grad_state.reshape(4, PLANE, 32, SHARED), *gout],
            [kept((3, SPAN, D), bf16), kept((SPAN, D)), kept((PLANE, 32, WIDE)), kept((PLANE, 32, WIDE)),
             kept((4, 32, SHARED)), kept((PLANE, SMALL, WIDE)), kept((2, HEAD_DIM, D)), kept((3, HEAD_DIM, D), bf16),
             kept((4, SPAN, D)), kept((4, SPAN, D)), kept((3, SPAN, D), bf16)],
            [*work.scratch, vmem(spans, SPAN, WIDE, dtype=bf16), vmem(WIDE, D), vmem(WIDE, D, dtype=bf16),
             vmem(SMALL, WIDE), vmem(2, SPAN, WIDE), vmem(3, SPAN, WIDE, dtype=bf16),
             vmem(SPAN, WIDE), vmem(SPAN, WIDE), piece, vmem(3, 4, 32, SHARED, dtype=bf16),
             vmem(3, 4, 32, SHARED, dtype=bf16), vmem(4, 32, SHARED),
             vmem(4, SMALL, WIDE), vmem(SMALL, WIDE)] + wires(60, 5),
        )
        return pgate, pinner, ps, [chip, rgp], psmall, spare, [gout[0], near_out, far_out]

    @staticmethod
    def total(part):
        return talk(
            total_kernel, 9, "sum_all", [kept((PLANE, *part.shape))], [part],
            [vmem(4, *part.shape), vmem(*part.shape)] + wires(11, 2),
        )[0]


class Plain:
    @staticmethod
    def start(in_weight, out_weight, tokens, docs, conv, head, gain, norm):
        main, shared, out_low = run_pack(in_weight, out_weight)
        rows = main.shape[1]
        main = lax.all_to_all(main, TP, split_axis=0, concat_axis=0, tiled=True)
        main = lax.all_gather(main.reshape(PLANE * rows, MAIN), "grp", axis=0, tiled=True)
        shared = lax.all_gather(shared, ALL, axis=0, tiled=True)
        x = lax.all_gather(tokens, TP, axis=0, tiled=True)
        groups, group = lax.axis_size("grp"), lax.axis_index("grp")
        halo = lax.ppermute(x[x.shape[0] - 16 :], "grp", [(g, (g + 1) % groups) for g in range(groups)])
        at = jnp.stack([group, lax.axis_index(TP)])
        flags = plain_flags(docs, group, x.shape[0])
        return main, shared, x, halo, run_prep(groups, at, conv, head, gain), *flags, out_low, norm

    @staticmethod
    def first(spans, work, cotangent, out):
        *outs, end = launch(
            functools.partial(first_plain, spans), "project_scan", 2 * spans, work.in_specs, work.ins,
            [*work.out_specs, whole(PACK, WIDE)], [*work.outs, shape(PACK, WIDE)], work.scratch,
        )
        groups, group = lax.axis_size("grp"), lax.axis_index("grp")
        ends = lax.all_gather(end, "grp")

        def one(g, carried):
            return jnp.where(g < group, ends[g, NSTATE : NSTATE + 1] * carried + ends[g, :NSTATE], carried)

        inc = lax.fori_loop(0, groups, one, jnp.zeros((NSTATE, WIDE), f32))
        every = lax.all_gather(out, ALL, axis=0, tiled=True).reshape(HERE, PLANE, HEAD_DIM, D)
        wo = lax.dynamic_index_in_dim(every, lax.axis_index(TP), 1, False).reshape(WIDE, D)
        return *outs, inc, lax.all_gather(cotangent, TP, axis=0, tiled=True), wo

    @staticmethod
    def second(spans, work):
        y, gno, sums = launch(
            second_kernel, "scan_carry", spans, work.in_specs, work.ins,
            [*work.out_specs, spec((1, 2, SPAN), lambda s: (s, 0, 0))], [*work.outs, shape(spans, 2, SPAN)],
        )
        return y, gno, lax.all_gather(sums, TP)

    @staticmethod
    def third(spans, work):
        start = (whole(PACK, WIDE), shape(PACK, WIDE))
        mix = (work.later(D), shape(spans * SPAN, D))
        *outs, start, mix = launch(
            functools.partial(third_plain, spans), "gate_norm_back", 2 * spans, work.in_specs, work.ins,
            [*work.out_specs, start[0], mix[0]], [*work.outs, start[1], mix[1]], work.scratch,
        )
        return *outs, lax.all_gather(start, "grp"), lax.psum_scatter(mix, TP, scatter_dimension=0, tiled=True)

    @staticmethod
    def fourth(spans, work, gout, ggw, mix):
        rows = spans * SPAN
        gpre, hsum, gst, gstep = launch(
            fourth_plain, "scan_back", spans, work.in_specs, work.ins,
            [*work.out_specs, spec((SPAN, STATES), lambda s: (s, 0)), spec((8, SPAN), lambda s: (0, s))],
            [*work.outs, shape(rows, STATES), shape(8, rows)], work.scratch,
        )
        groups = lax.axis_size("grp")
        back = [(g, (g - 1) % groups) for g in range(groups)]
        swap = lambda a: lax.all_to_all(a, TP, split_axis=0, concat_axis=0, tiled=True)
        blocks = gst.reshape(PLANE, SPAN, STATES)
        tails = jnp.concatenate([blocks[1:, 0:8], lax.ppermute(gst[0:8], "grp", back)[None]], axis=0)
        steps = gstep.reshape(8, PLANE, SPAN).transpose(1, 0, 2)
        empty = jnp.zeros((HERE, PLANE, HEAD_DIM, D), f32)
        mine = gout.reshape(HERE, HEAD_DIM, D)
        every = lax.dynamic_update_index_in_dim(empty, mine, lax.axis_index(TP), 1).reshape(INNER, D)
        out = lax.psum_scatter(every, ALL, scatter_dimension=0, tiled=True)
        after = lax.ppermute(gpre[0:8], "grp", back)
        return gpre, hsum, [swap(blocks)], swap(tails), swap(steps), after, [out], [mix], ggw

    @staticmethod
    def fifth(spans, work, ggw, grad_state, gout):
        gp, giw, small = launch(
            functools.partial(fifth_plain, spans), "conv_back", spans, work.in_specs, work.ins,
            [spec((SPAN, D), lambda s: (s, 0)), whole(WIDE, D), whole(SMALL, WIDE)],
            [shape(spans * SPAN, D), shape(WIDE, D), shape(SMALL, WIDE)],
            [*work.scratch, pltpu.VMEM((SPAN, WIDE), bf16)],
        )
        inner_z = lax.psum_scatter(giw.T, "grp", scatter_dimension=0, tiled=True)
        gate_z = lax.psum_scatter(ggw.T, "grp", scatter_dimension=0, tiled=True)
        rows = inner_z.shape[0] // PLANE
        home = lambda a: lax.all_to_all(a.reshape(PLANE, rows, WIDE), TP, split_axis=0, concat_axis=0, tiled=True)
        state = lax.psum_scatter(grad_state, ALL, scatter_dimension=0, tiled=True)
        small = lax.all_gather(lax.psum(small, "grp"), TP)
        gp = lax.psum_scatter(gp, TP, scatter_dimension=0, tiled=True)
        return home(gate_z), home(inner_z), state[None], [gp], small, [], gout

    @staticmethod
    def total(part):
        return lax.psum(part, ALL)[None]


def run_pack(in_weight, out_weight):
    rows = in_weight.shape[0]
    return pl.pallas_call(
        pack_kernel,
        out_shape=[shape(PLANE, rows, MAIN, dtype=bf16), shape(rows, SHARED, dtype=bf16),
                   shape(*out_weight.shape, dtype=bf16)],
        compiler_params=pltpu.CompilerParams(vmem_limit_bytes=SMALL_LIMIT),
        name="pack_weights",
    )(in_weight, out_weight)


def plain_flags(doc_ids, group, rows):
    spans = rows // SPAN
    padded = jnp.concatenate([jnp.full((8,), -1, jnp.int32), doc_ids, jnp.full((8,), -2, jnp.int32)])
    window = lax.dynamic_slice(padded, (group * rows,), (rows + 16,))
    now = window[8:]
    lags = [now == window[8 - k : rows + 16 - k] for k in range(1, CONV)]
    by_span = window[8 : rows + 8].reshape(spans, SPAN)
    rise = by_span == window[7 : rows + 7 : SPAN][:, None]
    tail = by_span == by_span[:, SPAN - 1 :]
    fill = lambda a: jnp.pad(a.reshape(rows), (0, 8))
    zero = jnp.zeros_like(now)
    flags = jnp.stack([a.astype(f32) for a in (*lags, fill(rise), fill(tail), now, zero, zero)], axis=1)
    return flags, by_span.astype(f32).reshape(spans, 1, SPAN)


def shards(
    plan,
    tokens, cotangent, doc_ids, norm_gain, in_weight, conv_params, head_params, out_gain, out_weight,
    norm_first, norm_second, in_first, in_second, conv_first, conv_second, head_first, head_second,
    gain_first, gain_second, out_first, out_second,
):
    groups = lax.axis_size("grp")
    group = lax.axis_index("grp")
    place = lax.axis_index(TP)
    tok_rows = tokens.shape[0]
    rows = PLANE * tok_rows
    spans = rows // SPAN

    wm, ws, x, halo, prepared, flags, doc_rows, out_low, norm_row = plan.start(
        in_weight, out_weight, tokens, doc_ids, conv_params, head_params, out_gain.reshape(INNER // 128, 128),
        norm_gain.reshape(1, D),
    )
    conv, bias, rate, skip, gain, pick, before_us, behind_us = prepared

    normed, gate, chan, pre, act, dt, cum, held, pref, edge, part, incoming, cot, wo = plan.first(
        spans, First(spans, x, halo, norm_row, wm, ws, pick, conv, bias, rate, flags, doc_rows, skip, before_us),
        cotangent, out_low,
    )
    y, gno, sums = plan.second(spans, Second(spans, act, cum, flags, held, pref, incoming, part, gate, cot, wo, gain))
    gy, ggate, behind, suff, gog, gskip, gout, ggw, starts, mix = plan.third(
        spans, Third(spans, y, gate, gno, sums, act, cum, flags, gain, cot, wo, normed)
    )
    gpre, hsum, parts, tails, steps, after, gout, mix, ggw = plan.fourth(
        spans,
        Fourth(spans, act, dt, cum, flags, doc_rows, held, pref, incoming, behind, suff, starts, behind_us, gy, pre,
               skip, rate),
        gout, ggw, mix,
    )
    gs, gconv_state, grad_state = run_sixth(parts, tails, steps, flags, chan, edge, conv, tokens, norm_row)
    g_gate, g_inner, g_shared, gp, small, spare, grads_out = plan.fifth(
        spans,
        Fifth(spans, gpre, after, flags, chan, edge, conv, normed, gconv_state, gog, gskip, hsum, ggate, wm),
        ggw, grad_state, gout,
    )
    mixed, grad_tokens, grad_norm_gain = run_seventh(gp, mix, gs, ws, tokens, cotangent, norm_row, spare)
    in_f, in_s, in_u, out_f, out_s, out_u, sums = run_adam(
        g_gate, g_inner, g_shared, grad_norm_gain, in_weight, in_first, in_second,
        out_weight, out_first, out_second, grads_out,
    )
    norm3 = [a.reshape(D // 128, 128) for a in (norm_gain, norm_first, norm_second)]
    gain3 = [a.reshape(INNER // 128, 128) for a in (out_gain, gain_first, gain_second)]
    params = [*norm3, conv_params, conv_first, conv_second, head_params, head_first, head_second, *gain3]
    in_w, out_w, *rest = run_last(plan.total(sums), small, [in_weight, in_u, out_weight, out_u], params)
    rest[0:3] = [a.reshape(D) for a in rest[0:3]]
    rest[9:12] = [a.reshape(INNER) for a in rest[9:12]]
    return (mixed, grad_tokens, *rest[0:3], in_f, in_s, in_w, *rest[3:12], out_f, out_s, out_w)


def solution(mesh):
    seq = mesh.shape["seq"]
    sub = PLANE // seq
    groups = mesh.shape["fsdp"] // sub
    cut = Mesh(mesh.devices.reshape(groups, sub, seq), ALL)
    plan = Direct if (groups, sub, seq) == (4, 4, 2) else Plain
    split = P(ALL, None)
    none = P()
    return jax.shard_map(
        functools.partial(shards, plan),
        mesh=cut,
        in_specs=(split, split, none, none, split, none, none, none, split, none, none, split, split)
        + (none,) * 6
        + (split, split),
        out_specs=(split, split) + (none,) * 3 + (split,) * 3 + (none,) * 9 + (split,) * 3,
        check_vma=False,
    )
```

time: 1480 us -> 184 us (0.12)
  waiting for transfers between devices: 938 us -> 0 us
  Pallas kernels: 0 us -> 183 us
  local copies, waits for them, and re-layouts: 138 us -> 0.13 us
  other arithmetic: 130 us -> 0 us
  matrix products: 111 us -> 0 us
  blocking collectives: 87.3 us -> 0 us
  starting transfers between devices: 28.4 us -> 0 us
  between operations: 24.7 us -> 1.16 us
    reduce_scatter x2 -> x0, waiting for transfers between devices: 626 us -> none  [the longest x1 370 us: shards(): lax.psum_scatter(grad_in_full, ('fsdp', 'seq'), scatter_dimension=0, tile...]
    all_gather x4 -> x0, waiting for transfers between devices: 261 us -> none  [the longest x2 114 us: prefix_2(): gathered = jax.tree.map(lambda a: lax.all_gather(a, axis), part)]
    pallas_call x0 -> x10, Pallas kernels: none -> 183 us  [the longest x4 129 us: flat(): pl.pallas_call(functools.partial(kernel, work), in_specs=[IN_VMEM] * (len...]
    dot_general x28 -> x0, matrix products: 99.6 us -> none  [the longest x2 13.4 us: span_grads(): jnp.einsum('hij,ihp->jhp', mixing, grad_c, precision=PRECISE)]
    add x23 -> x0, other arithmetic: 53.2 us -> none  [the longest x15 40.3 us: chain_combine(): later[0][:, None, None] * earlier[1] + later[1]]
    all_to_all x7 -> x0, waiting for transfers between devices: 50.3 us -> none  [the longest x1 14.3 us: shards(): lax.all_to_all(grad_y, 'seq', split_axis=1, concat_axis=0, tiled=True)]
    dynamic_slice x47 -> x0, local copies, waits for them, and re-layouts: 48.4 us -> none  [the longest x30 36 us: one(): lax.dynamic_index_in_dim(a, source, 0, False)]
    psum x1 -> x0, blocking collectives: 41.5 us -> none  [shards(): lax.psum((grad_norm_gain, grad_out_gain, grad_conv, grad_head), ('fsdp',...]
  transfers between devices with their start and end apart: 15 -> 0, of which waited for: 13 -> 0; matrix products, arithmetic and copies ran while one was open for 2% -> 0% of each run, Pallas kernels for 0% -> 0%
where the time goes in v1:
time: 184 us
  Pallas kernels  183 us (99%)
    pallas_call x4, Pallas kernels, flat(): pl.pallas_call(functools.partial(kernel, work), in_specs=[IN_VMEM] * (len...  129 us
    pallas_call x1, Pallas kernels, start(): pl.pallas_call(start_kernel, in_specs=[IN_HBM] * len(ins), out_specs=[IN_...  37.2 us
    pallas_call x1, Pallas kernels, talk(): pl.pallas_call(kernel, in_specs=[IN_VMEM] * len(ins), out_specs=[IN_VMEM]...  10.2 us

profile of v1, /device:TPU:0, one launch (start us, length us, event | category | flops | bytes accessed | tf_op | source)
XLA Modules:
  0.0 184.1 jit_solution(2692384039598030175)
XLA Ops:
  0.7 37.2 %gather_start.1 = (bf16[1024,512]{1,0:T(8,128)(2,1)S(1)}, bf16[4,8,32,384]{3,2,1,0:T(8,128)(2,1)S(1)}, bf16[2048,1024]{1,0:T(8,128)(2,1)S(1)}, bf16[16,1024]{1,0...) custom-call(f32[32,4384]{1,0:T(8,128)} %wi_ref.3, ...), custom_call_target="tpu_custom_call" | custom-call | tf_op jit(solution)/shard_map/gather_start/pallas_call | solution.py:1711
  37.8 29.7 %project_scan.1 = (bf16[2048,1024]{1,0:T(8,128)(2,1)S(1)}, bf16[2048,256]{1,0:T(8,128)(2,1)S(1)}, bf16[2048,512]{1,0:T(8,128)(2,1)S(1)}, f32[2048,512]{1,0:T(8,1...) custom-call(bf16[2048,1024]{1,0:T(8,128)(2,1)S(1)} %get-tuple-elemen, ...), custom_call_target="tpu_custom_call" | custom-call | tf_op jit(solution)/shard_map/project_scan/pallas_call | solution.py:1661
  67.5 28.4 %carry_gate_back.1 = (bf16[2048,256]{1,0:T(8,128)(2,1)S(1)}, bf16[2048,256]{1,0:T(8,128)(2,1)S(1)}, f32[8,128,256]{2,1,0:T(8,128)S(1)}, f32[8,8,256]{2,1,0:T(8,1...) custom-call(bf16[2048,512]{1,0:T(8,128)(2,1)S(1)} %get-tuple-element, ...), custom_call_target="tpu_custom_call" | custom-call | tf_op jit(solution)/shard_map/carry_gate_back/pallas_call | solution.py:1661
  95.9 0.0 copy-start.1
  95.9 28.6 %scan_back.1 = (f32[2048,256]{1,0:T(8,128)S(1)}, f32[8,128]{1,0:T(8,128)S(1)}, bf16[2,256,1024]{2,1,0:T(8,128)(2,1)S(1)}, bf16[128,1024]{1,0:T(8,128)(2,1)S(1)},...) custom-call(bf16[2048,512]{1,0:T(8,128)(2,1)S(1)} %get-tuple-element, ...), custom_call_target="tpu_custom_call" | custom-call | tf_op jit(solution)/shard_map/scan_back/pallas_call | solution.py:1661
  124.6 1.1 conv_back_state.1
  125.7 0.0 copy-start.3
  125.7 41.8 %conv_back_reduce.1 = (bf16[3,256,1024]{2,1,0:T(8,128)(2,1)S(1)}, f32[256,1024]{1,0:T(8,128)S(1)}, f32[8,32,256]{2,1,0:T(8,128)S(1)}, f32[8,32,256]{2,1,0:T(8,12...) custom-call(f32[2048,256]{1,0:T(8,128)S(1)} %get-tuple-element.148.r, ...), custom_call_target="tpu_custom_call" | custom-call | tf_op jit(solution)/shard_map/conv_back_reduce/pallas_call | solution.py:1661
  167.5 0.0 copy-start
  167.6 0.0 copy-start.2
  167.6 0.0 copy-start.4
  167.6 0.0 copy-start.5
  167.6 0.0 copy-start.7
  167.6 0.0 copy-start.8
  167.6 2.2 %token_gradient.1 = (bf16[256,1024]{1,0:T(8,128)(2,1)}, f32[256,1024]{1,0:T(8,128)}, f32[8,128]{1,0:T(8,128)S(1)}) custom-call(f32[4,256,1024]{2,1,0:T(8,128)S(1)} %get-tuple-element.166.refs_0_, f32[4,256,1024]{2,1,0:T(8,128)S(1)} %get-tuple-element.167.refs_1_, bf16[3,256,1024]{2,1,0:T(8,128)(2,1)S(1)} %get-tuple-element.168.refs_2_, ...), custom_call_target="tpu_custom_call" | custom-call | tf_op jit(solution)/shard_map/token_gradient/pallas_call | solution.py:887
  169.9 0.0 copy-done.4
  169.9 0.0 copy-done.5
  169.9 0.0 copy-start.6
  169.9 0.0 copy-start.9
  169.9 0.0 copy-start.10
  169.9 0.0 copy-start.11
  170.0 0.0 copy-start.12
  170.0 0.0 copy-start.13
  170.0 0.0 copy-start.14
  170.0 0.0 copy-start.15
  170.0 0.0 copy-start.16
  170.0 0.0 copy-start.17
  170.0 0.0 copy-start.18
  170.0 0.0 copy-start.19
  170.0 2.1 %adam_terms.1 = (f32[32,4384]{1,0:T(8,128)}, f32[32,4384]{1,0:T(8,128)}, f32[32,4384]{1,0:T(8,128)S(1)}, f32[64,1024]{1,0:T(8,128)}, f32[64,1024]{1,0:T(8,128)},...) custom-call(f32[8,32,256]{2,1,0:T(8,128)S(1)} %get-tuple-element.178.gate_ref, ...), custom_call_target="tpu_custom_call" | custom-call | tf_op jit(solution)/shard_map/adam_terms/pallas_call | solution.py:899
  172.1 10.2 %sum_all.1.every_ref = f32[8,16,128]{2,1,0:T(8,128)S(1)} custom-call(f32[16,128]{1,0:T(8,128)S(1)} %get-tuple-element.184.mine), custom_call_target="tpu_custom_call" | custom-call | tf_op jit(solution)/shard_map/sum_all/pallas_call | solution.py:1036
  182.5 1.4 lamb_apply.1
  (18 shorter events, 0.0 us)
Async XLA Ops:
  95.9 28.7 %copy-start.1 = (bf16[256,1024]{1,0:T(8,128)(2,1)S(1)}, bf16[256,1024]{1,0:T(8,128)(2,1)}, u32[]{:S(2)}) copy-start(bf16[256,1024]{1,0:T(8,128)(2,1)} %refs_11_.1) | copy-start | bytes 1572868
  125.7 41.8 %copy-start.3 = (bf16[256,1024]{1,0:T(8,128)(2,1)S(1)}, bf16[256,1024]{1,0:T(8,128)(2,1)}, u32[]{:S(2)}) copy-start(bf16[256,1024]{1,0:T(8,128)(2,1)} %refs_12_.1) | copy-start | bytes 1572868
  167.5 2.3 %copy-start = (f32[32,4384]{1,0:T(8,128)S(1)}, f32[32,4384]{1,0:T(8,128)}, u32[]{:S(2)}) copy-start(f32[32,4384]{1,0:T(8,128)} %wi_ref.3) | copy-start | bytes 1683460
  167.6 2.3 %copy-start.2 = (f32[64,1024]{1,0:T(8,128)S(1)}, f32[64,1024]{1,0:T(8,128)}, u32[]{:S(2)}) copy-start(f32[64,1024]{1,0:T(8,128)} %wo_ref.3) | copy-start | bytes 786436
  167.6 2.3 %copy-start.4 = (f32[32,4384]{1,0:T(8,128)S(1)}, f32[32,4384]{1,0:T(8,128)}, u32[]{:S(2)}) copy-start(f32[32,4384]{1,0:T(8,128)} %mi_ref.1) | copy-start | bytes 1683460
  167.6 2.3 %copy-start.5 = (f32[32,4384]{1,0:T(8,128)S(1)}, f32[32,4384]{1,0:T(8,128)}, u32[]{:S(2)}) copy-start(f32[32,4384]{1,0:T(8,128)} %vi_ref.1) | copy-start | bytes 1683460
  167.6 2.3 %copy-start.7 = (f32[64,1024]{1,0:T(8,128)S(1)}, f32[64,1024]{1,0:T(8,128)}, u32[]{:S(2)}) copy-start(f32[64,1024]{1,0:T(8,128)} %mo_ref.1) | copy-start | bytes 786436
  167.6 2.3 %copy-start.8 = (f32[64,1024]{1,0:T(8,128)S(1)}, f32[64,1024]{1,0:T(8,128)}, u32[]{:S(2)}) copy-start(f32[64,1024]{1,0:T(8,128)} %vo_ref.1) | copy-start | bytes 786436
  169.9 12.5 %copy-start.6 = (f32[5,2304]{1,0:T(8,128)S(1)}, f32[5,2304]{1,0:T(8,128)}, u32[]{:S(2)}) copy-start(f32[5,2304]{1,0:T(8,128)} %cw_ref.1) | copy-start | bytes 138244
  169.9 12.5 %copy-start.9 = (f32[5,2304]{1,0:T(8,128)S(1)}, f32[5,2304]{1,0:T(8,128)}, u32[]{:S(2)}) copy-start(f32[5,2304]{1,0:T(8,128)} %cm_ref.1) | copy-start | bytes 138244
  169.9 12.5 %copy-start.10 = (f32[5,2304]{1,0:T(8,128)S(1)}, f32[5,2304]{1,0:T(8,128)}, u32[]{:S(2)}) copy-start(f32[5,2304]{1,0:T(8,128)} %cv_ref.1) | copy-start | bytes 138244
  169.9 12.5 %copy-start.11 = (f32[2048]{0:T(1024)S(1)}, f32[2048]{0:T(1024)}, u32[]{:S(2)}) copy-start(f32[2048]{0:T(1024)} %param.28) | copy-start | bytes 24580
  170.0 12.5 %copy-start.12 = (f32[1024]{0:T(1024)S(1)}, f32[1024]{0:T(1024)}, u32[]{:S(2)}) copy-start(f32[1024]{0:T(1024)} %param.24) | copy-start | bytes 12292
  170.0 12.5 %copy-start.13 = (f32[2048]{0:T(1024)S(1)}, f32[2048]{0:T(1024)}, u32[]{:S(2)}) copy-start(f32[2048]{0:T(1024)} %param.38) | copy-start | bytes 24580
  170.0 12.5 %copy-start.14 = (f32[2048]{0:T(1024)S(1)}, f32[2048]{0:T(1024)}, u32[]{:S(2)}) copy-start(f32[2048]{0:T(1024)} %param.39) | copy-start | bytes 24580
  170.0 12.5 %copy-start.15 = (f32[3,32]{1,0:T(4,128)S(1)}, f32[3,32]{1,0:T(4,128)}, u32[]{:S(2)}) copy-start(f32[3,32]{1,0:T(4,128)} %hw_ref.1) | copy-start | bytes 1156
  170.0 12.4 %copy-start.16 = (f32[1024]{0:T(1024)S(1)}, f32[1024]{0:T(1024)}, u32[]{:S(2)}) copy-start(f32[1024]{0:T(1024)} %param.30) | copy-start | bytes 12292
  170.0 12.4 %copy-start.17 = (f32[1024]{0:T(1024)S(1)}, f32[1024]{0:T(1024)}, u32[]{:S(2)}) copy-start(f32[1024]{0:T(1024)} %param.31) | copy-start | bytes 12292
  170.0 12.4 %copy-start.18 = (f32[3,32]{1,0:T(4,128)S(1)}, f32[3,32]{1,0:T(4,128)}, u32[]{:S(2)}) copy-start(f32[3,32]{1,0:T(4,128)} %hm_ref.1) | copy-start | bytes 1156
  170.0 12.4 %copy-start.19 = (f32[3,32]{1,0:T(4,128)S(1)}, f32[3,32]{1,0:T(4,128)}, u32[]{:S(2)}) copy-start(f32[3,32]{1,0:T(4,128)} %hv_ref.1) | copy-start | bytes 1156

commit v2 on v1

--- a/solution.py
+++ b/solution.py
@@ -481,9 +481,9 @@
 
 
 def fifth_kernel(
-    span, spans, gpre_ref, after_ref, fl_ref, chan_ref, edge_ref, conv_ref, normed_ref,
+    span, gpre_ref, fl_ref, chan_ref, edge_ref, conv_ref, normed_ref,
     ginner_ref, giw_ref, small_ref,
-    chan_ext, gext, masked,
+    chan_ext, masked,
 ):
     start = pl.multiple_of(span * SPAN, SPAN)
 
@@ -496,17 +496,8 @@
         chan_ext[0:8, :] = chan_ref[pl.ds(pl.multiple_of(start - 16, 16), 16), :WIDE].astype(f32)[8:16, :]
 
     chan_ext[8 : SPAN + 8, :] = chan_ref[pl.ds(start, SPAN), :WIDE].astype(f32)
-    gext[0:SPAN, :] = gpre_ref[pl.ds(start, SPAN), :]
-
-    @pl.when(span < spans - 1)
-    def _():
-        gext[SPAN : SPAN + 8, :] = gpre_ref[pl.ds(pl.multiple_of(start + SPAN, SPAN), 8), :]
-
-    @pl.when(span == spans - 1)
-    def _():
-        gext[SPAN : SPAN + 8, :] = after_ref[...]
-
-    total, sums = conv_back(gext[...], fl_ref[pl.ds(start, SPAN + 8), :], chan_ext, conv_ref, masked)
+    gpre = gpre_ref[pl.ds(start, SPAN + 8), :]
+    total, sums = conv_back(gpre, fl_ref[pl.ds(start, SPAN + 8), :], chan_ext, conv_ref, masked)
     ginner = total.astype(bf16)
     small_ref[0:8, :] += sums
     ginner_ref[...] = ginner
@@ -556,12 +547,7 @@
     gs_ref, ws_ref, x_ref, cot_ref, ng_ref, mixed_ref, gt_ref, gain_ref = rest
 
     def add_all(total, refs):
-        halves = [ref[...] for ref in refs if ref.shape[0] == SPAN // 2]
-        if halves:
-            total = total + jnp.concatenate(halves, axis=0).astype(f32)
         for ref in refs:
-            if ref.shape[0] == SPAN // 2:
-                continue
             if len(ref.shape) == 2:
                 total = total + ref[...].astype(f32)
             else:
@@ -610,7 +596,11 @@
     return own + first + far[1].astype(f32) + third
 
 
-def adam_kernel(count, gate_ref, inner_ref, shared_ref, gain_ref, wi_ref, mi_ref, vi_ref, wo_ref, mo_ref, vo_ref, *refs):
+def adam_kernel(skip, count, *refs):
+    adam_body(count, *refs[skip:])
+
+
+def adam_body(count, gate_ref, inner_ref, shared_ref, gain_ref, wi_ref, mi_ref, vi_ref, wo_ref, mo_ref, vo_ref, *refs):
     outs, (mi_out, vi_out, ui_out, mo_out, vo_out, uo_out, sums_ref, grad) = refs[:count], refs[count:]
     for base, ref in ((0, gate_ref), (INNER, inner_ref)):
         for i in range(HERE):
@@ -696,7 +686,7 @@
 IN_HBM = pl.BlockSpec(memory_space=pltpu.HBM)
 MIB = 1024 * 1024
 VMEM_LIMIT = 60 * MIB
-SMALL_LIMIT = 13 * MIB
+SMALL_LIMIT = 12 * MIB
 
 
 def launch(kernel, name, steps, in_specs, ins, out_specs, outs, scratch=()):
@@ -836,7 +826,7 @@
             whole(groups, 1, WIDE), block(WIDE), block(LOCAL), whole(1, WIDE), whole(1, 128),
         ]
         self.out_specs = [block(WIDE), whole(8, 128)]
-        self.outs = [shape(rows, WIDE), shape(8, 128)]
+        self.outs = [shape(rows + 8, WIDE), shape(8, 128)]
         self.scratch = [pltpu.VMEM((NSTATE, WIDE), f32)]
 
 
@@ -846,28 +836,28 @@
 
 
 class Fifth:
-    def __init__(self, spans, gpre, after, flags, chan, edge, conv, normed, gstate, gog, gskip, hsum, ggate, wm):
+    def __init__(self, spans, gpre, flags, chan, edge, conv, normed, gstate, gog, gskip, hsum, ggate, wm):
         rows = spans * SPAN
         block = lambda cols: spec((SPAN, cols), lambda s: (s, 0))
-        self.ins = [gpre, after, flags, chan, edge, conv, normed, gstate, gog, gskip, hsum, ggate, wm]
+        self.ins = [gpre, flags, chan, edge, conv, normed, gstate, gog, gskip, hsum, ggate, wm]
         self.in_specs = [
-            whole(rows, WIDE), whole(8, WIDE), whole(rows + 8, 8), whole(rows, LOCAL), whole(8, LOCAL), whole(8, WIDE),
+            whole(rows + 8, WIDE), whole(rows + 8, 8), whole(rows, LOCAL), whole(8, LOCAL), whole(8, WIDE),
             block(D), whole(8, STATES), whole(1, WIDE), whole(1, WIDE), whole(8, 128), block(WIDE), whole(D, MAIN),
         ]
         self.outs = []
-        self.scratch = [pltpu.VMEM((SPAN + 8, WIDE), f32)] * 3
+        self.scratch = [pltpu.VMEM((SPAN + 8, WIDE), f32)] * 2
 
 
 def fifth_plain(spans, *refs):
     step = pl.program_id(0)
-    ins, (gp, giw, small), (*scratch, ginner) = refs[:13], refs[13:16], refs[16:]
+    ins, (gp, giw, small), (*scratch, ginner) = refs[:12], refs[12:15], refs[15:]
 
     @pl.when(step == 0)
     def _():
-        fifth_begin(*ins[7:11], giw, small)
-
-    fifth_kernel(step, spans, *ins[:7], ginner, giw, small, *scratch)
-    gp[...] = fifth_product(ins[11], ginner[...], ins[12])
+        fifth_begin(*ins[6:10], giw, small)
+
+    fifth_kernel(step, *ins[:6], ginner, giw, small, *scratch)
+    gp[...] = fifth_product(ins[10], ginner[...], ins[11])
 
 
 def run_sixth(parts, tails, steps, flags, chan, edge, conv, x, gain):
@@ -882,10 +872,10 @@
     )(*ins)
 
 
-def run_seventh(parts, mixes, gs, ws, x, cot, gain, spare):
-    ins = [*spare, *parts, *mixes, gs, ws, x, cot, gain]
+def run_seventh(parts, mixes, gs, ws, x, cot, gain):
+    ins = [*parts, *mixes, gs, ws, x, cot, gain]
     return pl.pallas_call(
-        functools.partial(seventh_kernel, len(spare), len(parts), len(mixes)),
+        functools.partial(seventh_kernel, 0, len(parts), len(mixes)),
         in_specs=[IN_VMEM] * len(ins),
         out_shape=[shape(SPAN, D, dtype=bf16), shape(SPAN, D), shape(D // 128, 128)],
         compiler_params=pltpu.CompilerParams(vmem_limit_bytes=SMALL_LIMIT),
@@ -893,11 +883,11 @@
     )(*ins)
 
 
-def run_adam(gate, inner, shared, gain, wi, mi, vi, wo, mo, vo, grads_out):
+def run_adam(gate, inner, shared, gain, wi, mi, vi, wo, mo, vo, grads_out, spare):
     like = lambda a: shape(*a.shape)
-    ins = [gate, inner, shared, gain, wi, mi, vi, wo, mo, vo, *grads_out]
+    ins = [*spare, gate, inner, shared, gain, wi, mi, vi, wo, mo, vo, *grads_out]
     return pl.pallas_call(
-        functools.partial(adam_kernel, len(grads_out)),
+        functools.partial(adam_kernel, len(spare), len(grads_out)),
         in_specs=[IN_VMEM] * len(ins),
         out_shape=[like(wi), like(wi), like(wi), like(wo), like(wo), like(wo), shape(16, 128)],
         scratch_shapes=[pltpu.VMEM(wi.shape, f32)],
@@ -1263,10 +1253,38 @@
     return x * 4 + c * 2 + y
 
 
+class Across:
+    def __init__(self, h, w, base, block, upper, lower):
+        self.w, self.base, self.block, self.upper, self.lower = w, base, block, upper, lower
+        self.near_x, self.near_y = h.mate(4)[0], h.mate(1)[0]
+
+    def copies(self):
+        half = SPAN // 2
+        return (
+            self.w.make(self.block.at[0:half], self.upper, self.base, self.near_x),
+            self.w.make(self.block.at[half:SPAN], self.lower, self.base + 1, self.near_y),
+        )
+
+    def start(self):
+        for copy in self.copies():
+            copy.start()
+
+    def extra(self, i):
+        if i == 1:
+            self.w.arrived(self.lower, self.base + 1, self.near_y)
+            return 1, self.lower
+        self.w.arrived(self.upper, self.base, self.near_x)
+        return 0, self.upper
+
+    def last(self):
+        for copy in self.copies():
+            copy.wait_send()
+
+
 class Fold:
-    def __init__(self, h, w, base, blocks, inbox, outbox, total, deliver):
+    def __init__(self, h, w, base, blocks, inbox, outbox, total, across, deliver=None):
         self.h, self.w, self.base, self.deliver = h, w, base, deliver
-        self.blocks, self.inbox, self.outbox, self.total = blocks, inbox, outbox, total
+        self.blocks, self.inbox, self.outbox, self.total, self.across = blocks, inbox, outbox, total, across
         self.mate, _ = h.mate(CORE)
         self.slots = blocks.shape[0]
 
@@ -1282,16 +1300,35 @@
 
         return jnp.where(step >= 4, step - 4, step) if self.slots == 4 else step
 
-    def add(self, pair, put):
-        @pl.loop(0, SPAN, step=32)
-        def _(row):
-            rows = pl.ds(pl.multiple_of(row, 32), 32)
-            put(rows, self.blocks[(2 * pair + 1) % self.slots, rows, :] + self.inbox[pair, rows, :])
+    def each(self, get, put, extra=None):
+        for half in range(2):
+
+            @pl.loop(0, SPAN // 2, step=32)
+            def _(row):
+                rows = pl.ds(pl.multiple_of(row + half * (SPAN // 2), 32), 32)
+                value = get(rows)
+                if extra is not None and extra[0] == half:
+                    value = value + extra[1][pl.ds(pl.multiple_of(row, 32), 32), :].astype(f32)
+                put(rows, value)
+
+    def add(self, pair, put, extra=None):
+        slot = (2 * pair + 1) % self.slots
+        self.each(lambda rows: self.blocks[slot, rows, :] + self.inbox[pair, rows, :], put, extra)
 
     def settle(self, i):
         self.w.arrived(self.inbox.at[i], self.base + i, self.mate)
-        self.add(i, put_in(self.outbox, i))
-        self.deliver(i)
+        if i == 0:
+            self.add(0, put_in(self.across.block))
+            self.across.start()
+        elif self.outbox is None:
+            self.add(i, put_in(self.inbox, i))
+        else:
+            self.add(i, put_in(self.outbox, i - 1), self.across.extra(i))
+            self.deliver(i - 1)
+
+    def collect(self, held):
+        for i in (1, 2):
+            self.each(lambda rows: self.inbox[i, rows, :], put_in(held, i - 1), self.across.extra(i))
 
     def step(self, step, early=0):
         for i in range(4):
@@ -1307,11 +1344,12 @@
         self.add(3, put_in(self.total))
         self.sent(2)
         self.sent(3)
+        self.across.last()
 
 
 class ToChips:
     def __init__(self, h, w, base, outbox, results):
-        self.copies = [w.make(outbox.at[i], results.at[i], base + i, h.mate(o)[0]) for i, o in enumerate(CHIPS)]
+        self.copies = [w.make(outbox.at[i], results.at[i], base + i, h.mate(o)[0]) for i, o in enumerate(CHIPS[1:])]
 
     def __call__(self, i):
         self.copies[i].start()
@@ -1334,10 +1372,10 @@
         self.copies = []
         for up in range(1, 4):
             device, z = h.plane(up)
-            wide = functools.partial(w.make, piece(full, z), near.at[up // 2], base + up, device)
+            wide = near is not None and functools.partial(w.make, piece(full, z), near.at[up // 2], base + up, device)
             slim = functools.partial(w.make, piece(low, z), far.at[up - 1], base + up, device)
-            to_near = {1: h.z < 3, 2: None, 3: h.z > 0}[up]
-            from_near = {1: h.z > 0, 2: None, 3: h.z < 3}[up]
+            to_near = {1: h.z < 3, 2: None, 3: h.z > 0}[up] if near is not None else None
+            from_near = {1: h.z > 0, 2: None, 3: h.z < 3}[up] if near is not None else None
             self.copies.append((wide, slim, to_near, from_near))
 
     def each(self, near, act_wide, act_slim):
@@ -1373,13 +1411,12 @@
 def third_direct(work, *refs):
     second, third = work.second, work
     ins, normed, refs = refs[:11], refs[11], refs[12:]
-    (gy, gg, behind, suff, gog, gskip, gout, ggw), (gout_low, ggw_low, ends, chip, held, far) = refs[:8], refs[8:14]
-    (blocks, inbox, state, decay, no_all, every, low, lows), sems = refs[14:22], refs[22:]
+    (gy, gg, behind, suff, gog, gskip, gout, ggw), (ends, chip, held) = refs[:8], refs[8:11]
+    (blocks, inbox, state, decay, no_all, every, low, lows), sems = refs[11:19], refs[19:]
     act, cum, flags, _, _, _, _, gate, cot, wo, gain = ins
     h = Here()
     w = Wires(*sems)
     spans = PLANE
-    across, _ = h.mate(CHIPS[0])
     start = ends.at[h.z]
     gates = Rows(gg)
 
@@ -1412,8 +1449,9 @@
 
     chain = Chain(h, w, ends, low, lows, True)
     chain.start()
-    cross = w.make(held.at[0, 0 : SPAN // 2], far, 8, across)
-    fold = Fold(h, w, 4, blocks, inbox, held, chip, lambda i: None if i else cross.start())
+    half = SPAN // 2
+    across = Across(h, w, 8, held.at[0], held.at[1, 0:half], held.at[1, half:SPAN])
+    fold = Fold(h, w, 4, blocks, inbox, None, chip, across)
 
     @pl.loop(0, spans)
     def _(span):
@@ -1421,24 +1459,24 @@
         third_second(span, turn(span), *taken, blocks.at[fold.slot(span)], gout, ggw, no_all, gates)
         fold.step(span)
 
-    gout_low[...] = gout[...].astype(bf16)
-    ggw_low[...] = ggw[...].astype(bf16)
     fold.last()
-    cross.wait()
     chain.wait()
+    fold.collect(held)
     w.finish()
 
 
 def fourth_direct(work, *refs):
-    ins, (held, ggw, ggw_low), refs = refs[:16], refs[16:19], refs[19:]
-    (gpre, hsum), (rmix, far, near_gate, far_gate) = refs[:2], refs[2:6]
-    (parts, total, tails, steps, after), refs = refs[6:11], refs[11:]
-    (out, blocks, inbox, outbox, gstep, edge, first), sems = refs[:7], refs[7:]
+    ins, (held, ggw), refs = refs[:16], refs[16:18], refs[18:]
+    (gpre, hsum), (rmix, near_gate, far_gate) = refs[:2], refs[2:5]
+    (parts, total, tails, steps), refs = refs[5:9], refs[9:]
+    (out, blocks, inbox, outbox, gstep, edge, cross, upper, lower, ggw_low), sems = refs[:10], refs[10:]
     h = Here()
     w = Wires(*sems)
     local = sems[2]
     spans = PLANE
-    below, above = h.plane(3)[0], h.plane(1)[0]
+    below = h.plane(3)[0]
+    corner = (h.onward(3), 3, 1)
+    after = gpre.at[pl.ds(PLANE * SPAN, 8)]
     gate_planes = Planes(h, w, 32, ggw, ggw_low, lanes_at, near_gate, far_gate)
 
     def to_place(src, dst, base, keep, place):
@@ -1452,14 +1490,21 @@
         def _():
             pltpu.make_async_copy(src, dst, local.at[keep]).start()
 
-    greet(near(h) + line(h))
+    friends = near(h) + line(h)
+    barrier = call(friends)
+
+    @pl.when(h.t == 7)
+    def _():
+        call([h.mate(o, 1)[0] for o in range(8)])
+
+    ggw_low[...] = ggw[...].astype(bf16)
+    pl.semaphore_wait(barrier, len(friends) + 1)
     gate_planes.start()
-    branch = [w.make(held.at[1 + i], rmix.at[i], 12 + i, h.mate(o)[0]) for i, o in enumerate(CHIPS[1:])]
-    branch.append(w.make(held.at[0, SPAN // 2 : SPAN], far, 11, h.mate(CHIPS[0])[0]))
+    branch = [w.make(held.at[i], rmix.at[i], 12 + i, h.mate(o)[0]) for i, o in enumerate(CHIPS[1:])]
     for copy in branch:
         copy.start()
     chips = ToChips(h, w, 8, outbox, parts)
-    fold = Fold(h, w, 4, blocks, inbox, outbox, total, chips)
+    fold = Fold(h, w, 4, blocks, inbox, outbox, total, Across(h, w, 10, cross, upper, lower), chips)
 
     @pl.loop(0, spans)
     def _(step):
@@ -1474,39 +1519,48 @@
         def _():
             edge[...] = mine[0:8, :]
             w.make(edge, after, 14, below).start()
-            w.make(blocks.at[step, 0:8], first, 15, below).start()
+            w.make(blocks.at[step, 0:8], tails.at[h.t], 31, corner, 24 + h.t).start()
 
         @pl.when(place > 0)
         def _():
             to_place(blocks.at[step, 0:8], tails.at[h.t], 24, 2, place - 1)
 
-    w.arrived(first, 15, above)
-    to_place(first, tails.at[h.t], 24, 2, 7)
     fold.last()
     gate_planes.wait()
     for copy in branch:
         copy.wait()
     w.make(edge, after, 14, below).wait()
-    w.make(blocks.at[0, 0:8], first, 15, below).wait_send()
+    rows = blocks.at[0, 0:8]
     for place in range(PLANE):
+        device = (h.z, place // 2, place % 2)
 
         @pl.when(place != h.t)
         def _():
-            device = (h.z, place // 2, place % 2)
             w.make(gstep.at[0], steps.at[place], 16 + place, device).wait()
-            w.make(first, tails.at[place], 24 + place, device).wait()
+
+        @pl.when((place != h.t) | (h.t == 7))
+        def _():
+            w.arrived(tails.at[place], 24 + place, device)
+
+        @pl.when((place != h.t) | (place == 7))
+        def _():
+            w.make(rows, tails.at[place], 24 + place, device).wait_send()
 
     pltpu.make_async_copy(gstep.at[0], steps.at[h.t], local.at[1]).wait()
-    pltpu.make_async_copy(first, tails.at[h.t], local.at[2]).wait()
+
+    @pl.when(h.t < 7)
+    def _():
+        pltpu.make_async_copy(rows, tails.at[h.t], local.at[2]).wait()
+
     chips.last()
 
 
 def fifth_direct(work, *refs):
-    ins, (ggw, near_gate, far_gate, gstate, gout, gout_low), refs = refs[:13], refs[13:19], refs[19:]
-    (rgp, chip, pgate, pinner, ps, psmall, near_out, far_out), refs = refs[:8], refs[8:]
-    (blocks, inbox, outbox), scratch, (ginner, giw, giw_low, small) = refs[:3], refs[3:6], refs[6:10]
-    (near_inner, far_inner, zsum, gatesum, state_in, state_low, state_got), refs = refs[10:17], refs[17:]
-    (ssum, rsmall, smallsum), sems = refs[:3], refs[3:]
+    ins, (ggw, near_gate, far_gate, gstate, gout), rest, refs = refs[:12], refs[12:17], refs[17:24], refs[24:]
+    (pgate, pinner, ps, psmall, near_out, far_out, mixed, gtok, gain), refs = refs[:9], refs[9:]
+    (blocks, inbox, outbox, rgp, chip), scratch, (ginner, giw, giw_low, small) = refs[:5], refs[5:7], refs[7:11]
+    (far_inner, zsum, gatesum, state_in, state_low, state_got), refs = refs[11:17], refs[17:]
+    (ssum, rsmall, smallsum, cross, upper, lower, gout_low), sems = refs[:7], refs[7:]
     h = Here()
     w = Wires(*sems)
     local = sems[2]
@@ -1517,6 +1571,7 @@
     barrier = call(friends)
     lanes = pl.ds(pl.multiple_of(h.z * SPAN, SPAN), SPAN)
     gatesum[...] = from_planes(h.z, ggw[:, lanes], near_gate, far_gate).T
+    gout_low[...] = gout[...].astype(bf16)
     pl.semaphore_wait(barrier, len(friends))
     out_planes = Planes(h, w, 0, gout, gout_low, head_rows, near_out, far_out)
     out_planes.start()
@@ -1530,6 +1585,26 @@
         device, place = h.mate(o)
         w.send(rows_at(gatesum, place, 32), pgate.at[h.t], 44 + o, device)
     keep = [w.keep(rows_at(gatesum, h.t, 32), pgate.at[h.t])]
+    chips = ToChips(h, w, 8, outbox, rgp)
+    fold = Fold(h, w, 4, blocks, inbox, outbox, chip, Across(h, w, 10, cross, upper, lower), chips)
+
+    def conv_step(step):
+        place = turn(step)
+        taken = views(work.in_specs[:6], ins, place)
+        fifth_kernel(place, *taken, ginner.at[step], giw, small, *scratch)
+
+    def block_step(step):
+        taken = views(work.in_specs[10:], ins[10:], turn(step))
+        blocks[fold.slot(step)] = fifth_product(taken[0], ginner[step], taken[1])
+        fold.step(step, early=1)
+
+    fifth_begin(*ins[6:10], giw, small)
+
+    @pl.loop(0, 2)
+    def _(step):
+        conv_step(step)
+        block_step(step)
+
     for i, (o, (near_core, on)) in enumerate(zip((*CHIPS, 0), state)):
         near_core.wait()
         both = gstate[:, h.mate(o)[1]] + state_in[i]
@@ -1539,26 +1614,6 @@
             state_low[i] = both.astype(bf16)
             on.start()
 
-    chips = ToChips(h, w, 8, outbox, rgp)
-    fold = Fold(h, w, 4, blocks, inbox, outbox, chip, chips)
-
-    def conv_step(step):
-        place = turn(step)
-        taken = views(work.in_specs[:7], ins, place)
-        fifth_kernel(place, spans, *taken, ginner.at[step], giw, small, *scratch)
-
-    def block_step(step):
-        taken = views(work.in_specs[11:], ins[11:], turn(step))
-        blocks[fold.slot(step)] = fifth_product(taken[0], ginner[step], taken[1])
-        fold.step(step, early=1)
-
-    fifth_begin(*ins[7:11], giw, small)
-
-    @pl.loop(0, 2)
-    def _(step):
-        conv_step(step)
-        block_step(step)
-
     @pl.loop(2, spans)
     def _(step):
         conv_step(step)
@@ -1568,7 +1623,7 @@
             fold.settle(0)
 
     giw_low[...] = giw[...].astype(bf16)
-    inner_planes = Planes(h, w, 16, giw, giw_low, lanes_at, near_inner, far_inner)
+    inner_planes = Planes(h, w, 16, giw, giw_low, lanes_at, None, far_inner)
     inner_planes.start()
     for up in range(1, 4):
         w.send(small, rsmall.at[h.z], 20 + up, h.plane(up)[0])
@@ -1594,11 +1649,13 @@
     keep.append(w.keep(smallsum, psmall.at[h.t]))
 
     inner_planes.wait()
-    zsum[...] = from_planes(h.z, giw[:, lanes], near_inner, far_inner).T
+    zsum[...] = (giw[:, lanes] + jnp.sum(far_inner[...].astype(f32), axis=0)).T
     for o in range(1, 8):
         device, place = h.mate(o)
         w.send(rows_at(zsum, place, 32), pinner.at[h.t], 52 + o, device)
     keep.append(w.keep(rows_at(zsum, h.t, 32), pinner.at[h.t]))
+    chips.last()
+    seventh_kernel(0, 2, 2, chip, rgp, *rest, mixed, gtok, gain)
 
     for i, o in enumerate(CHIPS):
         device, place = h.mate(o)
@@ -1614,7 +1671,6 @@
     for up in range(1, 4):
         device, z = h.plane(4 - up)
         w.arrived(ps.at[z], 32 + up, device)
-    chips.last()
     out_planes.wait()
     for copy in keep:
         copy.wait()
@@ -1738,44 +1794,47 @@
     def third(spans, work):
         work.second, normed = work.ins[0], work.ins[10]
         work.ins = [*work.second.ins, normed]
-        *outs, gout, ggw, gout_low, ggw_low, ends, chip, held, far = flat(
+        *outs, gout, ggw, ends, chip, held = flat(
             third_direct, 4, "carry_gate_back", work, [],
-            [kept((WIDE, D), bf16), kept((WIDE, D), bf16), kept((4, PACK, WIDE)), kept((SPAN, D)),
-             kept((3, SPAN, D), bf16), kept((SPAN // 2, D), bf16)],
+            [kept((4, PACK, WIDE)), kept((SPAN, D)), kept((2, SPAN, D), bf16)],
             [vmem(4, SPAN, D), vmem(4, SPAN, D), *work.scratch[:3], vmem(PLANE, spans, 2, SPAN),
              vmem(PACK, WIDE, dtype=bf16), vmem(4, PACK, WIDE, dtype=bf16)] + wires(18, 1),
         )
-        return *outs, (gout, gout_low), (ggw, ggw_low), ends, (chip, held, far)
+        return *outs, gout, ggw, ends, (chip, held)
 
     @staticmethod
     def fourth(spans, work, gout, ggw, mix):
-        chip, held, far = mix
-        gpre, hsum, rmix, far2, near_gate, far_gate, parts, own, tails, steps, after = flat(
-            fourth_direct, 5, "scan_back", work, [held, *ggw],
-            [kept((2, SPAN, D), bf16), kept((SPAN // 2, D), bf16), kept((2, WIDE, SPAN)),
-             kept((3, WIDE, SPAN), bf16), kept((3, SPAN, STATES), bf16), kept((SPAN, STATES)), kept((PLANE, 8, STATES)),
-             kept((PLANE, 8, SPAN)), kept((8, WIDE))],
-            [*work.scratch, vmem(PLANE, SPAN, STATES), vmem(4, SPAN, STATES), vmem(3, SPAN, STATES, dtype=bf16), vmem(spans, 8, SPAN),
-             vmem(8, WIDE), vmem(8, STATES)] + wires(36, 3),
+        chip, held = mix
+        gpre, hsum, rmix, near_gate, far_gate, parts, own, tails, steps = flat(
+            fourth_direct, 5, "scan_back", work, [held, ggw],
+            [kept((2, SPAN, D), bf16), kept((2, WIDE, SPAN)),
+             kept((3, WIDE, SPAN), bf16), kept((2, SPAN, STATES), bf16), kept((SPAN, STATES)), kept((PLANE, 8, STATES)),
+             kept((PLANE, 8, SPAN))],
+            [*work.scratch, vmem(PLANE, SPAN, STATES), vmem(4, SPAN, STATES), vmem(2, SPAN, STATES, dtype=bf16), vmem(spans, 8, SPAN),
+             vmem(8, WIDE), vmem(SPAN, STATES, dtype=bf16), vmem(SPAN // 2, STATES, dtype=bf16),
+             vmem(SPAN // 2, STATES, dtype=bf16), vmem(WIDE, D, dtype=bf16)] + wires(36, 3),
         )
-        ggw = [ggw[0], near_gate, far_gate]
-        return gpre, hsum, [parts, own], tails, steps, after, gout, [chip, far, far2, rmix], ggw
+        ggw = [ggw, near_gate, far_gate]
+        return gpre, hsum, [parts, own], tails, steps, gout, [chip, rmix], ggw
 
     @staticmethod
-    def fifth(spans, work, ggw, grad_state, gout):
+    def fifth(spans, work, ggw, grad_state, gout, rest):
         piece = vmem(4, 4, 32, SHARED)
-        rgp, chip, pgate, pinner, ps, psmall, near_out, far_out, *spare = flat(
-            fifth_direct, 6, "conv_back_reduce", work, [*ggw, grad_state.reshape(4, PLANE, 32, SHARED), *gout],
-            [kept((3, SPAN, D), bf16), kept((SPAN, D)), kept((PLANE, 32, WIDE)), kept((PLANE, 32, WIDE)),
-             kept((4, 32, SHARED)), kept((PLANE, SMALL, WIDE)), kept((2, HEAD_DIM, D)), kept((3, HEAD_DIM, D), bf16),
-             kept((4, SPAN, D)), kept((4, SPAN, D)), kept((3, SPAN, D), bf16)],
+        mix, *rest = rest
+        pgate, pinner, ps, psmall, near_out, far_out, *tokens_back = flat(
+            fifth_direct, 6, "conv_back_reduce", work, [*ggw, grad_state.reshape(4, PLANE, 32, SHARED), gout, *mix, *rest],
+            [kept((PLANE, 32, WIDE)), kept((PLANE, 32, WIDE)), kept((4, 32, SHARED)), kept((PLANE, SMALL, WIDE)),
+             kept((2, HEAD_DIM, D)), kept((3, HEAD_DIM, D), bf16), kept((SPAN, D), bf16), kept((SPAN, D)),
+             kept((D // 128, 128)), kept((4, SPAN, D)), kept((4, SPAN, D)), kept((2, SPAN, D), bf16),
+             kept((2, SPAN, D), bf16), kept((SPAN, D))],
             [*work.scratch, vmem(spans, SPAN, WIDE, dtype=bf16), vmem(WIDE, D), vmem(WIDE, D, dtype=bf16),
-             vmem(SMALL, WIDE), vmem(2, SPAN, WIDE), vmem(3, SPAN, WIDE, dtype=bf16),
+             vmem(SMALL, WIDE), vmem(3, SPAN, WIDE, dtype=bf16),
              vmem(SPAN, WIDE), vmem(SPAN, WIDE), piece, vmem(3, 4, 32, SHARED, dtype=bf16),
              vmem(3, 4, 32, SHARED, dtype=bf16), vmem(4, 32, SHARED),
-             vmem(4, SMALL, WIDE), vmem(SMALL, WIDE)] + wires(60, 5),
+             vmem(4, SMALL, WIDE), vmem(SMALL, WIDE), vmem(SPAN, D, dtype=bf16), vmem(SPAN // 2, D, dtype=bf16),
+             vmem(SPAN // 2, D, dtype=bf16), vmem(WIDE, D, dtype=bf16)] + wires(60, 5),
         )
-        return pgate, pinner, ps, [chip, rgp], psmall, spare, [gout[0], near_out, far_out]
+        return pgate, pinner, ps, tokens_back[:3], psmall, tokens_back[3:], [gout, near_out, far_out]
 
     @staticmethod
     def total(part):
@@ -1841,7 +1900,7 @@
         gpre, hsum, gst, gstep = launch(
             fourth_plain, "scan_back", spans, work.in_specs, work.ins,
             [*work.out_specs, spec((SPAN, STATES), lambda s: (s, 0)), spec((8, SPAN), lambda s: (0, s))],
-            [*work.outs, shape(rows, STATES), shape(8, rows)], work.scratch,
+            [shape(rows, WIDE), work.outs[1], shape(rows, STATES), shape(8, rows)], work.scratch,
         )
         groups = lax.axis_size("grp")
         back = [(g, (g - 1) % groups) for g in range(groups)]
@@ -1853,11 +1912,11 @@
         mine = gout.reshape(HERE, HEAD_DIM, D)
         every = lax.dynamic_update_index_in_dim(empty, mine, lax.axis_index(TP), 1).reshape(INNER, D)
         out = lax.psum_scatter(every, ALL, scatter_dimension=0, tiled=True)
-        after = lax.ppermute(gpre[0:8], "grp", back)
-        return gpre, hsum, [swap(blocks)], swap(tails), swap(steps), after, [out], [mix], ggw
+        gpre = jnp.concatenate([gpre, lax.ppermute(gpre[0:8], "grp", back)], axis=0)
+        return gpre, hsum, [swap(blocks)], swap(tails), swap(steps), [out], [mix], ggw
 
     @staticmethod
-    def fifth(spans, work, ggw, grad_state, gout):
+    def fifth(spans, work, ggw, grad_state, gout, rest):
         gp, giw, small = launch(
             functools.partial(fifth_plain, spans), "conv_back", spans, work.in_specs, work.ins,
             [spec((SPAN, D), lambda s: (s, 0)), whole(WIDE, D), whole(SMALL, WIDE)],
@@ -1871,7 +1930,7 @@
         state = lax.psum_scatter(grad_state, ALL, scatter_dimension=0, tiled=True)
         small = lax.all_gather(lax.psum(small, "grp"), TP)
         gp = lax.psum_scatter(gp, TP, scatter_dimension=0, tiled=True)
-        return home(gate_z), home(inner_z), state[None], [gp], small, [], gout
+        return home(gate_z), home(inner_z), state[None], run_seventh([gp], *rest), small, [], gout
 
     @staticmethod
     def total(part):
@@ -1931,22 +1990,22 @@
     gy, ggate, behind, suff, gog, gskip, gout, ggw, starts, mix = plan.third(
         spans, Third(spans, y, gate, gno, sums, act, cum, flags, gain, cot, wo, normed)
     )
-    gpre, hsum, parts, tails, steps, after, gout, mix, ggw = plan.fourth(
+    gpre, hsum, parts, tails, steps, gout, mix, ggw = plan.fourth(
         spans,
         Fourth(spans, act, dt, cum, flags, doc_rows, held, pref, incoming, behind, suff, starts, behind_us, gy, pre,
                skip, rate),
         gout, ggw, mix,
     )
     gs, gconv_state, grad_state = run_sixth(parts, tails, steps, flags, chan, edge, conv, tokens, norm_row)
-    g_gate, g_inner, g_shared, gp, small, spare, grads_out = plan.fifth(
+    g_gate, g_inner, g_shared, tokens_back, small, spare, grads_out = plan.fifth(
         spans,
-        Fifth(spans, gpre, after, flags, chan, edge, conv, normed, gconv_state, gog, gskip, hsum, ggate, wm),
-        ggw, grad_state, gout,
+        Fifth(spans, gpre, flags, chan, edge, conv, normed, gconv_state, gog, gskip, hsum, ggate, wm),
+        ggw, grad_state, gout, (mix, gs, ws, tokens, cotangent, norm_row),
     )
-    mixed, grad_tokens, grad_norm_gain = run_seventh(gp, mix, gs, ws, tokens, cotangent, norm_row, spare)
+    mixed, grad_tokens, grad_norm_gain = tokens_back
     in_f, in_s, in_u, out_f, out_s, out_u, sums = run_adam(
         g_gate, g_inner, g_shared, grad_norm_gain, in_weight, in_first, in_second,
-        out_weight, out_first, out_second, grads_out,
+        out_weight, out_first, out_second, grads_out, spare,
     )
     norm3 = [a.reshape(D // 128, 128) for a in (norm_gain, norm_first, norm_second)]
     gain3 = [a.reshape(INNER // 128, 128) for a in (out_gain, gain_first, gain_second)]

time: 184 us -> 179 us (0.973)
  Pallas kernels: 183 us -> 176 us
    pallas_call x4, Pallas kernels: 129 us -> 126 us  [flat(): pl.pallas_call(functools.partial(kernel, work), in_specs=[IN_VMEM] * (len...]
    pallas_call x2 -> x1, Pallas kernels: 4.34 us -> 2.09 us  [run_adam(): pl.pallas_call(functools.partial(adam_kernel, len(spare), len(grads_out))...]
    pallas_call x1, Pallas kernels: 10.2 us -> 8.28 us  [talk(): pl.pallas_call(kernel, in_specs=[IN_VMEM] * len(ins), out_specs=[IN_VMEM]...]
where the time goes in v2:
time: 179 us
  Pallas kernels  176 us (98%)
  local copies, waits for them, and re-layouts  1.89 us (1%)
    pallas_call x4, Pallas kernels, flat(): pl.pallas_call(functools.partial(kernel, work), in_specs=[IN_VMEM] * (len...  126 us
    pallas_call x1, Pallas kernels, start(): pl.pallas_call(start_kernel, in_specs=[IN_HBM] * len(ins), out_specs=[IN_...  37.2 us
    pallas_call x1, Pallas kernels, talk(): pl.pallas_call(kernel, in_specs=[IN_VMEM] * len(ins), out_specs=[IN_VMEM]...  8.28 us

profile of v2, /device:TPU:0, one launch (start us, length us, event | category | flops | bytes accessed | tf_op | source)
XLA Modules:
  0.0 179.0 jit_solution(15610709055572335530)
XLA Ops:
  0.7 37.2 %gather_start.1 = (bf16[1024,512]{1,0:T(8,128)(2,1)S(1)}, bf16[4,8,32,384]{3,2,1,0:T(8,128)(2,1)S(1)}, bf16[2048,1024]{1,0:T(8,128)(2,1)S(1)}, bf16[16,1024]{1,0...) custom-call(f32[32,4384]{1,0:T(8,128)} %wi_ref.1, ...), custom_call_target="tpu_custom_call" | custom-call | tf_op jit(solution)/shard_map/gather_start/pallas_call | solution.py:1767
  37.8 29.6 %project_scan.1 = (bf16[2048,1024]{1,0:T(8,128)(2,1)S(1)}, bf16[2048,256]{1,0:T(8,128)(2,1)S(1)}, bf16[2048,512]{1,0:T(8,128)(2,1)S(1)}, f32[2048,512]{1,0:T(8,1...) custom-call(bf16[2048,1024]{1,0:T(8,128)(2,1)S(1)} %get-tuple-elemen, ...), custom_call_target="tpu_custom_call" | custom-call | tf_op jit(solution)/shard_map/project_scan/pallas_call | solution.py:1717
  67.5 27.4 %carry_gate_back.1 = (bf16[2048,256]{1,0:T(8,128)(2,1)S(1)}, bf16[2048,256]{1,0:T(8,128)(2,1)S(1)}, f32[8,128,256]{2,1,0:T(8,128)S(1)}, f32[8,8,256]{2,1,0:T(8,1...) custom-call(bf16[2048,512]{1,0:T(8,128)(2,1)S(1)} %get-tuple-element, ...), custom_call_target="tpu_custom_call" | custom-call | tf_op jit(solution)/shard_map/carry_gate_back/pallas_call | solution.py:1717
  94.9 0.0 copy-start.1
  94.9 28.3 %scan_back.1 = (f32[2056,256]{1,0:T(8,128)S(1)}, f32[8,128]{1,0:T(8,128)S(1)}, bf16[2,256,1024]{2,1,0:T(8,128)(2,1)S(1)}, f32[2,256,256]{2,1,0:T(8,128)S(1)}, bf...) custom-call(bf16[2048,512]{1,0:T(8,128)(2,1)S(1)} %get-tuple-element, ...), custom_call_target="tpu_custom_call" | custom-call | tf_op jit(solution)/shard_map/scan_back/pallas_call | solution.py:1717
  123.2 0.0 copy-start.3
  123.2 1.1 conv_back_state.1
  124.3 0.0 copy-done.3
  124.3 0.0 copy-start
  124.3 0.0 copy-start.2
  124.3 0.0 copy-start.4
  124.4 0.0 copy-start.5
  124.4 0.0 copy-start.7
  124.4 0.0 copy-start.8
  124.4 40.6 %conv_back_reduce.1 = (f32[8,32,256]{2,1,0:T(8,128)S(1)}, f32[8,32,256]{2,1,0:T(8,128)S(1)}, f32[4,32,384]{2,1,0:T(8,128)S(1)}, f32[8,24,256]{2,1,0:T(8,128)S(1)...) custom-call(f32[2056,256]{1,0:T(8,128)S(1)} %get-tuple-element.142.r, ...), custom_call_target="tpu_custom_call" | custom-call | tf_op jit(solution)/shard_map/conv_back_reduce/pallas_call | solution.py:1717
  165.0 0.8 copy.43
  165.8 1.0 copy.44
  166.8 0.0 copy-start.6
  166.8 0.0 copy-start.9
  166.8 0.0 copy-start.10
  166.9 0.0 copy-start.11
  166.9 0.0 copy-start.12
  166.9 0.0 copy-start.13
  166.9 0.0 copy-start.14
  166.9 0.0 copy-start.15
  166.9 0.0 copy-start.16
  166.9 0.0 copy-start.17
  166.9 0.0 copy-start.18
  167.0 0.0 copy-start.19
  167.0 2.1 %adam_terms.1 = (f32[32,4384]{1,0:T(8,128)}, f32[32,4384]{1,0:T(8,128)}, f32[32,4384]{1,0:T(8,128)S(1)}, f32[64,1024]{1,0:T(8,128)}, f32[64,1024]{1,0:T(8,128)},...) custom-call(f32[4,256,1024]{2,1,0:T(8,128)S(1)} %get-tuple-element.163.refs_0_, ...), custom_call_target="tpu_custom_call" | custom-call | tf_op jit(solution)/shard_map/adam_terms/pallas_call | solution.py:889
  169.1 8.3 %sum_all.1.every_ref = f32[8,16,128]{2,1,0:T(8,128)S(1)} custom-call(f32[16,128]{1,0:T(8,128)S(1)} %get-tuple-element.174.mine), custom_call_target="tpu_custom_call" | custom-call | tf_op jit(solution)/shard_map/sum_all/pallas_call | solution.py:1026
  177.5 1.4 lamb_apply.1
  (19 shorter events, 0.0 us)
Async XLA Ops:
  94.9 28.3 %copy-start.1 = (bf16[256,1024]{1,0:T(8,128)(2,1)S(1)}, bf16[256,1024]{1,0:T(8,128)(2,1)}, u32[]{:S(2)}) copy-start(bf16[256,1024]{1,0:T(8,128)(2,1)} %refs_21_.1) | copy-start | bytes 1572868
  123.2 1.1 copy-start.3
  124.3 42.5 %copy-start = (f32[32,4384]{1,0:T(8,128)S(1)}, f32[32,4384]{1,0:T(8,128)}, u32[]{:S(2)}) copy-start(f32[32,4384]{1,0:T(8,128)} %wi_ref.1) | copy-start | bytes 1683460
  124.3 42.5 %copy-start.2 = (f32[64,1024]{1,0:T(8,128)S(1)}, f32[64,1024]{1,0:T(8,128)}, u32[]{:S(2)}) copy-start(f32[64,1024]{1,0:T(8,128)} %wo_ref.1) | copy-start | bytes 786436
  124.3 42.5 %copy-start.4 = (f32[32,4384]{1,0:T(8,128)S(1)}, f32[32,4384]{1,0:T(8,128)}, u32[]{:S(2)}) copy-start(f32[32,4384]{1,0:T(8,128)} %refs_10_.1) | copy-start | bytes 1683460
  124.4 42.4 %copy-start.5 = (f32[32,4384]{1,0:T(8,128)S(1)}, f32[32,4384]{1,0:T(8,128)}, u32[]{:S(2)}) copy-start(f32[32,4384]{1,0:T(8,128)} %refs_11_.1) | copy-start | bytes 1683460
  124.4 42.4 %copy-start.7 = (f32[64,1024]{1,0:T(8,128)S(1)}, f32[64,1024]{1,0:T(8,128)}, u32[]{:S(2)}) copy-start(f32[64,1024]{1,0:T(8,128)} %refs_13_.1) | copy-start | bytes 786436
  124.4 42.4 %copy-start.8 = (f32[64,1024]{1,0:T(8,128)S(1)}, f32[64,1024]{1,0:T(8,128)}, u32[]{:S(2)}) copy-start(f32[64,1024]{1,0:T(8,128)} %refs_14_.3) | copy-start | bytes 786436
  166.8 10.5 %copy-start.6 = (f32[5,2304]{1,0:T(8,128)S(1)}, f32[5,2304]{1,0:T(8,128)}, u32[]{:S(2)}) copy-start(f32[5,2304]{1,0:T(8,128)} %cw_ref.1) | copy-start | bytes 138244
  166.8 10.5 %copy-start.9 = (f32[5,2304]{1,0:T(8,128)S(1)}, f32[5,2304]{1,0:T(8,128)}, u32[]{:S(2)}) copy-start(f32[5,2304]{1,0:T(8,128)} %cm_ref.1) | copy-start | bytes 138244
  166.8 10.5 %copy-start.10 = (f32[5,2304]{1,0:T(8,128)S(1)}, f32[5,2304]{1,0:T(8,128)}, u32[]{:S(2)}) copy-start(f32[5,2304]{1,0:T(8,128)} %cv_ref.1) | copy-start | bytes 138244
  166.9 10.5 %copy-start.11 = (f32[2048]{0:T(1024)S(1)}, f32[2048]{0:T(1024)}, u32[]{:S(2)}) copy-start(f32[2048]{0:T(1024)} %param.28) | copy-start | bytes 24580
  166.9 10.5 %copy-start.12 = (f32[1024]{0:T(1024)S(1)}, f32[1024]{0:T(1024)}, u32[]{:S(2)}) copy-start(f32[1024]{0:T(1024)} %param.24) | copy-start | bytes 12292
  166.9 10.5 %copy-start.13 = (f32[2048]{0:T(1024)S(1)}, f32[2048]{0:T(1024)}, u32[]{:S(2)}) copy-start(f32[2048]{0:T(1024)} %param.38) | copy-start | bytes 24580
  166.9 10.5 %copy-start.14 = (f32[2048]{0:T(1024)S(1)}, f32[2048]{0:T(1024)}, u32[]{:S(2)}) copy-start(f32[2048]{0:T(1024)} %param.39) | copy-start | bytes 24580
  166.9 10.5 %copy-start.15 = (f32[3,32]{1,0:T(4,128)S(1)}, f32[3,32]{1,0:T(4,128)}, u32[]{:S(2)}) copy-start(f32[3,32]{1,0:T(4,128)} %hw_ref.1) | copy-start | bytes 1156
  166.9 10.5 %copy-start.16 = (f32[1024]{0:T(1024)S(1)}, f32[1024]{0:T(1024)}, u32[]{:S(2)}) copy-start(f32[1024]{0:T(1024)} %param.30) | copy-start | bytes 12292
  166.9 10.5 %copy-start.17 = (f32[1024]{0:T(1024)S(1)}, f32[1024]{0:T(1024)}, u32[]{:S(2)}) copy-start(f32[1024]{0:T(1024)} %param.31) | copy-start | bytes 12292
  166.9 10.5 %copy-start.18 = (f32[3,32]{1,0:T(4,128)S(1)}, f32[3,32]{1,0:T(4,128)}, u32[]{:S(2)}) copy-start(f32[3,32]{1,0:T(4,128)} %hm_ref.1) | copy-start | bytes 1156
  167.0 10.5 %copy-start.19 = (f32[3,32]{1,0:T(4,128)S(1)}, f32[3,32]{1,0:T(4,128)}, u32[]{:S(2)}) copy-start(f32[3,32]{1,0:T(4,128)} %hv_ref.1) | copy-start | bytes 1156

commit v3 on v2

--- a/solution.py
+++ b/solution.py
@@ -597,11 +597,13 @@
 
 
 def adam_kernel(skip, count, *refs):
-    adam_body(count, *refs[skip:])
-
-
-def adam_body(count, gate_ref, inner_ref, shared_ref, gain_ref, wi_ref, mi_ref, vi_ref, wo_ref, mo_ref, vo_ref, *refs):
-    outs, (mi_out, vi_out, ui_out, mo_out, vo_out, uo_out, sums_ref, grad) = refs[:count], refs[count:]
+    refs = refs[skip:]
+    results, refs = refs[:2], refs[2:]
+    gate_ref, inner_ref, shared_ref, gain_ref, wi_ref, mi_ref, vi_ref, wo_ref, mo_ref, vo_ref = refs[:10]
+    outs, refs = refs[10 : 10 + count], refs[10 + count :]
+    mi_out, vi_out, ui_out, mo_out, vo_out, uo_out, sums_ref, *passed, grad = refs
+    for ref, out in zip(results, passed):
+        out[...] = ref[...]
     for base, ref in ((0, gate_ref), (INNER, inner_ref)):
         for i in range(HERE):
             for pair in range(PLANE // 2):
@@ -883,13 +885,14 @@
     )(*ins)
 
 
-def run_adam(gate, inner, shared, gain, wi, mi, vi, wo, mo, vo, grads_out, spare):
+def run_adam(results, gate, inner, shared, gain, wi, mi, vi, wo, mo, vo, grads_out, spare):
     like = lambda a: shape(*a.shape)
-    ins = [*spare, gate, inner, shared, gain, wi, mi, vi, wo, mo, vo, *grads_out]
+    ins = [*spare, *results, gate, inner, shared, gain, wi, mi, vi, wo, mo, vo, *grads_out]
     return pl.pallas_call(
         functools.partial(adam_kernel, len(spare), len(grads_out)),
         in_specs=[IN_VMEM] * len(ins),
-        out_shape=[like(wi), like(wi), like(wi), like(wo), like(wo), like(wo), shape(16, 128)],
+        out_shape=[like(wi), like(wi), like(wi), like(wo), like(wo), like(wo), shape(16, 128), shape(SPAN, D, dtype=bf16),
+                   shape(SPAN, D)],
         scratch_shapes=[pltpu.VMEM(wi.shape, f32)],
         compiler_params=pltpu.CompilerParams(vmem_limit_bytes=SMALL_LIMIT),
         name="adam_terms",
@@ -1614,13 +1617,9 @@
             state_low[i] = both.astype(bf16)
             on.start()
 
-    @pl.loop(2, spans)
-    def _(step):
-        conv_step(step)
-
-        @pl.when(step == 3)
-        def _():
-            fold.settle(0)
+    pl.loop(2, 4)(conv_step)
+    fold.settle(0)
+    pl.loop(4, spans)(conv_step)
 
     giw_low[...] = giw[...].astype(bf16)
     inner_planes = Planes(h, w, 16, giw, giw_low, lanes_at, None, far_inner)
@@ -2002,9 +2001,9 @@
         Fifth(spans, gpre, flags, chan, edge, conv, normed, gconv_state, gog, gskip, hsum, ggate, wm),
         ggw, grad_state, gout, (mix, gs, ws, tokens, cotangent, norm_row),
     )
-    mixed, grad_tokens, grad_norm_gain = tokens_back
-    in_f, in_s, in_u, out_f, out_s, out_u, sums = run_adam(
-        g_gate, g_inner, g_shared, grad_norm_gain, in_weight, in_first, in_second,
+    *results, grad_norm_gain = tokens_back
+    in_f, in_s, in_u, out_f, out_s, out_u, sums, mixed, grad_tokens = run_adam(
+        results, g_gate, g_inner, g_shared, grad_norm_gain, in_weight, in_first, in_second,
         out_weight, out_first, out_second, grads_out, spare,
     )
     norm3 = [a.reshape(D // 128, 128) for a in (norm_gain, norm_first, norm_second)]

time: 179 us -> 178 us (level)
  no operation moved by 1% of the time
where the time goes in v3:
time: 178 us
  Pallas kernels  177 us (99%)
    pallas_call x4, Pallas kernels, flat(): pl.pallas_call(functools.partial(kernel, work), in_specs=[IN_VMEM] * (len...  126 us
    pallas_call x1, Pallas kernels, start(): pl.pallas_call(start_kernel, in_specs=[IN_HBM] * len(ins), out_specs=[IN_...  37.2 us
    pallas_call x1, Pallas kernels, talk(): pl.pallas_call(kernel, in_specs=[IN_VMEM] * len(ins), out_specs=[IN_VMEM]...  8.41 us

profile of v3, /device:TPU:0, one launch (start us, length us, event | category | flops | bytes accessed | tf_op | source)
XLA Modules:
  0.0 177.9 jit_solution(16934739718152586450)
XLA Ops:
  0.7 37.2 %gather_start.1 = (bf16[1024,512]{1,0:T(8,128)(2,1)S(1)}, bf16[4,8,32,384]{3,2,1,0:T(8,128)(2,1)S(1)}, bf16[2048,1024]{1,0:T(8,128)(2,1)S(1)}, bf16[16,1024]{1,0...) custom-call(f32[32,4384]{1,0:T(8,128)} %wi_ref.1, ...), custom_call_target="tpu_custom_call" | custom-call | tf_op jit(solution)/shard_map/gather_start/pallas_call | solution.py:1766
  37.8 29.6 %project_scan.1 = (bf16[2048,1024]{1,0:T(8,128)(2,1)S(1)}, bf16[2048,256]{1,0:T(8,128)(2,1)S(1)}, bf16[2048,512]{1,0:T(8,128)(2,1)S(1)}, f32[2048,512]{1,0:T(8,1...) custom-call(bf16[2048,1024]{1,0:T(8,128)(2,1)S(1)} %get-tuple-elemen, ...), custom_call_target="tpu_custom_call" | custom-call | tf_op jit(solution)/shard_map/project_scan/pallas_call | solution.py:1716
  67.5 27.4 %carry_gate_back.1 = (bf16[2048,256]{1,0:T(8,128)(2,1)S(1)}, bf16[2048,256]{1,0:T(8,128)(2,1)S(1)}, f32[8,128,256]{2,1,0:T(8,128)S(1)}, f32[8,8,256]{2,1,0:T(8,1...) custom-call(bf16[2048,512]{1,0:T(8,128)(2,1)S(1)} %get-tuple-element, ...), custom_call_target="tpu_custom_call" | custom-call | tf_op jit(solution)/shard_map/carry_gate_back/pallas_call | solution.py:1716
  94.9 0.0 copy-start.1
  94.9 28.3 %scan_back.1 = (f32[2056,256]{1,0:T(8,128)S(1)}, f32[8,128]{1,0:T(8,128)S(1)}, bf16[2,256,1024]{2,1,0:T(8,128)(2,1)S(1)}, f32[2,256,256]{2,1,0:T(8,128)S(1)}, bf...) custom-call(bf16[2048,512]{1,0:T(8,128)(2,1)S(1)} %get-tuple-element, ...), custom_call_target="tpu_custom_call" | custom-call | tf_op jit(solution)/shard_map/scan_back/pallas_call | solution.py:1716
  123.2 0.0 copy-start.3
  123.2 1.1 conv_back_state.1
  124.3 0.0 copy-done.3
  124.3 0.0 copy-start
  124.3 0.0 copy-start.2
  124.3 0.0 copy-start.4
  124.3 0.0 copy-start.5
  124.3 0.0 copy-start.7
  124.3 0.0 copy-start.8
  124.4 40.6 %conv_back_reduce.1 = (f32[8,32,256]{2,1,0:T(8,128)S(1)}, f32[8,32,256]{2,1,0:T(8,128)S(1)}, f32[4,32,384]{2,1,0:T(8,128)S(1)}, f32[8,24,256]{2,1,0:T(8,128)S(1)...) custom-call(f32[2056,256]{1,0:T(8,128)S(1)} %get-tuple-element.144.r, ...), custom_call_target="tpu_custom_call" | custom-call | tf_op jit(solution)/shard_map/conv_back_reduce/pallas_call | solution.py:1716
  165.0 0.0 copy-start.6
  165.0 0.0 copy-start.9
  165.0 0.0 copy-start.10
  165.0 0.0 copy-start.11
  165.0 0.0 copy-start.12
  165.0 0.0 copy-start.13
  165.1 0.0 copy-start.14
  165.1 0.0 copy-start.15
  165.1 0.0 copy-start.16
  165.1 0.0 copy-start.17
  165.1 0.0 copy-start.18
  165.1 0.0 copy-start.19
  165.1 2.7 %adam_terms.1 = (f32[32,4384]{1,0:T(8,128)}, f32[32,4384]{1,0:T(8,128)}, f32[32,4384]{1,0:T(8,128)S(1)}, f32[64,1024]{1,0:T(8,128)}, f32[64,1024]{1,0:T(8,128)},...) custom-call(f32[4,256,1024]{2,1,0:T(8,128)S(1)} %get-tuple-element.163.refs_0_, ...), custom_call_target="tpu_custom_call" | custom-call | tf_op jit(solution)/shard_map/adam_terms/pallas_call | solution.py:891
  167.8 8.4 %sum_all.1.every_ref = f32[8,16,128]{2,1,0:T(8,128)S(1)} custom-call(f32[16,128]{1,0:T(8,128)S(1)} %get-tuple-element.178.mine), custom_call_target="tpu_custom_call" | custom-call | tf_op jit(solution)/shard_map/sum_all/pallas_call | solution.py:1029
  176.2 0.0 copy-done.6
  176.2 0.0 copy-done.9
  176.3 1.4 lamb_apply.1
  (17 shorter events, 0.0 us)
Async XLA Ops:
  94.9 28.3 %copy-start.1 = (bf16[256,1024]{1,0:T(8,128)(2,1)S(1)}, bf16[256,1024]{1,0:T(8,128)(2,1)}, u32[]{:S(2)}) copy-start(bf16[256,1024]{1,0:T(8,128)(2,1)} %refs_21_.1) | copy-start | bytes 1572868
  123.2 1.1 copy-start.3
  124.3 40.6 %copy-start = (f32[32,4384]{1,0:T(8,128)S(1)}, f32[32,4384]{1,0:T(8,128)}, u32[]{:S(2)}) copy-start(f32[32,4384]{1,0:T(8,128)} %wi_ref.1) | copy-start | bytes 1683460
  124.3 40.6 %copy-start.2 = (f32[64,1024]{1,0:T(8,128)S(1)}, f32[64,1024]{1,0:T(8,128)}, u32[]{:S(2)}) copy-start(f32[64,1024]{1,0:T(8,128)} %wo_ref.1) | copy-start | bytes 786436
  124.3 40.6 %copy-start.4 = (f32[32,4384]{1,0:T(8,128)S(1)}, f32[32,4384]{1,0:T(8,128)}, u32[]{:S(2)}) copy-start(f32[32,4384]{1,0:T(8,128)} %refs_12_.1) | copy-start | bytes 1683460
  124.3 40.6 %copy-start.5 = (f32[32,4384]{1,0:T(8,128)S(1)}, f32[32,4384]{1,0:T(8,128)}, u32[]{:S(2)}) copy-start(f32[32,4384]{1,0:T(8,128)} %refs_13_.1) | copy-start | bytes 1683460
  124.3 40.6 %copy-start.7 = (f32[64,1024]{1,0:T(8,128)S(1)}, f32[64,1024]{1,0:T(8,128)}, u32[]{:S(2)}) copy-start(f32[64,1024]{1,0:T(8,128)} %refs_15_.1) | copy-start | bytes 786436
  124.3 40.6 %copy-start.8 = (f32[64,1024]{1,0:T(8,128)S(1)}, f32[64,1024]{1,0:T(8,128)}, u32[]{:S(2)}) copy-start(f32[64,1024]{1,0:T(8,128)} %refs_16_.1) | copy-start | bytes 786436
  165.0 11.2 %copy-start.6 = (f32[5,2304]{1,0:T(8,128)S(1)}, f32[5,2304]{1,0:T(8,128)}, u32[]{:S(2)}) copy-start(f32[5,2304]{1,0:T(8,128)} %cw_ref.1) | copy-start | bytes 138244
  165.0 11.2 %copy-start.9 = (f32[5,2304]{1,0:T(8,128)S(1)}, f32[5,2304]{1,0:T(8,128)}, u32[]{:S(2)}) copy-start(f32[5,2304]{1,0:T(8,128)} %cm_ref.1) | copy-start | bytes 138244
  165.0 11.2 %copy-start.10 = (f32[5,2304]{1,0:T(8,128)S(1)}, f32[5,2304]{1,0:T(8,128)}, u32[]{:S(2)}) copy-start(f32[5,2304]{1,0:T(8,128)} %cv_ref.1) | copy-start | bytes 138244
  165.0 11.2 %copy-start.11 = (f32[2048]{0:T(1024)S(1)}, f32[2048]{0:T(1024)}, u32[]{:S(2)}) copy-start(f32[2048]{0:T(1024)} %param.28) | copy-start | bytes 24580
  165.0 11.2 %copy-start.12 = (f32[1024]{0:T(1024)S(1)}, f32[1024]{0:T(1024)}, u32[]{:S(2)}) copy-start(f32[1024]{0:T(1024)} %param.24) | copy-start | bytes 12292
  165.0 11.2 %copy-start.13 = (f32[2048]{0:T(1024)S(1)}, f32[2048]{0:T(1024)}, u32[]{:S(2)}) copy-start(f32[2048]{0:T(1024)} %param.38) | copy-start | bytes 24580
  165.1 11.2 %copy-start.14 = (f32[2048]{0:T(1024)S(1)}, f32[2048]{0:T(1024)}, u32[]{:S(2)}) copy-start(f32[2048]{0:T(1024)} %param.39) | copy-start | bytes 24580
  165.1 11.2 %copy-start.15 = (f32[3,32]{1,0:T(4,128)S(1)}, f32[3,32]{1,0:T(4,128)}, u32[]{:S(2)}) copy-start(f32[3,32]{1,0:T(4,128)} %hw_ref.1) | copy-start | bytes 1156
  165.1 11.2 %copy-start.16 = (f32[1024]{0:T(1024)S(1)}, f32[1024]{0:T(1024)}, u32[]{:S(2)}) copy-start(f32[1024]{0:T(1024)} %param.30) | copy-start | bytes 12292
  165.1 11.2 %copy-start.17 = (f32[1024]{0:T(1024)S(1)}, f32[1024]{0:T(1024)}, u32[]{:S(2)}) copy-start(f32[1024]{0:T(1024)} %param.31) | copy-start | bytes 12292
  165.1 11.2 %copy-start.18 = (f32[3,32]{1,0:T(4,128)S(1)}, f32[3,32]{1,0:T(4,128)}, u32[]{:S(2)}) copy-start(f32[3,32]{1,0:T(4,128)} %hm_ref.1) | copy-start | bytes 1156
  165.1 11.2 %copy-start.19 = (f32[3,32]{1,0:T(4,128)S(1)}, f32[3,32]{1,0:T(4,128)}, u32[]{:S(2)}) copy-start(f32[3,32]{1,0:T(4,128)} %hv_ref.1) | copy-start | bytes 1156
